TPU v7x, 32 devices: a whole 2x2x4 slice. The times are simulated.
32 devices in a mesh: member: 2 (over x), lon: 8 (over z, y), lat: 2 (over core).
Axes of the slice: x: 2, y: 2, z: 4, core: 2. Of those that a mesh axis runs over, the one named last changes fastest.
Arguments:
- state: float32 [128, 256, 640], P(('member', 'lat'), 'lon'), parts along dimension 0, may hold values from -6 to 6
- dep_shift: int32 [2, 128, 256], P(None, ('member', 'lat'), 'lon'), parts along dimension 1, may hold values from -8 to 8, as said below
- dep_frac: float32 [2, 128, 256], P(None, ('member', 'lat'), 'lon'), parts along dimension 1, may hold values from 0 to 1
- stiff: float32 [640], replicated, may hold values from 0.05 to 0.2
Outputs:
- advanced: float32 [128, 256, 640], P(('member', 'lat'), 'lon'), parts along dimension 0
There are 2 independent parts, one for each index of `member`. A program takes and returns all parts, laid end to end along the dimension named above; an argument that names none is the same for every part. Nothing has to cross between parts.
Inputs may be any that keep to these rules, and one draw needn't show every extreme that they name: `dep_shift`: both ends of the range are taken in every draw; the spread of displacements differs from row to row.
All inputs are finite; a program needn't handle non-finite values.
Results may differ from a plain program's by a relative error of at most 0.00007.
Values sent between devices are 32-bit elements; how exact they have to be, the bound alone decides.
No kernel may reach another device: no remote copies, remote signals or barrier semaphores. Data moves between devices by JAX's collectives and lax.ppermute only.
A program may use at most 64 MiB of HBM per device.

v0:
```python
import jax
import jax.numpy as jnp
from jax import lax
from jax.sharding import PartitionSpec as P

LEV = 128
TRAJ = 2
REACH = 8


OMEGAS = (0.4227, 0.8104)


def extended(block, sides, width, periodic):
    for axis, dim in sides:
        count = lax.axis_size(axis)
        forward = [(i, i + 1) for i in range(count - 1)]
        if periodic:
            forward.append((count - 1, 0))
        backward = [(target, source) for source, target in forward]
        low = lax.ppermute(
            lax.slice_in_dim(block, block.shape[dim] - width, None, axis=dim), axis, forward
        )
        high = lax.ppermute(lax.slice_in_dim(block, 0, width, axis=dim), axis, backward)
        block = jnp.concatenate([low, block, high], axis=dim)
    return block


def vertical(rows, frac, levels):
    width = rows.shape[-1]
    shifted = jnp.concatenate([rows[..., 1:], rows[..., -1:]], axis=-1)
    level_top = jnp.arange(width, dtype=jnp.int32) % levels == levels - 1
    upper = jnp.where(level_top, rows, shifted)
    return rows + frac[..., None] * (upper - rows)


def relax(padded, rhs, stiff, omega):
    center = padded[1:-1, 1:-1]
    north = padded[2:, 1:-1]
    south = padded[:-2, 1:-1]
    east = padded[1:-1, 2:]
    west = padded[1:-1, :-2]
    lap = south + north + (west + east) - 4.0 * center
    resid = rhs - (center - stiff * lap)
    return center + omega * resid


def shards(state, dep_shift, dep_frac, stiff):
    lat_rows, lon_cols, width = state.shape
    banded = extended(state, (("lon", 1),), REACH, True)
    band_cols = banded.shape[1]
    local_cols = jnp.arange(lon_cols, dtype=jnp.int32)[None, :]
    band_index = jnp.arange(band_cols, dtype=jnp.int32)[None, None, :]
    field = state
    for turn in range(TRAJ):
        wanted = REACH + local_cols + dep_shift[turn]
        picker = (wanted[:, :, None] == band_index).astype(jnp.float32)
        upstream = jnp.einsum("rqk,rkf->rqf", picker, banded, precision=lax.Precision.HIGHEST)
        rhs = vertical(upstream, dep_frac[turn], LEV)
        for which in range(2):
            padded = extended(field, (("lon", 1),), 1, True)
            padded = extended(padded, (("lat", 0),), 1, False)
            field = relax(padded, rhs, stiff, OMEGAS[which])
    return field


def solution(mesh):
    in_specs = (
        P(("member", "lat"), "lon", None),
        P(None, ("member", "lat"), "lon"),
        P(None, ("member", "lat"), "lon"),
        P(),
    )
    out_specs = P(("member", "lat"), "lon", None)
    return jax.shard_map(shards, mesh=mesh, in_specs=in_specs, out_specs=out_specs, check_vma=False)
```

profile of v0, /device:TPU:0, one launch (start us, length us, event | category | flops | bytes accessed | tf_op | source)
XLA Modules:
  0.0 96.8 jit_solution(955618590551562701)
XLA Ops:
  0.0 0.0 copy-start
  0.0 0.0 copy-start.2
  0.0 0.0 copy-start.3
  0.0 1.6 %fusion.52 = (f32[32,1,640]{2,1,0:T(1,128)S(1)}, f32[32,1,640]{2,1,0:T(1,128)S(1)}) fusion(f32[32,32,640]{2,1,0:T(8,128)} %param.4), kind=kLoop, calls=%fused_computation.110 | loop fusion | bytes 327680 | tf_op jit(solution)/shard_map/slice | solution.py:22
  1.6 3.0 %collective-permute-start.2 = (f32[32,1,640]{2,1,0:T(1,128)S(1)}, f32[32,1,640]{2,1,0:T(1,128)S(1)}, u32[]{:S(2)}, u32[]{:S(2)}) collective-permute-start(f32[32,1,640]{2,1,0:T(1,128)S(1)} %get-tuple-element.21), channel_id=1, source_target_pairs={{0,2},{2,4},{4,6},{6,8},{8,10},{10,12},{12,14},{14,0},{1,3},{3,5},... | collective-permute-start | bytes 245768 | tf_op jit(solution)/shard_map/ppermute | solution.py:21
  4.6 3.1 %collective-permute-start.3 = (f32[32,1,640]{2,1,0:T(1,128)S(1)}, f32[32,1,640]{2,1,0:T(1,128)S(1)}, u32[]{:S(2)}, u32[]{:S(2)}) collective-permute-start(f32[32,1,640]{2,1,0:T(1,128)S(1)} %get-tuple-element.22), channel_id=1, source_target_pairs={{2,0},{4,2},{6,4},{8,6},{10,8},{12,10},{14,12},{0,14},{3,1},{5,3},... | collective-permute-start | bytes 245768 | tf_op jit(solution)/shard_map/ppermute | solution.py:24
  7.7 1.4 %fusion.51 = (f32[32,8,640]{2,1,0:T(8,128)S(1)}, f32[32,8,640]{2,1,0:T(8,128)S(1)}) fusion(f32[32,32,640]{2,1,0:T(8,128)} %param.4), kind=kLoop, calls=%fused_computation.109 | loop fusion | bytes 2621440 | tf_op jit(solution)/shard_map/slice | solution.py:24
  9.1 2.0 %collective-permute-start.1 = (f32[32,8,640]{2,1,0:T(8,128)S(1)}, f32[32,8,640]{2,1,0:T(8,128)S(1)}, u32[]{:S(2)}, u32[]{:S(2)}) collective-permute-start(f32[32,8,640]{2,1,0:T(8,128)S(1)} %get-tuple-element.19), channel_id=1, source_target_pairs={{2,0},{4,2},{6,4},{8,6},{10,8},{12,10},{14,12},{0,14},{3,1},{5,3},... | collective-permute-start | bytes 1966088 | tf_op jit(solution)/shard_map/ppermute | solution.py:24
  11.1 0.1 collective-permute-start
  11.1 0.0 copy-done.2
  11.2 0.0 copy-done.3
  11.2 0.0 collective-permute-done.2
  11.2 0.0 collective-permute-done.3
  11.2 0.0 copy-done
  11.3 1.3 %collective-permute-start.4 = (f32[1,34,640]{2,1,0:T(8,128)S(1)}, f32[1,34,640]{2,1,0:T(8,128)S(1)}, u32[]{:S(2)}, u32[]{:S(2)}) collective-permute-start(f32[1,34,640]{2,1,0:T(8,128)S(1)} %get-tuple-element.11), channel_id=1, source_target_pairs={{0,1},{2,3},{4,5},{6,7},{8,9},{10,11},{12,13},{14,15},{16,17},{18,... | collective-permute-start | bytes 261128 | tf_op jit(solution)/shard_map/ppermute | solution.py:21
  12.6 1.3 %collective-permute-start.5 = (f32[1,34,640]{2,1,0:T(8,128)S(1)}, f32[1,34,640]{2,1,0:T(8,128)S(1)}, u32[]{:S(2)}, u32[]{:S(2)}) collective-permute-start(f32[1,34,640]{2,1,0:T(8,128)S(1)} %get-tuple-element.12), channel_id=1, source_target_pairs={{1,0},{3,2},{5,4},{7,6},{9,8},{11,10},{13,12},{15,14},{17,16},{19,... | collective-permute-start | bytes 261128 | tf_op jit(solution)/shard_map/ppermute | solution.py:24
  13.9 23.2 %collective-permute-done = f32[32,8,640]{2,1,0:T(8,128)S(1)} collective-permute-done((f32[32,8,640]{2,1,0:T(8,128)S(1)}, f32[32,8,640]{2,1,0:T(8,128)S(1)}, u32[]{:S(2)}, u32[]{:S(2)}) %collective-permute-start) | collective-permute-done | bytes 655392 | tf_op jit(solution)/shard_map/ppermute | solution.py:21
  37.1 0.2 constant_dynamic-update-slice_fusion.1
  37.3 2.1 %collective-permute-done.1 = f32[32,8,640]{2,1,0:T(8,128)S(1)} collective-permute-done((f32[32,8,640]{2,1,0:T(8,128)S(1)}, f32[32,8,640]{2,1,0:T(8,128)S(1)}, u32[]{:S(2)}, u32[]{:S(2)}) %collective-permute-start.1) | collective-permute-done | bytes 655392 | tf_op jit(solution)/shard_map/ppermute | solution.py:24
  39.4 1.9 %fusion.40 = f32[32,32,640]{2,1,0:T(8,128)S(1)} fusion(f32[32,48,640]{2,1,0:T(8,128)S(1)} %constant_dynamic-update-slice_fusion, s32[32,32]{1,0:T(8,128)S(1)} %get-tuple-element.24), kind=kOutput, calls=%fused_computation.76 | convolution fusion | flops 377536512 | bytes 6557696 | tf_op jit(solution)/shard_map/rqk,rkf->rqf/dot_general | solution.py:58
  41.3 0.2 slice.185
  41.5 0.0 copy-start.1
  41.5 0.7 slice.184
  42.2 0.0 collective-permute-done.4
  42.2 0.0 collective-permute-done.5
  42.2 0.0 copy-done.1
  42.3 3.7 %fusion.38 = f32[32,32,640]{2,1,0:T(8,128)S(1)} fusion(f32[32,32,640]{2,1,0:T(8,128)S(1)} %copy-done, f32[32,1,640]{2,1,0:T(1,128)S(1)} %collective-permute-done.3, f32[32,1,640]{2,1,0:T(1,128)S(1)} %collective-permute-done.2, f32[1,34,640]{2,1,0:T(8,128)S(1)} %collective-permute-done.5, f32[1,34,640]{2,1,0:T(8,128)S(1)} %collective-permute-done.4, ...), kind=kLoop, calls=%fused_computation.65 | loop fusion | flops 15073280 | bytes 10830976 | tf_op jit(solution)/shard_map/add | solution.py:45
  46.0 0.1 fusion.50
  46.1 0.5 collective-permute-start.6
  46.6 4.3 %collective-permute-start.7 = (f32[32,1,640]{2,1,0:T(1,128)S(1)}, f32[32,1,640]{2,1,0:T(1,128)S(1)}, u32[]{:S(2)}, u32[]{:S(2)}) collective-permute-start(f32[32,1,640]{2,1,0:T(1,128)S(1)} %get-tuple-element.18), channel_id=1, source_target_pairs={{2,0},{4,2},{6,4},{8,6},{10,8},{12,10},{14,12},{0,14},{3,1},{5,3},... | collective-permute-start | bytes 245768 | tf_op jit(solution)/shard_map/ppermute | solution.py:24
  50.9 2.4 %collective-permute-done.6 = f32[32,1,640]{2,1,0:T(1,128)S(1)} collective-permute-done((f32[32,1,640]{2,1,0:T(1,128)S(1)}, f32[32,1,640]{2,1,0:T(1,128)S(1)}, u32[]{:S(2)}, u32[]{:S(2)}) %collective-permute-start.6) | collective-permute-done | bytes 81952 | tf_op jit(solution)/shard_map/ppermute | solution.py:21
  53.3 0.0 collective-permute-done.7
  53.3 1.3 %collective-permute-start.8 = (f32[1,34,640]{2,1,0:T(8,128)S(1)}, f32[1,34,640]{2,1,0:T(8,128)S(1)}, u32[]{:S(2)}, u32[]{:S(2)}) collective-permute-start(f32[1,34,640]{2,1,0:T(8,128)S(1)} %get-tuple-element.9), channel_id=1, source_target_pairs={{0,1},{2,3},{4,5},{6,7},{8,9},{10,11},{12,13},{14,15},{16,17},{18,... | collective-permute-start | bytes 261128 | tf_op jit(solution)/shard_map/ppermute | solution.py:21
  54.6 1.3 %collective-permute-start.9 = (f32[1,34,640]{2,1,0:T(8,128)S(1)}, f32[1,34,640]{2,1,0:T(8,128)S(1)}, u32[]{:S(2)}, u32[]{:S(2)}) collective-permute-start(f32[1,34,640]{2,1,0:T(8,128)S(1)} %get-tuple-element.10), channel_id=1, source_target_pairs={{1,0},{3,2},{5,4},{7,6},{9,8},{11,10},{13,12},{15,14},{17,16},{19,... | collective-permute-start | bytes 261128 | tf_op jit(solution)/shard_map/ppermute | solution.py:24
  55.9 0.0 collective-permute-done.8
  56.0 1.9 %collective-permute-done.9 = f32[1,34,640]{2,1,0:T(8,128)S(1)} collective-permute-done((f32[1,34,640]{2,1,0:T(8,128)S(1)}, f32[1,34,640]{2,1,0:T(8,128)S(1)}, u32[]{:S(2)}, u32[]{:S(2)}) %collective-permute-start.9) | collective-permute-done | bytes 87072 | tf_op jit(solution)/shard_map/ppermute | solution.py:24
  57.8 3.7 %fusion.29 = f32[32,32,640]{2,1,0:T(8,128)S(1)} fusion(f32[32,32,640]{2,1,0:T(8,128)S(1)} %fusion.38, f32[32,1,640]{2,1,0:T(1,128)S(1)} %collective-permute-done.7, f32[32,1,640]{2,1,0:T(1,128)S(1)} %collective-permute-done.6, f32[1,34,640]{2,1,0:T(8,128)S(1)} %collective-permute-done.9, f32[1,34,640]{2,1,0:T(8,128)S(1)} %collective-permute-done.8, ...), kind=kLoop, calls=%fused_computation.48 | loop fusion | flops 15073280 | bytes 10830976 | tf_op jit(solution)/shard_map/add | solution.py:45
  61.6 0.1 fusion.49
  61.7 0.1 collective-permute-start.10
  61.8 4.8 %collective-permute-start.11 = (f32[32,1,640]{2,1,0:T(1,128)S(1)}, f32[32,1,640]{2,1,0:T(1,128)S(1)}, u32[]{:S(2)}, u32[]{:S(2)}) collective-permute-start(f32[32,1,640]{2,1,0:T(1,128)S(1)} %get-tuple-element.16), channel_id=1, source_target_pairs={{2,0},{4,2},{6,4},{8,6},{10,8},{12,10},{14,12},{0,14},{3,1},{5,3},... | collective-permute-start | bytes 245768 | tf_op jit(solution)/shard_map/ppermute | solution.py:24
  66.5 2.7 %collective-permute-done.10 = f32[32,1,640]{2,1,0:T(1,128)S(1)} collective-permute-done((f32[32,1,640]{2,1,0:T(1,128)S(1)}, f32[32,1,640]{2,1,0:T(1,128)S(1)}, u32[]{:S(2)}, u32[]{:S(2)}) %collective-permute-start.10) | collective-permute-done | bytes 81952 | tf_op jit(solution)/shard_map/ppermute | solution.py:21
  69.2 0.0 collective-permute-done.11
  69.3 1.5 %collective-permute-start.12 = (f32[1,34,640]{2,1,0:T(8,128)S(1)}, f32[1,34,640]{2,1,0:T(8,128)S(1)}, u32[]{:S(2)}, u32[]{:S(2)}) collective-permute-start(f32[1,34,640]{2,1,0:T(8,128)S(1)} %get-tuple-element.7), channel_id=1, source_target_pairs={{0,1},{2,3},{4,5},{6,7},{8,9},{10,11},{12,13},{14,15},{16,17},{18,... | collective-permute-start | bytes 261128 | tf_op jit(solution)/shard_map/ppermute | solution.py:21
  70.8 1.3 %collective-permute-start.13 = (f32[1,34,640]{2,1,0:T(8,128)S(1)}, f32[1,34,640]{2,1,0:T(8,128)S(1)}, u32[]{:S(2)}, u32[]{:S(2)}) collective-permute-start(f32[1,34,640]{2,1,0:T(8,128)S(1)} %get-tuple-element.8), channel_id=1, source_target_pairs={{1,0},{3,2},{5,4},{7,6},{9,8},{11,10},{13,12},{15,14},{17,16},{19,... | collective-permute-start | bytes 261128 | tf_op jit(solution)/shard_map/ppermute | solution.py:24
  72.1 1.9 %fusion.41 = f32[32,32,640]{2,1,0:T(8,128)S(1)} fusion(f32[32,48,640]{2,1,0:T(8,128)S(1)} %constant_dynamic-update-slice_fusion, s32[32,32]{1,0:T(8,128)S(1)} %get-tuple-element.23), kind=kOutput, calls=%fused_computation.77 | convolution fusion | flops 377536512 | bytes 6557696 | tf_op jit(solution)/shard_map/rqk,rkf->rqf/dot_general | solution.py:58
  74.0 0.2 slice.189
  74.2 0.7 slice.188
  74.9 0.0 collective-permute-done.12
  74.9 0.0 collective-permute-done.13
  74.9 3.8 %fusion.20 = f32[32,32,640]{2,1,0:T(8,128)S(1)} fusion(f32[32,32,640]{2,1,0:T(8,128)S(1)} %fusion.29, f32[32,1,640]{2,1,0:T(1,128)S(1)} %collective-permute-done.11, f32[32,1,640]{2,1,0:T(1,128)S(1)} %collective-permute-done.10, f32[1,34,640]{2,1,0:T(8,128)S(1)} %collective-permute-done.13, f32[1,34,640]{2,1,0:T(8,128)S(1)} %collective-permute-done.12, ...), kind=kLoop, calls=%fused_computation.31 | loop fusion | flops 15073280 | bytes 10830976 | tf_op jit(solution)/shard_map/add | solution.py:45
  78.7 0.1 fusion.48
  78.8 0.1 collective-permute-start.14
  78.9 4.7 %collective-permute-start.15 = (f32[32,1,640]{2,1,0:T(1,128)S(1)}, f32[32,1,640]{2,1,0:T(1,128)S(1)}, u32[]{:S(2)}, u32[]{:S(2)}) collective-permute-start(f32[32,1,640]{2,1,0:T(1,128)S(1)} %get-tuple-element.14), channel_id=1, source_target_pairs={{2,0},{4,2},{6,4},{8,6},{10,8},{12,10},{14,12},{0,14},{3,1},{5,3},... | collective-permute-start | bytes 245768 | tf_op jit(solution)/shard_map/ppermute | solution.py:24
  83.6 3.1 %collective-permute-done.14 = f32[32,1,640]{2,1,0:T(1,128)S(1)} collective-permute-done((f32[32,1,640]{2,1,0:T(1,128)S(1)}, f32[32,1,640]{2,1,0:T(1,128)S(1)}, u32[]{:S(2)}, u32[]{:S(2)}) %collective-permute-start.14) | collective-permute-done | bytes 81952 | tf_op jit(solution)/shard_map/ppermute | solution.py:21
  86.7 0.0 collective-permute-done.15
  86.8 2.0 %collective-permute-start.16 = (f32[1,34,640]{2,1,0:T(8,128)S(1)}, f32[1,34,640]{2,1,0:T(8,128)S(1)}, u32[]{:S(2)}, u32[]{:S(2)}) collective-permute-start(f32[1,34,640]{2,1,0:T(8,128)S(1)} %get-tuple-element.5), channel_id=1, source_target_pairs={{0,1},{2,3},{4,5},{6,7},{8,9},{10,11},{12,13},{14,15},{16,17},{18,... | collective-permute-start | bytes 261128 | tf_op jit(solution)/shard_map/ppermute | solution.py:21
  88.8 1.3 %collective-permute-start.17 = (f32[1,34,640]{2,1,0:T(8,128)S(1)}, f32[1,34,640]{2,1,0:T(8,128)S(1)}, u32[]{:S(2)}, u32[]{:S(2)}) collective-permute-start(f32[1,34,640]{2,1,0:T(8,128)S(1)} %get-tuple-element.6), channel_id=1, source_target_pairs={{1,0},{3,2},{5,4},{7,6},{9,8},{11,10},{13,12},{15,14},{17,16},{19,... | collective-permute-start | bytes 261128 | tf_op jit(solution)/shard_map/ppermute | solution.py:24
  90.1 0.0 collective-permute-done.16
  90.1 1.9 %collective-permute-done.17 = f32[1,34,640]{2,1,0:T(8,128)S(1)} collective-permute-done((f32[1,34,640]{2,1,0:T(8,128)S(1)}, f32[1,34,640]{2,1,0:T(8,128)S(1)}, u32[]{:S(2)}, u32[]{:S(2)}) %collective-permute-start.17) | collective-permute-done | bytes 87072 | tf_op jit(solution)/shard_map/ppermute | solution.py:24
  92.0 4.8 %fusion.11 = f32[32,32,640]{2,1,0:T(8,128)} fusion(f32[32,32,640]{2,1,0:T(8,128)S(1)} %fusion.20, f32[32,1,640]{2,1,0:T(1,128)S(1)} %collective-permute-done.15, f32[32,1,640]{2,1,0:T(1,128)S(1)} %collective-permute-done.14, f32[1,34,640]{2,1,0:T(8,128)S(1)} %collective-permute-done.17, f32[1,34,640]{2,1,0:T(8,128)S(1)} %collective-permute-done.16, ...), kind=kLoop, calls=%fused_computation.14 | loop fusion | flops 15073280 | bytes 10830976 | tf_op jit(solution)/shard_map/add | solution.py:45
  (10 shorter events, 0.2 us)
Async XLA Ops:
  0.0 11.2 %copy-start = (f32[32,32,640]{2,1,0:T(8,128)S(1)}, f32[32,32,640]{2,1,0:T(8,128)}, u32[]{:S(2)}) copy-start(f32[32,32,640]{2,1,0:T(8,128)} %param.4) | copy-start | bytes 7864324
  0.0 11.1 %copy-start.2 = (s32[2,32,32]{2,1,0:T(8,128)S(1)}, s32[2,32,32]{2,1,0:T(8,128)}, u32[]{:S(2)}) copy-start(s32[2,32,32]{2,1,0:T(8,128)} %param.5) | copy-start | bytes 24580
  0.0 11.2 %copy-start.3 = (f32[2,32,32]{2,1,0:T(8,128)S(1)}, f32[2,32,32]{2,1,0:T(8,128)}, u32[]{:S(2)}) copy-start(f32[2,32,32]{2,1,0:T(8,128)} %param.6) | copy-start | bytes 24580
  1.6 9.6 %collective-permute-start.2 = (f32[32,1,640]{2,1,0:T(1,128)S(1)}, f32[32,1,640]{2,1,0:T(1,128)S(1)}, u32[]{:S(2)}, u32[]{:S(2)}) collective-permute-start(f32[32,1,640]{2,1,0:T(1,128)S(1)} %get-tuple-element.21), channel_id=1, source_target_pairs={{0,2},{2,4},{4,6},{6,8},{8,10},{10,12},{12,14},{14,0},{1,3},{3,5},... | collective-permute-start | bytes 245768 | tf_op jit(solution)/shard_map/ppermute | solution.py:21
  4.6 6.6 %collective-permute-start.3 = (f32[32,1,640]{2,1,0:T(1,128)S(1)}, f32[32,1,640]{2,1,0:T(1,128)S(1)}, u32[]{:S(2)}, u32[]{:S(2)}) collective-permute-start(f32[32,1,640]{2,1,0:T(1,128)S(1)} %get-tuple-element.22), channel_id=1, source_target_pairs={{2,0},{4,2},{6,4},{8,6},{10,8},{12,10},{14,12},{0,14},{3,1},{5,3},... | collective-permute-start | bytes 245768 | tf_op jit(solution)/shard_map/ppermute | solution.py:24
  9.1 30.3 %collective-permute-start.1 = (f32[32,8,640]{2,1,0:T(8,128)S(1)}, f32[32,8,640]{2,1,0:T(8,128)S(1)}, u32[]{:S(2)}, u32[]{:S(2)}) collective-permute-start(f32[32,8,640]{2,1,0:T(8,128)S(1)} %get-tuple-element.19), channel_id=1, source_target_pairs={{2,0},{4,2},{6,4},{8,6},{10,8},{12,10},{14,12},{0,14},{3,1},{5,3},... | collective-permute-start | bytes 1966088 | tf_op jit(solution)/shard_map/ppermute | solution.py:24
  11.1 26.0 %collective-permute-start = (f32[32,8,640]{2,1,0:T(8,128)S(1)}, f32[32,8,640]{2,1,0:T(8,128)S(1)}, u32[]{:S(2)}, u32[]{:S(2)}) collective-permute-start(f32[32,8,640]{2,1,0:T(8,128)S(1)} %get-tuple-element.20), channel_id=1, source_target_pairs={{0,2},{2,4},{4,6},{6,8},{8,10},{10,12},{12,14},{14,0},{1,3},{3,5},... | collective-permute-start | bytes 1966088 | tf_op jit(solution)/shard_map/ppermute | solution.py:21
  11.3 31.0 %collective-permute-start.4 = (f32[1,34,640]{2,1,0:T(8,128)S(1)}, f32[1,34,640]{2,1,0:T(8,128)S(1)}, u32[]{:S(2)}, u32[]{:S(2)}) collective-permute-start(f32[1,34,640]{2,1,0:T(8,128)S(1)} %get-tuple-element.11), channel_id=1, source_target_pairs={{0,1},{2,3},{4,5},{6,7},{8,9},{10,11},{12,13},{14,15},{16,17},{18,... | collective-permute-start | bytes 261128 | tf_op jit(solution)/shard_map/ppermute | solution.py:21
  12.6 29.7 %collective-permute-start.5 = (f32[1,34,640]{2,1,0:T(8,128)S(1)}, f32[1,34,640]{2,1,0:T(8,128)S(1)}, u32[]{:S(2)}, u32[]{:S(2)}) collective-permute-start(f32[1,34,640]{2,1,0:T(8,128)S(1)} %get-tuple-element.12), channel_id=1, source_target_pairs={{1,0},{3,2},{5,4},{7,6},{9,8},{11,10},{13,12},{15,14},{17,16},{19,... | collective-permute-start | bytes 261128 | tf_op jit(solution)/shard_map/ppermute | solution.py:24
  41.5 0.8 copy-start.1
  46.1 7.2 %collective-permute-start.6 = (f32[32,1,640]{2,1,0:T(1,128)S(1)}, f32[32,1,640]{2,1,0:T(1,128)S(1)}, u32[]{:S(2)}, u32[]{:S(2)}) collective-permute-start(f32[32,1,640]{2,1,0:T(1,128)S(1)} %get-tuple-element.17), channel_id=1, source_target_pairs={{0,2},{2,4},{4,6},{6,8},{8,10},{10,12},{12,14},{14,0},{1,3},{3,5},... | collective-permute-start | bytes 245768 | tf_op jit(solution)/shard_map/ppermute | solution.py:21
  46.6 6.7 %collective-permute-start.7 = (f32[32,1,640]{2,1,0:T(1,128)S(1)}, f32[32,1,640]{2,1,0:T(1,128)S(1)}, u32[]{:S(2)}, u32[]{:S(2)}) collective-permute-start(f32[32,1,640]{2,1,0:T(1,128)S(1)} %get-tuple-element.18), channel_id=1, source_target_pairs={{2,0},{4,2},{6,4},{8,6},{10,8},{12,10},{14,12},{0,14},{3,1},{5,3},... | collective-permute-start | bytes 245768 | tf_op jit(solution)/shard_map/ppermute | solution.py:24
  53.3 2.6 %collective-permute-start.8 = (f32[1,34,640]{2,1,0:T(8,128)S(1)}, f32[1,34,640]{2,1,0:T(8,128)S(1)}, u32[]{:S(2)}, u32[]{:S(2)}) collective-permute-start(f32[1,34,640]{2,1,0:T(8,128)S(1)} %get-tuple-element.9), channel_id=1, source_target_pairs={{0,1},{2,3},{4,5},{6,7},{8,9},{10,11},{12,13},{14,15},{16,17},{18,... | collective-permute-start | bytes 261128 | tf_op jit(solution)/shard_map/ppermute | solution.py:21
  54.6 3.2 %collective-permute-start.9 = (f32[1,34,640]{2,1,0:T(8,128)S(1)}, f32[1,34,640]{2,1,0:T(8,128)S(1)}, u32[]{:S(2)}, u32[]{:S(2)}) collective-permute-start(f32[1,34,640]{2,1,0:T(8,128)S(1)} %get-tuple-element.10), channel_id=1, source_target_pairs={{1,0},{3,2},{5,4},{7,6},{9,8},{11,10},{13,12},{15,14},{17,16},{19,... | collective-permute-start | bytes 261128 | tf_op jit(solution)/shard_map/ppermute | solution.py:24
  61.7 7.5 %collective-permute-start.10 = (f32[32,1,640]{2,1,0:T(1,128)S(1)}, f32[32,1,640]{2,1,0:T(1,128)S(1)}, u32[]{:S(2)}, u32[]{:S(2)}) collective-permute-start(f32[32,1,640]{2,1,0:T(1,128)S(1)} %get-tuple-element.15), channel_id=1, source_target_pairs={{0,2},{2,4},{4,6},{6,8},{8,10},{10,12},{12,14},{14,0},{1,3},{3,5},... | collective-permute-start | bytes 245768 | tf_op jit(solution)/shard_map/ppermute | solution.py:21
  61.8 7.5 %collective-permute-start.11 = (f32[32,1,640]{2,1,0:T(1,128)S(1)}, f32[32,1,640]{2,1,0:T(1,128)S(1)}, u32[]{:S(2)}, u32[]{:S(2)}) collective-permute-start(f32[32,1,640]{2,1,0:T(1,128)S(1)} %get-tuple-element.16), channel_id=1, source_target_pairs={{2,0},{4,2},{6,4},{8,6},{10,8},{12,10},{14,12},{0,14},{3,1},{5,3},... | collective-permute-start | bytes 245768 | tf_op jit(solution)/shard_map/ppermute | solution.py:24
  69.3 5.7 %collective-permute-start.12 = (f32[1,34,640]{2,1,0:T(8,128)S(1)}, f32[1,34,640]{2,1,0:T(8,128)S(1)}, u32[]{:S(2)}, u32[]{:S(2)}) collective-permute-start(f32[1,34,640]{2,1,0:T(8,128)S(1)} %get-tuple-element.7), channel_id=1, source_target_pairs={{0,1},{2,3},{4,5},{6,7},{8,9},{10,11},{12,13},{14,15},{16,17},{18,... | collective-permute-start | bytes 261128 | tf_op jit(solution)/shard_map/ppermute | solution.py:21
  70.8 4.1 %collective-permute-start.13 = (f32[1,34,640]{2,1,0:T(8,128)S(1)}, f32[1,34,640]{2,1,0:T(8,128)S(1)}, u32[]{:S(2)}, u32[]{:S(2)}) collective-permute-start(f32[1,34,640]{2,1,0:T(8,128)S(1)} %get-tuple-element.8), channel_id=1, source_target_pairs={{1,0},{3,2},{5,4},{7,6},{9,8},{11,10},{13,12},{15,14},{17,16},{19,... | collective-permute-start | bytes 261128 | tf_op jit(solution)/shard_map/ppermute | solution.py:24
  78.8 7.9 %collective-permute-start.14 = (f32[32,1,640]{2,1,0:T(1,128)S(1)}, f32[32,1,640]{2,1,0:T(1,128)S(1)}, u32[]{:S(2)}, u32[]{:S(2)}) collective-permute-start(f32[32,1,640]{2,1,0:T(1,128)S(1)} %get-tuple-element.13), channel_id=1, source_target_pairs={{0,2},{2,4},{4,6},{6,8},{8,10},{10,12},{12,14},{14,0},{1,3},{3,5},... | collective-permute-start | bytes 245768 | tf_op jit(solution)/shard_map/ppermute | solution.py:21
  78.9 7.8 %collective-permute-start.15 = (f32[32,1,640]{2,1,0:T(1,128)S(1)}, f32[32,1,640]{2,1,0:T(1,128)S(1)}, u32[]{:S(2)}, u32[]{:S(2)}) collective-permute-start(f32[32,1,640]{2,1,0:T(1,128)S(1)} %get-tuple-element.14), channel_id=1, source_target_pairs={{2,0},{4,2},{6,4},{8,6},{10,8},{12,10},{14,12},{0,14},{3,1},{5,3},... | collective-permute-start | bytes 245768 | tf_op jit(solution)/shard_map/ppermute | solution.py:24
  86.8 3.3 %collective-permute-start.16 = (f32[1,34,640]{2,1,0:T(8,128)S(1)}, f32[1,34,640]{2,1,0:T(8,128)S(1)}, u32[]{:S(2)}, u32[]{:S(2)}) collective-permute-start(f32[1,34,640]{2,1,0:T(8,128)S(1)} %get-tuple-element.5), channel_id=1, source_target_pairs={{0,1},{2,3},{4,5},{6,7},{8,9},{10,11},{12,13},{14,15},{16,17},{18,... | collective-permute-start | bytes 261128 | tf_op jit(solution)/shard_map/ppermute | solution.py:21
  88.8 3.2 %collective-permute-start.17 = (f32[1,34,640]{2,1,0:T(8,128)S(1)}, f32[1,34,640]{2,1,0:T(8,128)S(1)}, u32[]{:S(2)}, u32[]{:S(2)}) collective-permute-start(f32[1,34,640]{2,1,0:T(8,128)S(1)} %get-tuple-element.6), channel_id=1, source_target_pairs={{1,0},{3,2},{5,4},{7,6},{9,8},{11,10},{13,12},{15,14},{17,16},{19,... | collective-permute-start | bytes 261128 | tf_op jit(solution)/shard_map/ppermute | solution.py:24
where the time goes:
time: 97.1 us; the launch traced here: 96.8 us
  waiting for transfers between devices  37.3 us (38%)
  starting transfers between devices  33.9 us (35%)
  other arithmetic  16.1 us (17%)
  local copies, waits for them, and re-layouts  5.43 us (6%)
  matrix products  3.73 us (4%)
    ppermute x9, waiting for transfers between devices, extended(): lax.ppermute(lax.slice_in_dim(block, block.shape[dim] - width, None, axis...  31.4 us
    ppermute x9, starting transfers between devices, extended(): lax.ppermute(lax.slice_in_dim(block, 0, width, axis=dim), axis, backward)  24.1 us
    add x4, other arithmetic, relax(): return center + omega * resid  15.9 us
    ppermute x9, starting transfers between devices, extended(): lax.ppermute(lax.slice_in_dim(block, block.shape[dim] - width, None, axis...  9.85 us
    ppermute x9, waiting for transfers between devices, extended(): lax.ppermute(lax.slice_in_dim(block, 0, width, axis=dim), axis, backward)  5.87 us
    dot_general x2, matrix products, shards(): jnp.einsum('rqk,rkf->rqf', picker, banded, precision=lax.Precision.HIGHEST)  3.73 us
  transfers between devices with their start and end apart: 18, of which 7 were waited for; matrix products, arithmetic and copies ran while one was open for 8% of the time, Pallas kernels for 0%

commit v1 on v0

v1 whole, which is shorter than its diff:
```python
import functools

import jax
import jax.numpy as jnp
from jax import lax
from jax.experimental import pallas as pl
from jax.experimental.pallas import tpu as pltpu
from jax.sharding import PartitionSpec as P

LEV = 128
TRAJ = 2
REACH = 8
OMEGAS = (0.4227, 0.8104)

NEAR = 2 * TRAJ
FAR = REACH - 1
SLOTS = 80
LANES = 128
SIDE = 16
UP_ROWS = 4
SWEEP_ROWS = 6


def ring(axis, step):
    count = lax.axis_size(axis)
    return [(i, (i + step) % count) for i in range(count)]


def pairs(axis, start):
    count = lax.axis_size(axis)
    edges = [(i, (i + 1) % count) for i in range(start, count, 2)]
    return edges + [(b, a) for a, b in edges]


def start_kernel(
    info_ref,
    shift_ref,
    frac_ref,
    state_ref,
    own_ref,
    edge_ref,
    left_a_ref,
    left_b_ref,
    right_a_ref,
    right_b_ref,
    pad,
    sides,
    sems,
):
    turns, rows, cols = shift_ref.shape
    edge_row = jnp.where(info_ref[0] == 0, rows - NEAR, 0)
    fetch = [
        pltpu.make_async_copy(state_ref.at[:, pl.ds(0, 8), :], sides.at[0], sems.at[0]),
        pltpu.make_async_copy(state_ref.at[:, pl.ds(cols - 8, 8), :], sides.at[1], sems.at[1]),
        pltpu.make_async_copy(state_ref.at[pl.ds(edge_row, NEAR)], edge_ref, sems.at[2]),
    ]
    for copy in fetch:
        copy.start()
    pad[...] = jnp.zeros_like(pad)
    for kind in range(2 * turns):
        value = shift_ref[kind].astype(jnp.float32) if kind < turns else frac_ref[kind - turns]
        pad[0:rows, 0:cols] = value
        own_ref[kind] = jnp.transpose(pad[...])[0:cols, :]
    half = left_a_ref.shape[0] // NEAR
    for side, (first, refs) in enumerate(((0, (left_a_ref, left_b_ref)), (8 - NEAR, (right_a_ref, right_b_ref)))):
        fetch[side].wait()
        for r in range(0, rows, 2):
            two = jnp.concatenate([sides[side, r + v, first : first + NEAR, :] for v in range(2)], axis=0)
            n = r % half * NEAR
            refs[r // half][n : n + 2 * NEAR, :] = two
    fetch[2].wait()


def second_kernel(
    info_ref,
    own_ref,
    next_ref,
    edge_ref,
    left_ref,
    right_ref,
    to_left_ref,
    to_right_ref,
    more_left_ref,
    more_right_ref,
    dep_ref,
    *,
    rows,
):
    kinds, cols, _ = own_ref.shape
    low = info_ref[0] == 0
    lat_rows = rows - NEAR
    lane = lax.broadcasted_iota(jnp.int32, (cols, LANES), 1)
    head = jnp.zeros((8, to_left_ref.shape[1]), jnp.float32)
    to_left_ref[...] = head
    to_right_ref[...] = head
    for kind in range(kinds):
        own, other = own_ref[kind], next_ref[kind]
        other = jnp.where(low, pltpu.roll(other, lat_rows, 1), pltpu.roll(other, NEAR, 1))
        both = jnp.where(lane < lat_rows, own, other)
        dep_ref[kind] = both
        to_left_ref[0:NEAR, kind * LANES : (kind + 1) * LANES] = both[0:NEAR, :]
        to_right_ref[0:NEAR, kind * LANES : (kind + 1) * LANES] = both[cols - NEAR : cols, :]
    count = left_ref.shape[0]
    more_left_ref[0:count, :] = left_ref[...]
    more_right_ref[0:count, :] = right_ref[...]
    for r in range(NEAR):
        more_left_ref[count + r * NEAR : count + r * NEAR + NEAR, :] = edge_ref[r, 0:NEAR, :]
        more_right_ref[count + r * NEAR : count + r * NEAR + NEAR, :] = edge_ref[r, cols - NEAR : cols, :]


def list_slots(bits_ref, which, rows, cols, firsts, list_ref, slots):
    def row(m, counts):
        low, high = counts
        base = m * cols
        low_bits, high_bits = bits_ref[which, m], bits_ref[which + 1, m]
        for j in range(FAR):
            list_ref[0, jnp.minimum(low, slots)] = base + (firsts[0][0] + firsts[0][1] * j)
            list_ref[1, jnp.minimum(high, slots)] = base + (firsts[1][0] + firsts[1][1] * j)
            low = low + ((low_bits >> j) & 1)
            high = high + ((high_bits >> j) & 1)
        return low, high

    low, high = lax.fori_loop(0, rows, row, (jnp.int32(0), jnp.int32(0)))
    list_ref[0, slots + 1] = low
    list_ref[1, slots + 1] = high


def pack_kernel(
    info_ref,
    dep_ref,
    state_ref,
    edge_ref,
    from_left_ref,
    from_right_ref,
    low_ref,
    high_ref,
    flags,
    wide_ref,
    buf,
    heads,
    bits,
    lists,
    sems,
    *,
    rows,
    slots,
):
    kinds, cols, _ = dep_ref.shape
    wide = cols + 2 * NEAR
    lat_rows = rows - NEAR
    low = info_ref[0] == 0
    own, extra = lat_rows * cols, NEAR * cols
    fetch = [
        pltpu.make_async_copy(from_left_ref, heads.at[0], sems.at[0]),
        pltpu.make_async_copy(from_right_ref, heads.at[1], sems.at[1]),
        pltpu.make_async_copy(state_ref, buf.at[pl.ds(0, own)], sems.at[2]),
        pltpu.make_async_copy(edge_ref, buf.at[pl.ds(own, extra)], sems.at[3]),
    ]
    for copy in fetch:
        copy.start()

    def clear(n, _):
        for side in range(2):
            lists[side, n] = 0
        return 0

    lax.fori_loop(0, slots + 1, clear, 0)
    fetch[0].wait()
    fetch[1].wait()
    for kind in range(kinds):
        lanes = slice(kind * LANES, (kind + 1) * LANES)
        wide_ref[kind, 0:NEAR, :] = heads[0, 0:NEAR, lanes]
        wide_ref[kind, NEAR : NEAR + cols, :] = dep_ref[kind]
        wide_ref[kind, NEAR + cols : wide, :] = heads[1, 0:NEAR, lanes]

    lane = lax.broadcasted_iota(jnp.int32, (1, LANES), 1)
    beyond = jnp.where(low, lane - lat_rows + 1, rows - lane)
    beyond = jnp.where(lane < lat_rows, 0, jnp.where(lane < rows, beyond, rows))
    reach = [NEAR - 1 - 2 * turn for turn in range(TRAJ)]
    groups = (
        ([0] * TRAJ, 0, 1),
        ([cols + NEAR - r for r in reach], cols - 1, -1),
        ([NEAR - r for r in reach], -1, -1),
        ([cols] * TRAJ, cols, 1),
    )
    for which, (first, anchor, sign) in enumerate(groups):
        total = jnp.zeros((1, LANES), jnp.int32)
        hits = [jnp.zeros((1, LANES), bool) for _ in range(FAR)]
        for turn in range(TRAJ):
            for q in range(first[turn], first[turn] + NEAR + reach[turn]):
                target = wide_ref[turn, q : q + 1, :].astype(jnp.int32) + (q - NEAR)
                target = jnp.where(beyond <= reach[turn], target, -4 * LANES)
                for j in range(FAR):
                    hits[j] = hits[j] | (target == anchor + sign * (NEAR + j))
        for j in range(FAR):
            total = total + jnp.where(hits[j], 1 << j, 0)
        flags[which : which + 1, :] = total
    flags[len(groups) : 8, :] = jnp.zeros((8 - len(groups), LANES), jnp.int32)
    copy = pltpu.make_async_copy(flags, bits, sems.at[4])
    copy.start()
    copy.wait()

    list_slots(bits, 0, rows, cols, ((NEAR, 1), (cols - 1 - NEAR, -1)), lists, slots)
    fetch[2].wait()
    fetch[3].wait()

    def gather(group, _):
        for u in range(8):
            n = group * 8 + u
            low_ref[pl.ds(n, 1), :] = buf[pl.ds(lists[0, n], 1), :]
            high_ref[pl.ds(n, 1), :] = buf[pl.ds(lists[1, n], 1), :]
        return 0

    lax.fori_loop(0, slots // 8, gather, 0)


def weights_kernel(bits_ref, wide_ref, pick_ref, frac_ref, taken, counts, sent, *, rows, slots):
    kinds, wide, _ = wide_ref.shape
    cols = wide - 2 * NEAR
    list_slots(bits_ref, 2, rows, LANES, ((SIDE - 1 - NEAR, -1), (SIDE + cols + NEAR, 1)), taken, slots)
    list_slots(bits_ref, 0, rows, LANES, ((0, 0), (0, 0)), sent, slots)
    for side in range(2):
        counts[side] = jnp.maximum(taken[side, slots + 1], sent[side, slots + 1])
    groups, band = wide // 8, wide - 2 * NEAR + 2 * SIDE
    place = lax.broadcasted_iota(jnp.int32, (8, LANES), 1)
    place = jnp.where(place < band, place, place - band).astype(jnp.float32)
    column = lax.broadcasted_iota(jnp.int32, (8, LANES), 0) * groups + (SIDE - NEAR)
    for turn in range(TRAJ):
        for k in range(groups):
            target = wide_ref[turn, pl.ds(k, 8, stride=groups), :] + (column + k).astype(jnp.float32)
            frac = wide_ref[TRAJ + turn, pl.ds(k, 8, stride=groups), :]
            at = slice(turn * wide + 8 * k, turn * wide + 8 * k + 8)
            for m in range(rows):
                pick_ref[m, at, :] = jnp.where(target[:, m : m + 1] == place, 1.0, 0.0)
                frac_ref[m, at, :] = jnp.broadcast_to(frac[:, m : m + 1], (8, LANES))


def main_kernel(
    rows,
    cols,
    slots,
    info_ref,
    lists_ref,
    state_ref,
    edge_ref,
    low_a_ref,
    low_b_ref,
    high_a_ref,
    high_b_ref,
    far_low_ref,
    far_high_ref,
    full_ref,
    counts_ref,
    pick_any,
    frac_any,
    stiff_ref,
    out_any,
    out_ref,
    full,
    ext,
    rhs,
    xa,
    xb,
    nat,
    pick_ref,
    frac_ref,
    sems,
):
    lat_rows = state_ref.shape[0]
    tiles = state_ref.shape[2] // LEV
    wide = cols + 2 * NEAR
    groups = wide // 8
    own0 = jnp.where(info_ref[0] == 0, 0, NEAR)
    ext0 = jnp.where(info_ref[0] == 0, lat_rows, 0)
    copies = []
    for f in range(tiles):
        lanes = pl.ds(f * LEV, LEV)
        copies.append(
            pltpu.make_async_copy(
                state_ref.at[:, :, lanes],
                ext.at[f, pl.ds(own0, lat_rows), pl.ds(SIDE, cols), :],
                sems.at[f],
            )
        )
        copies[-1].start()
        copies.append(
            pltpu.make_async_copy(
                edge_ref.at[:, :, lanes],
                ext.at[f, pl.ds(ext0, NEAR), pl.ds(SIDE, cols), :],
                sems.at[tiles + f],
            )
        )
        copies[-1].start()
    copies.append(pltpu.make_async_copy(pick_any, pick_ref, sems.at[2 * tiles]))
    copies.append(pltpu.make_async_copy(frac_any, frac_ref, sems.at[2 * tiles + 1]))
    copies[-2].start()
    copies[-1].start()

    zero = jnp.zeros((8, LEV), jnp.float32)

    def clear(e, _):
        for f in range(tiles):
            for start in (0, 8, SIDE + cols, SIDE + cols + 8):
                ext[f, e, start : start + 8, :] = zero
        return 0

    lax.fori_loop(0, rows, clear, 0)
    for f in range(tiles):
        for start in range(0, SIDE * 2 + cols, 8):
            ext[f, rows, start : start + 8, :] = zero
        for k in range(groups):
            xa[f, rows, 8 * k : 8 * k + 8, :] = zero
            xb[f, rows, 8 * k : 8 * k + 8, :] = zero
    half = low_a_ref.shape[0] // NEAR

    def near(m, base, refs):
        e = jnp.where(m < lat_rows, own0 + m, ext0 + m - lat_rows)
        start = pl.multiple_of(base, 8)
        for ref, col in zip(refs, (SIDE - NEAR, SIDE + cols)):
            two = ref[pl.ds(start, 2 * NEAR), :]
            for f in range(tiles):
                for v in range(2):
                    ext[f, e + v, col : col + NEAR, :] = two[v * NEAR : (v + 1) * NEAR, f * LEV : (f + 1) * LEV]

    def near_a(group, _):
        near(2 * group, group * 8, (low_a_ref, high_a_ref))
        return 0

    def near_b(group, _):
        near(half + 2 * group, group * 8, (low_b_ref, high_b_ref))
        return 0

    lax.fori_loop(0, half // 2, near_a, 0)
    lax.fori_loop(0, (rows - half) // 2, near_b, 0)
    for side, far_ref in enumerate((far_low_ref, far_high_ref)):

        def put(m, col, column):
            e = jnp.where(m < lat_rows, own0 + m, ext0 + m - lat_rows)
            for f in range(tiles):
                ext[f, e, pl.ds(col, 1), :] = column[:, f * LEV : (f + 1) * LEV]

        @pl.when(counts_ref[side] <= slots)
        def _(side=side, far_ref=far_ref, put=put):
            def place(n, _):
                address = lists_ref[side, n]
                put(address >> 7, address & (LANES - 1), far_ref[pl.ds(n, 1), :])
                return 0

            lax.fori_loop(0, lists_ref[side, slots + 1], place, 0)

        @pl.when(counts_ref[side] > slots)
        def _(side=side, put=put):
            copy = pltpu.make_async_copy(full_ref.at[side], full, sems.at[2 * tiles + 2])
            copy.start()
            copy.wait()
            first_col = (SIDE - NEAR - FAR, SIDE + cols + NEAR)[side]

            def place(m, _):
                for j in range(FAR):
                    put(m, first_col + j, full[pl.ds(m * FAR + j, 1), :])
                return 0

            lax.fori_loop(0, rows, place, 0)

    for copy in copies:
        copy.wait()

    top = lax.broadcasted_iota(jnp.int32, (wide, LEV), 1) == LEV - 1

    def upstream(group, _):
        for v in range(UP_ROWS):
            e = group * UP_ROWS + v
            his, los = [], []
            for f in range(tiles):
                value = ext[f, e]
                hi = value.astype(jnp.bfloat16)
                his.append(hi)
                los.append((value - hi.astype(jnp.float32)).astype(jnp.bfloat16))
            band = jnp.concatenate([jnp.concatenate(his, axis=1), jnp.concatenate(los, axis=1)], axis=0)
            own = (e >= own0) & (e < own0 + lat_rows)
            m = jnp.where(own, e - own0, e - ext0 + lat_rows)
            got = jnp.dot(pick_ref[m].astype(jnp.bfloat16), band, preferred_element_type=jnp.float32)
            for turn in range(TRAJ):
                frac = frac_ref[m, turn * wide : (turn + 1) * wide, :]
                for f in range(tiles):
                    u = got[turn * wide : (turn + 1) * wide, f * LEV : (f + 1) * LEV]
                    up = jnp.where(top, u, pltpu.roll(u, LEV - 1, 1))
                    rhs[turn, f, e] = u + frac * (up - u)
        return 0

    lax.fori_loop(0, rows // UP_ROWS, upstream, 0)

    def tile(f, _):
        s = stiff_ref[f]
        prev = 1.0
        for sweep in range(2 * TRAJ):
            omega = OMEGAS[sweep % 2]
            alpha = jnp.broadcast_to((1.0 - omega - 4.0 * omega * s) * (prev / omega), (8, LEV))
            beta = jnp.broadcast_to(s * prev, (8, LEV))
            prev = omega
            turn = sweep // 2
            src, dst = (None, xa, xb, xa)[sweep], (xa, xb, xa, None)[sweep]

            def load(e, src=src):
                if src is None:
                    return [ext[f, e, pl.ds(SIDE - NEAR + k, 8, stride=groups), :] for k in range(groups)]
                return [src[f, e, 8 * k : 8 * k + 8, :] for k in range(groups)]

            def block(group, carry, load=load, dst=dst, alpha=alpha, beta=beta, turn=turn, omega=omega):
                south, mid = carry
                for v in range(SWEEP_ROWS):
                    e = group * SWEEP_ROWS + v
                    north = load(e + 1)
                    for k in range(groups):
                        west = mid[k - 1] if k else pltpu.roll(mid[groups - 1], 1, 0)
                        east = mid[k + 1] if k < groups - 1 else pltpu.roll(mid[0], 7, 0)
                        around = (south[k] + north[k]) + (west + east)
                        new = alpha * mid[k] + beta * around + rhs[turn, f, e, 8 * k : 8 * k + 8, :]
                        if dst is None:
                            nat[e, pl.ds(k, 8, stride=groups), :] = new * omega
                        else:
                            dst[f, e, 8 * k : 8 * k + 8, :] = new
                    south, mid = mid, north
                return south, mid

            lax.fori_loop(0, rows // SWEEP_ROWS, block, ([zero] * groups, load(0)))

        for r in range(lat_rows):
            out_ref[f, r] = nat[own0 + r, NEAR : NEAR + cols, :]
        lanes = pl.ds(pl.multiple_of(f * LEV, LEV), LEV)
        pltpu.make_async_copy(out_ref.at[f], out_any.at[:, :, lanes], sems.at[f]).start()
        return 0

    lax.fori_loop(0, tiles, tile, 0)
    for f in range(tiles):
        pltpu.make_async_copy(out_ref.at[f], out_any.at[:, :, pl.ds(f * LEV, LEV)], sems.at[f]).wait()


def shards(state, dep_shift, dep_frac, stiff):
    lat_rows, cols, width = state.shape
    tiles = width // LEV
    rows = lat_rows + NEAR
    wide = cols + 2 * NEAR
    band = cols + 2 * SIDE
    kinds = 2 * TRAJ
    lat = lax.axis_index("lat")
    low = lat == 0
    right, left = ring("lon", 1), ring("lon", -1)
    swap = ring("lat", 1)
    info = lat[None]
    shape = functools.partial(jax.ShapeDtypeStruct, dtype=jnp.float32)
    smem = pl.BlockSpec(memory_space=pltpu.SMEM)
    vmem = pl.BlockSpec(memory_space=pltpu.VMEM)
    anywhere = pl.BlockSpec(memory_space=pl.ANY)

    half = shape((lat_rows // 2 * NEAR, width))
    own, edge, left_a, left_b, right_a, right_b = pl.pallas_call(
        start_kernel,
        out_shape=(shape((kinds, cols, LANES)), shape((NEAR, cols, width)), half, half, half, half),
        in_specs=[smem, vmem, vmem, anywhere],
        out_specs=(vmem,) * 6,
        scratch_shapes=[
            pltpu.VMEM((LANES, LANES), jnp.float32),
            pltpu.VMEM((2, lat_rows, 8, width), jnp.float32),
            pltpu.SemaphoreType.DMA((3,)),
        ],
        compiler_params=pltpu.CompilerParams(vmem_limit_bytes=16 * 2**20),
    )(info, dep_shift, dep_frac, state)
    other = lax.ppermute(own, "lat", swap)
    edge = lax.ppermute(edge, "lat", swap)
    low_a = lax.ppermute(right_a, "lon", right)
    high_a = lax.ppermute(left_a, "lon", left)
    head = shape((8, width))
    more = shape((half.shape[0] + NEAR * NEAR, width))
    to_left, to_right, left_b, right_b, dep = pl.pallas_call(
        functools.partial(second_kernel, rows=rows),
        out_shape=(head, head, more, more, shape((kinds, cols, LANES))),
        in_specs=[smem] + [vmem] * 5,
        out_specs=(vmem,) * 5,
    )(info, own, other, edge, left_b, right_b)
    from_left = lax.ppermute(to_right, "lon", right)
    from_right = lax.ppermute(to_left, "lon", left)
    low_b = lax.ppermute(right_b, "lon", right)
    high_b = lax.ppermute(left_b, "lon", left)

    message = shape((SLOTS, width))
    send_low, send_high, flags, around = pl.pallas_call(
        functools.partial(pack_kernel, rows=rows, slots=SLOTS),
        out_shape=(message, message, jax.ShapeDtypeStruct((8, LANES), jnp.int32), shape((kinds, wide, LANES))),
        in_specs=[smem, vmem] + [anywhere] * 4,
        out_specs=(vmem,) * 4,
        scratch_shapes=[
            pltpu.VMEM((rows * cols, width), jnp.float32),
            pltpu.VMEM((2, 8, width), jnp.float32),
            pltpu.SMEM((8, LANES), jnp.int32),
            pltpu.SMEM((2, SLOTS + 8), jnp.int32),
            pltpu.SemaphoreType.DMA((5,)),
        ],
        compiler_params=pltpu.CompilerParams(vmem_limit_bytes=16 * 2**20),
        cost_estimate=pl.CostEstimate(flops=0, bytes_accessed=4 * 2**20, transcendentals=0),
    )(info, dep, state.reshape(lat_rows * cols, width), edge.reshape(NEAR * cols, width), from_left, from_right)
    far_high = lax.ppermute(send_low, "lon", left)
    far_low = lax.ppermute(send_high, "lon", right)

    pick, frac, taken, counts = pl.pallas_call(
        functools.partial(weights_kernel, rows=rows, slots=SLOTS),
        out_shape=(
            shape((rows, TRAJ * wide, LANES)),
            shape((rows, TRAJ * wide, LANES)),
            jax.ShapeDtypeStruct((2, SLOTS + 8), jnp.int32),
            jax.ShapeDtypeStruct((2,), jnp.int32),
        ),
        in_specs=[smem, vmem],
        out_specs=(vmem, vmem, smem, smem),
        scratch_shapes=[pltpu.SMEM((2, SLOTS + 8), jnp.int32)],
        compiler_params=pltpu.CompilerParams(vmem_limit_bytes=16 * 2**20),
    )(flags, around)

    over_left, over_right = counts[0] > SLOTS, counts[1] > SLOTS
    size = -(-rows * FAR // 8) * 8
    nothing = jnp.zeros((size, width), jnp.float32)

    def whole():
        field = jnp.concatenate([state, edge], axis=0)
        pad = ((0, size - rows * FAR), (0, 0))
        at_left = jnp.pad(field[:, NEAR : NEAR + FAR].reshape(rows * FAR, width), pad)
        at_right = jnp.pad(field[:, cols - NEAR - FAR : cols - NEAR].reshape(rows * FAR, width), pad)
        even = lax.axis_index("lon") % 2 == 0
        got_even = lax.cond(
            jnp.where(even, over_right, over_left),
            lambda: lax.ppermute(jnp.where(even, at_right, at_left), "lon", pairs("lon", 0)),
            lambda: nothing,
        )
        got_odd = lax.cond(
            jnp.where(even, over_left, over_right),
            lambda: lax.ppermute(jnp.where(even, at_left, at_right), "lon", pairs("lon", 1)),
            lambda: nothing,
        )
        return jnp.where(even, jnp.stack([got_odd, got_even]), jnp.stack([got_even, got_odd]))

    full = lax.cond(over_left | over_right, whole, lambda: jnp.stack([nothing, nothing]))

    return pl.pallas_call(
        functools.partial(main_kernel, rows, cols, SLOTS),
        out_shape=shape(state.shape),
        in_specs=[smem, smem, anywhere, anywhere] + [vmem] * 6 + [anywhere, smem] + [anywhere] * 2 + [vmem],
        out_specs=anywhere,
        scratch_shapes=[
            pltpu.VMEM((tiles, lat_rows, cols, LEV), jnp.float32),
            pltpu.VMEM((size, width), jnp.float32),
            pltpu.VMEM((tiles, rows + 1, band, LEV), jnp.float32),
            pltpu.VMEM((TRAJ, tiles, rows, wide, LEV), jnp.float32),
            pltpu.VMEM((tiles, rows + 1, wide, LEV), jnp.float32),
            pltpu.VMEM((tiles, rows + 1, wide, LEV), jnp.float32),
            pltpu.VMEM((rows, wide, LEV), jnp.float32),
            pltpu.VMEM((rows, TRAJ * wide, LANES), jnp.float32),
            pltpu.VMEM((rows, TRAJ * wide, LANES), jnp.float32),
            pltpu.SemaphoreType.DMA((2 * tiles + 3,)),
        ],
        compiler_params=pltpu.CompilerParams(vmem_limit_bytes=40 * 2**20),
        cost_estimate=pl.CostEstimate(flops=200_000_000, bytes_accessed=8 * 2**20, transcendentals=0),
    )(
        info, taken, state, edge, low_a, low_b, high_a, high_b, far_low, far_high, full, counts, pick, frac,
        stiff.reshape(tiles, 1, LEV),
    )


def solution(mesh):
    in_specs = (
        P(("member", "lat"), "lon", None),
        P(None, ("member", "lat"), "lon"),
        P(None, ("member", "lat"), "lon"),
        P(),
    )
    out_specs = P(("member", "lat"), "lon", None)
    return jax.shard_map(shards, mesh=mesh, in_specs=in_specs, out_specs=out_specs, check_vma=False)
```

time: 97.1 us -> 62 us (0.64)
  waiting for transfers between devices: 37.3 us -> 11.1 us
  Pallas kernels: 0 us -> 25.8 us
  starting transfers between devices: 33.9 us -> 16 us
  other arithmetic: 16.1 us -> 0 us
  matrix products: 3.73 us -> 0 us
  local copies, waits for them, and re-layouts: 5.43 us -> 7.4 us
  between operations: 0.31 us -> 1.39 us
    ppermute x18 -> x10, waiting for transfers between devices: 37.3 us -> 11.1 us  [the longest x1 9.76 us: shards(): high_a = lax.ppermute(left_a, 'lon', left)]
    pallas_call x0 -> x5, Pallas kernels: none -> 25.8 us  [the longest x1 12.6 us: shards(): pl.pallas_call(functools.partial(main_kernel, rows, cols, SLOTS), out_sha...]
    ppermute x18 -> x10, starting transfers between devices: 33.9 us -> 16 us  [the longest x1 4.68 us: shards(): far_high = lax.ppermute(send_low, 'lon', left)]
    add x6 -> x0, other arithmetic: 16 us -> none  [the longest x4 15.9 us: relax(): return center + omega * resid]
    unnamed x10 -> x24, local copies, waits for them, and re-layouts: 0.23 us -> 5.66 us
    slice x9 -> x1, local copies, waits for them, and re-layouts: 5.15 us -> 0.58 us  [shards(): over_left, over_right = (counts[0] > SLOTS, counts[1] > SLOTS)]
    dot_general x2 -> x0, matrix products: 3.73 us -> none  [shards(): jnp.einsum('rqk,rkf->rqf', picker, banded, precision=lax.Precision.HIGHEST)]
    another operation x0 -> x1, local copies, waits for them, and re-layouts: none -> 1.15 us
  transfers between devices with their start and end apart: 18 -> 10, of which waited for: 7 -> 2; matrix products, arithmetic and copies ran while one was open for 8% -> 3% of each run, Pallas kernels for 0% -> 15%
where the time goes in v1:
time: 62 us; the launch traced here: 61.6 us
  Pallas kernels  25.8 us (42%)
  starting transfers between devices  16 us (26%)
  waiting for transfers between devices  11.1 us (18%)
  local copies, waits for them, and re-layouts  7.4 us (12%)
  between operations  1.39 us (2%)
    pallas_call x1, Pallas kernels, shards(): pl.pallas_call(functools.partial(main_kernel, rows, cols, SLOTS), out_sha...  12.6 us
    ppermute x1, waiting for transfers between devices, shards(): high_a = lax.ppermute(left_a, 'lon', left)  9.76 us
    unnamed x24, local copies, waits for them, and re-layouts  5.66 us
    pallas_call x1, Pallas kernels, shards(): pl.pallas_call(functools.partial(weights_kernel, rows=rows, slots=SLOTS),...  5.34 us
    ppermute x1, starting transfers between devices, shards(): far_high = lax.ppermute(send_low, 'lon', left)  4.68 us
    pallas_call x1, Pallas kernels, shards(): pl.pallas_call(functools.partial(pack_kernel, rows=rows, slots=SLOTS), ou...  3.88 us
    ppermute x1, starting transfers between devices, shards(): high_b = lax.ppermute(left_b, 'lon', left)  3.37 us
    ppermute x1, starting transfers between devices, shards(): from_right = lax.ppermute(to_left, 'lon', left)  3.05 us
  transfers between devices with their start and end apart: 10, of which 2 were waited for; matrix products, arithmetic and copies ran while one was open for 3% of the time, Pallas kernels for 15%

profile of v1, /device:TPU:0, one launch (start us, length us, event | category | flops | bytes accessed | tf_op | source)
XLA Modules:
  0.0 61.6 jit_solution(15732917400219246354)
XLA Ops:
  0.0 0.0 copy-start.4
  0.0 0.8 %copy-done.4 = s32[2,32,32]{2,1,0:T(8,128)S(1)} copy-done((s32[2,32,32]{2,1,0:T(8,128)S(1)}, s32[2,32,32]{2,1,0:T(8,128)}, u32[]{:S(2)}) %copy-start.4) | copy-done | bytes 8216
  0.8 0.0 copy-start.5
  0.8 0.8 %copy-done.5 = f32[2,32,32]{2,1,0:T(8,128)S(1)} copy-done((f32[2,32,32]{2,1,0:T(8,128)S(1)}, f32[2,32,32]{2,1,0:T(8,128)}, u32[]{:S(2)}) %copy-start.5) | copy-done | bytes 8216
  1.5 2.1 %shard_map.46 = (f32[4,32,128]{2,1,0:T(8,128)S(1)}, f32[4,32,640]{2,1,0:T(8,128)S(1)}, f32[64,640]{1,0:T(8,128)S(1)}, f32[64,640]{1,0:T(8,128)S(1)}, f32[64,640]{1,0:T(8,128)}, /*index=5*/f32[64,640]{1,0:T(8,128)S(1)}) custom-call(s32[1]{0:T(128)} %bitcast.2.info_ref, s32[2,32,32]{2,1,0:T(8,128)S(1)} %copy-done.4, f32[2,32,32]{2,1,0:T(8,128)S(1)} %copy-done.5, ...), custom_call_target="tpu_custom_call" | custom-call | tf_op jit(solution)/shard_map/pallas_call | solution.py:457
  3.6 0.0 copy-start
  3.6 0.7 %copy-done = f32[64,640]{1,0:T(8,128)} copy-done((f32[64,640]{1,0:T(8,128)}, f32[64,640]{1,0:T(8,128)S(1)}, u32[]{:S(2)}) %copy-start) | copy-done | bytes 163864
  4.3 0.0 copy-start.1
  4.3 0.7 %copy-done.1 = f32[64,640]{1,0:T(8,128)} copy-done((f32[64,640]{1,0:T(8,128)}, f32[64,640]{1,0:T(8,128)S(1)}, u32[]{:S(2)}) %copy-start.1) | copy-done | bytes 163864
  4.9 0.0 copy-start.3
  4.9 0.0 copy-start.8
  4.9 0.5 collective-permute-start.3
  5.4 0.1 collective-permute-start.2
  5.4 1.3 %collective-permute-done.2.next_ref = f32[4,32,128]{2,1,0:T(8,128)S(1)} collective-permute-done((f32[4,32,128]{2,1,0:T(8,128)S(1)}, f32[4,32,128]{2,1,0:T(8,128)S(1)}, u32[]{:S(2)}, u32[]{:S(2)}) %collective-permute-start.2) | collective-permute-done | bytes 65568 | tf_op jit(solution)/shard_map/ppermute | solution.py:469
  6.7 0.0 copy-start.11
  6.7 0.0 collective-permute-done.3.edge_ref
  6.7 0.0 copy-start.9
  6.7 0.0 copy-done.3
  6.7 0.6 copy-done.11
  7.4 1.9 %shard_map.47 = (f32[8,640]{1,0:T(8,128)}, f32[8,640]{1,0:T(8,128)}, f32[80,640]{1,0:T(8,128)}, f32[80,640]{1,0:T(8,128)}, f32[4,32,128]{2,1,0:T(8,128)}) custom-call(s32[1]{0:T(128)} %bitcast.2.info_ref, f32[4,32,128]{2,1,0:T(8,128)} %copy-done.3, f32[4,32,128]{2,1,0:T(8,128)} %copy-done.11, f32[4,32,640]{2,1,0:T(8,128)S(1)} %collective-permute-done.3.edge_ref, ...), custom_call_target="tpu_custom_call" | custom-call | tf_op jit(solution)/shard_map/pallas_call | solution.py:475
  9.3 2.9 %collective-permute-start.4 = (f32[8,640]{1,0:T(8,128)}, f32[8,640]{1,0:T(8,128)S(1)}, u32[]{:S(2)}, u32[]{:S(2)}) collective-permute-start(f32[8,640]{1,0:T(8,128)} %get-tuple-element.70), channel_id=1, source_target_pairs={{0,2},{2,4},{4,6},{6,8},{8,10},{10,12},{12,14},{14,0},{1,3},{3,5},... | collective-permute-start | bytes 61448 | tf_op jit(solution)/shard_map/ppermute | solution.py:481
  12.2 3.1 %collective-permute-start.5 = (f32[8,640]{1,0:T(8,128)}, f32[8,640]{1,0:T(8,128)S(1)}, u32[]{:S(2)}, u32[]{:S(2)}) collective-permute-start(f32[8,640]{1,0:T(8,128)} %get-tuple-element.71), channel_id=1, source_target_pairs={{0,14},{2,0},{4,2},{6,4},{8,6},{10,8},{12,10},{14,12},{1,15},{3,1}... | collective-permute-start | bytes 61448 | tf_op jit(solution)/shard_map/ppermute | solution.py:482
  15.2 0.0 collective-permute-start.6
  15.2 1.4 %collective-permute-start.7 = (f32[80,640]{1,0:T(8,128)}, f32[80,640]{1,0:T(8,128)S(1)}, u32[]{:S(2)}, u32[]{:S(2)}) collective-permute-start(f32[80,640]{1,0:T(8,128)} %get-tuple-element.76), channel_id=1, source_target_pairs={{0,2},{2,4},{4,6},{6,8},{8,10},{10,12},{12,14},{14,0},{1,3},{3,5},... | collective-permute-start | bytes 614408 | tf_op jit(solution)/shard_map/ppermute | solution.py:483
  16.6 3.4 %collective-permute-start.9 = (f32[80,640]{1,0:T(8,128)}, f32[80,640]{1,0:T(8,128)S(1)}, u32[]{:S(2)}, u32[]{:S(2)}) collective-permute-start(f32[80,640]{1,0:T(8,128)} %get-tuple-element.78), channel_id=1, source_target_pairs={{0,14},{2,0},{4,2},{6,4},{8,6},{10,8},{12,10},{14,12},{1,15},{3,1}... | collective-permute-start | bytes 614408 | tf_op jit(solution)/shard_map/ppermute | solution.py:484
  20.0 0.0 collective-permute-done.4.from_left_ref
  20.0 0.0 collective-permute-done.5.from_right_ref
  20.0 0.0 copy-done.8
  20.0 0.0 copy-start.2
  20.0 0.8 %copy-done.2 = f32[4,32,128]{2,1,0:T(8,128)S(1)} copy-done((f32[4,32,128]{2,1,0:T(8,128)S(1)}, f32[4,32,128]{2,1,0:T(8,128)}, u32[]{:S(2)}) %copy-start.2) | copy-done | bytes 65560
  20.8 3.9 %shard_map.48 = (f32[80,640]{1,0:T(8,128)S(1)}, f32[80,640]{1,0:T(8,128)S(1)}, s32[8,128]{1,0:T(8,128)S(1)}, f32[4,40,128]{2,1,0:T(8,128)S(1)}) custom-call(s32[1]{0:T(128)} %bitcast.2.info_ref, f32[4,32,128]{2,1,0:T(8,128)S(1)} %copy-done.2, f32[1024,640]{1,0:T(8,128)} %bitcast.7, f32[128,640]{1,0:T(8,128)S(1)} %bitcast.8, ...), custom_call_target="tpu_custom_call" | custom-call | bytes 4194304 | tf_op jit(solution)/shard_map/pallas_call | solution.py:487
  24.7 0.0 copy-done.9
  24.7 0.0 copy-start.6
  24.7 0.7 %copy-done.6 = f32[80,640]{1,0:T(8,128)} copy-done((f32[80,640]{1,0:T(8,128)}, f32[80,640]{1,0:T(8,128)S(1)}, u32[]{:S(2)}) %copy-start.6) | copy-done | bytes 204824
  25.4 0.0 copy-start.7
  25.4 0.7 %copy-done.7 = f32[80,640]{1,0:T(8,128)} copy-done((f32[80,640]{1,0:T(8,128)}, f32[80,640]{1,0:T(8,128)S(1)}, u32[]{:S(2)}) %copy-start.7) | copy-done | bytes 204824
  26.1 5.3 %shard_map.49 = (f32[36,80,128]{2,1,0:T(8,128)S(1)}, f32[36,80,128]{2,1,0:T(8,128)S(1)}, s32[2,88]{1,0:T(2,128)S(1)}, s32[2]{0:T(128)S(1)}) custom-call(s32[8,128]{1,0:T(8,128)S(1)} %get-tuple-element.72.bits_ref, f32[4,40,128]{2,1,0:T(8,128)S(1)} %get-tuple-element.73.wide_ref), custom_call_target="tpu_custom_call" | custom-call | tf_op jit(solution)/shard_map/pallas_call | solution.py:505
  31.4 0.6 fusion.1
  33.3 0.1 collective-permute-start.10
  33.4 0.0 copy-start.12
  33.4 1.2 %conditional.3 = (f32[2,256,640]{2,1,0:T(8,128)}) conditional(s32[]{:T(128)} %convert_element_type.12, () %tuple.27, (pred[]{:T(512)}, pred[]{:T(512)}, f32[32,32,640]{2,1,0:T(8,128)}, f32[4,32,640]{2,1,0:T(8,128)}) %tuple.37), branch_computations={%region_0.0_spmd, %region_1.6_spmd} | conditional | flops 1310739 | bytes 26767716 | solution.py:541
  33.4 1.1 %broadcast.7 = f32[2,256,640]{2,1,0:T(8,128)} broadcast(f32[]{:T(128)} %constant.25.clone), dimensions={} | broadcast | bytes 1310724 | tf_op jit(solution)/shard_map/broadcast.1
  34.5 4.7 %collective-permute-start.11 = (f32[80,640]{1,0:T(8,128)}, f32[80,640]{1,0:T(8,128)}, u32[]{:S(2)}, u32[]{:S(2)}) collective-permute-start(f32[80,640]{1,0:T(8,128)} %copy-done.6), channel_id=1, source_target_pairs={{0,14},{2,0},{4,2},{6,4},{8,6},{10,8},{12,10},{14,12},{1,15},{3,1}... | collective-permute-start | bytes 614408 | tf_op jit(solution)/shard_map/ppermute | solution.py:502
  39.2 0.0 collective-permute-done.6.low_a_ref
  39.2 0.0 collective-permute-start.8
  39.3 0.0 copy-done.12
  39.3 9.8 %collective-permute-done.8.high_a_ref = f32[64,640]{1,0:T(8,128)} collective-permute-done((f32[64,640]{1,0:T(8,128)}, f32[64,640]{1,0:T(8,128)}, u32[]{:S(2)}, u32[]{:S(2)}) %collective-permute-start.8) | collective-permute-done | bytes 163872 | tf_op jit(solution)/shard_map/ppermute | solution.py:472
  49.0 0.0 collective-permute-done.7.low_b_ref
  49.0 0.0 collective-permute-done.9.high_b_ref
  49.0 0.0 collective-permute-done.10.far_low_ref
  49.0 0.0 collective-permute-done.11.far_high_ref
  49.1 12.6 %shard_map.50 = f32[32,32,640]{2,1,0:T(8,128)} custom-call(s32[1]{0:T(128)} %bitcast.2.info_ref, s32[2,88]{1,0:T(2,128)S(1)} %get-tuple-element.74.lists_ref, f32[32,32,640]{2,1,0:T(8,128)} %state_ref.3, f32[4,32,640]{2,1,0:T(8,128)} %copy-done.9, f32[64,640]{1,0:T(8,128)S(1)} %collective-permute-done.6.low_a_ref, ...), custom_call_target="tpu_custom_call" | custom-call | flops 200000000 | bytes 8388608 | tf_op jit(solution)/shard_map/pallas_call | solution.py:543
  (1 shorter events, 0.0 us)
Async XLA Ops:
  0.0 0.8 %copy-start.4 = (s32[2,32,32]{2,1,0:T(8,128)S(1)}, s32[2,32,32]{2,1,0:T(8,128)}, u32[]{:S(2)}) copy-start(s32[2,32,32]{2,1,0:T(8,128)} %shift_ref.1) | copy-start | bytes 24580
  0.8 0.8 %copy-start.5 = (f32[2,32,32]{2,1,0:T(8,128)S(1)}, f32[2,32,32]{2,1,0:T(8,128)}, u32[]{:S(2)}) copy-start(f32[2,32,32]{2,1,0:T(8,128)} %frac_ref.1) | copy-start | bytes 24580
  3.6 0.7 %copy-start = (f32[64,640]{1,0:T(8,128)}, f32[64,640]{1,0:T(8,128)S(1)}, u32[]{:S(2)}) copy-start(f32[64,640]{1,0:T(8,128)S(1)} %get-tuple-element.67.left_ref) | copy-start | bytes 491524
  4.3 0.7 %copy-start.1 = (f32[64,640]{1,0:T(8,128)}, f32[64,640]{1,0:T(8,128)S(1)}, u32[]{:S(2)}) copy-start(f32[64,640]{1,0:T(8,128)S(1)} %get-tuple-element.68.right_ref) | copy-start | bytes 491524
  4.9 1.8 %copy-start.3 = (f32[4,32,128]{2,1,0:T(8,128)}, f32[4,32,128]{2,1,0:T(8,128)S(1)}, u32[]{:S(2)}) copy-start(f32[4,32,128]{2,1,0:T(8,128)S(1)} %get-tuple-element.65.own_ref) | copy-start | bytes 196612
  4.9 15.0 %copy-start.8 = (f32[64,640]{1,0:T(8,128)}, f32[64,640]{1,0:T(8,128)S(1)}, u32[]{:S(2)}) copy-start(f32[64,640]{1,0:T(8,128)S(1)} %get-tuple-element.77) | copy-start | bytes 491524
  4.9 1.8 %collective-permute-start.3 = (f32[4,32,640]{2,1,0:T(8,128)S(1)}, f32[4,32,640]{2,1,0:T(8,128)S(1)}, u32[]{:S(2)}, u32[]{:S(2)}) collective-permute-start(f32[4,32,640]{2,1,0:T(8,128)S(1)} %get-tuple-element.66), channel_id=1, source_target_pairs={{0,1},{1,0},{2,3},{3,2},{4,5},{5,4},{6,7},{7,6},{8,9},{9,8},{10,11... | collective-permute-start | bytes 983048 | tf_op jit(solution)/shard_map/ppermute | solution.py:470
  5.4 1.3 %collective-permute-start.2 = (f32[4,32,128]{2,1,0:T(8,128)S(1)}, f32[4,32,128]{2,1,0:T(8,128)S(1)}, u32[]{:S(2)}, u32[]{:S(2)}) collective-permute-start(f32[4,32,128]{2,1,0:T(8,128)S(1)} %get-tuple-element.65.own_ref), channel_id=1, source_target_pairs={{0,1},{1,0},{2,3},{3,2},{4,5},{5,4},{6,7},{7,6},{8,9},{9,8},{10,11... | collective-permute-start | bytes 196616 | tf_op jit(solution)/shard_map/ppermute | solution.py:469
  6.7 0.6 copy-start.11
  6.7 18.0 %copy-start.9 = (f32[4,32,640]{2,1,0:T(8,128)}, f32[4,32,640]{2,1,0:T(8,128)S(1)}, u32[]{:S(2)}) copy-start(f32[4,32,640]{2,1,0:T(8,128)S(1)} %collective-permute-done.3.edge_ref) | copy-start | bytes 983044
  9.3 10.7 %collective-permute-start.4 = (f32[8,640]{1,0:T(8,128)}, f32[8,640]{1,0:T(8,128)S(1)}, u32[]{:S(2)}, u32[]{:S(2)}) collective-permute-start(f32[8,640]{1,0:T(8,128)} %get-tuple-element.70), channel_id=1, source_target_pairs={{0,2},{2,4},{4,6},{6,8},{8,10},{10,12},{12,14},{14,0},{1,3},{3,5},... | collective-permute-start | bytes 61448 | tf_op jit(solution)/shard_map/ppermute | solution.py:481
  12.2 7.8 %collective-permute-start.5 = (f32[8,640]{1,0:T(8,128)}, f32[8,640]{1,0:T(8,128)S(1)}, u32[]{:S(2)}, u32[]{:S(2)}) collective-permute-start(f32[8,640]{1,0:T(8,128)} %get-tuple-element.71), channel_id=1, source_target_pairs={{0,14},{2,0},{4,2},{6,4},{8,6},{10,8},{12,10},{14,12},{1,15},{3,1}... | collective-permute-start | bytes 61448 | tf_op jit(solution)/shard_map/ppermute | solution.py:482
  15.2 24.0 %collective-permute-start.6 = (f32[64,640]{1,0:T(8,128)}, f32[64,640]{1,0:T(8,128)S(1)}, u32[]{:S(2)}, u32[]{:S(2)}) collective-permute-start(f32[64,640]{1,0:T(8,128)} %get-tuple-element.75), channel_id=1, source_target_pairs={{0,2},{2,4},{4,6},{6,8},{8,10},{10,12},{12,14},{14,0},{1,3},{3,5},... | collective-permute-start | bytes 491528 | tf_op jit(solution)/shard_map/ppermute | solution.py:471
  15.2 33.8 %collective-permute-start.7 = (f32[80,640]{1,0:T(8,128)}, f32[80,640]{1,0:T(8,128)S(1)}, u32[]{:S(2)}, u32[]{:S(2)}) collective-permute-start(f32[80,640]{1,0:T(8,128)} %get-tuple-element.76), channel_id=1, source_target_pairs={{0,2},{2,4},{4,6},{6,8},{8,10},{10,12},{12,14},{14,0},{1,3},{3,5},... | collective-permute-start | bytes 614408 | tf_op jit(solution)/shard_map/ppermute | solution.py:483
  16.6 32.4 %collective-permute-start.9 = (f32[80,640]{1,0:T(8,128)}, f32[80,640]{1,0:T(8,128)S(1)}, u32[]{:S(2)}, u32[]{:S(2)}) collective-permute-start(f32[80,640]{1,0:T(8,128)} %get-tuple-element.78), channel_id=1, source_target_pairs={{0,14},{2,0},{4,2},{6,4},{8,6},{10,8},{12,10},{14,12},{1,15},{3,1}... | collective-permute-start | bytes 614408 | tf_op jit(solution)/shard_map/ppermute | solution.py:484
  20.0 0.8 %copy-start.2 = (f32[4,32,128]{2,1,0:T(8,128)S(1)}, f32[4,32,128]{2,1,0:T(8,128)}, u32[]{:S(2)}) copy-start(f32[4,32,128]{2,1,0:T(8,128)} %get-tuple-element.69.dep_ref) | copy-start | bytes 196612
  24.7 0.7 %copy-start.6 = (f32[80,640]{1,0:T(8,128)}, f32[80,640]{1,0:T(8,128)S(1)}, u32[]{:S(2)}) copy-start(f32[80,640]{1,0:T(8,128)S(1)} %get-tuple-element.80) | copy-start | bytes 614404
  25.4 0.7 %copy-start.7 = (f32[80,640]{1,0:T(8,128)}, f32[80,640]{1,0:T(8,128)S(1)}, u32[]{:S(2)}) copy-start(f32[80,640]{1,0:T(8,128)S(1)} %get-tuple-element.79) | copy-start | bytes 614404
  33.3 15.7 %collective-permute-start.10 = (f32[80,640]{1,0:T(8,128)}, f32[80,640]{1,0:T(8,128)}, u32[]{:S(2)}, u32[]{:S(2)}) collective-permute-start(f32[80,640]{1,0:T(8,128)} %copy-done.7), channel_id=1, source_target_pairs={{0,2},{2,4},{4,6},{6,8},{8,10},{10,12},{12,14},{14,0},{1,3},{3,5},... | collective-permute-start | bytes 614408 | tf_op jit(solution)/shard_map/ppermute | solution.py:503
  33.4 5.9 %copy-start.12 = (f32[640]{0:T(1024)S(1)}, f32[640]{0:T(1024)}, u32[]{:S(2)}) copy-start(f32[640]{0:T(1024)} %param.13) | copy-start | bytes 7684
  34.5 14.5 %collective-permute-start.11 = (f32[80,640]{1,0:T(8,128)}, f32[80,640]{1,0:T(8,128)}, u32[]{:S(2)}, u32[]{:S(2)}) collective-permute-start(f32[80,640]{1,0:T(8,128)} %copy-done.6), channel_id=1, source_target_pairs={{0,14},{2,0},{4,2},{6,4},{8,6},{10,8},{12,10},{14,12},{1,15},{3,1}... | collective-permute-start | bytes 614408 | tf_op jit(solution)/shard_map/ppermute | solution.py:502
  39.2 9.8 %collective-permute-start.8 = (f32[64,640]{1,0:T(8,128)}, f32[64,640]{1,0:T(8,128)}, u32[]{:S(2)}, u32[]{:S(2)}) collective-permute-start(f32[64,640]{1,0:T(8,128)} %copy-done.8), channel_id=1, source_target_pairs={{0,14},{2,0},{4,2},{6,4},{8,6},{10,8},{12,10},{14,12},{1,15},{3,1}... | collective-permute-start | bytes 491528 | tf_op jit(solution)/shard_map/ppermute | solution.py:472

commit v2 on v1

--- a/solution.py
+++ b/solution.py
@@ -39,10 +39,10 @@
     state_ref,
     own_ref,
     edge_ref,
-    left_a_ref,
-    left_b_ref,
-    right_a_ref,
-    right_b_ref,
+    left_ref,
+    right_ref,
+    shift,
+    frac,
     pad,
     sides,
     sems,
@@ -53,21 +53,23 @@
         pltpu.make_async_copy(state_ref.at[:, pl.ds(0, 8), :], sides.at[0], sems.at[0]),
         pltpu.make_async_copy(state_ref.at[:, pl.ds(cols - 8, 8), :], sides.at[1], sems.at[1]),
         pltpu.make_async_copy(state_ref.at[pl.ds(edge_row, NEAR)], edge_ref, sems.at[2]),
+        pltpu.make_async_copy(shift_ref, shift, sems.at[3]),
+        pltpu.make_async_copy(frac_ref, frac, sems.at[4]),
     ]
-    for copy in fetch:
+    for copy in reversed(fetch):
         copy.start()
     pad[...] = jnp.zeros_like(pad)
+    fetch[3].wait()
+    fetch[4].wait()
     for kind in range(2 * turns):
-        value = shift_ref[kind].astype(jnp.float32) if kind < turns else frac_ref[kind - turns]
+        value = shift[kind].astype(jnp.float32) if kind < turns else frac[kind - turns]
         pad[0:rows, 0:cols] = value
         own_ref[kind] = jnp.transpose(pad[...])[0:cols, :]
-    half = left_a_ref.shape[0] // NEAR
-    for side, (first, refs) in enumerate(((0, (left_a_ref, left_b_ref)), (8 - NEAR, (right_a_ref, right_b_ref)))):
+    for side, (first, ref) in enumerate(((0, left_ref), (8 - NEAR, right_ref))):
         fetch[side].wait()
         for r in range(0, rows, 2):
             two = jnp.concatenate([sides[side, r + v, first : first + NEAR, :] for v in range(2)], axis=0)
-            n = r % half * NEAR
-            refs[r // half][n : n + 2 * NEAR, :] = two
+            ref[r * NEAR : (r + 2) * NEAR, :] = two
     fetch[2].wait()
 
 
@@ -78,10 +80,10 @@
     edge_ref,
     left_ref,
     right_ref,
-    to_left_ref,
-    to_right_ref,
-    more_left_ref,
-    more_right_ref,
+    left_a_ref,
+    right_a_ref,
+    left_b_ref,
+    right_b_ref,
     dep_ref,
     *,
     rows,
@@ -90,39 +92,41 @@
     low = info_ref[0] == 0
     lat_rows = rows - NEAR
     lane = lax.broadcasted_iota(jnp.int32, (cols, LANES), 1)
-    head = jnp.zeros((8, to_left_ref.shape[1]), jnp.float32)
-    to_left_ref[...] = head
-    to_right_ref[...] = head
+    head = jnp.zeros((8, left_ref.shape[1]), jnp.float32)
+    left_a_ref[0:8, :] = head
+    right_a_ref[0:8, :] = head
     for kind in range(kinds):
         own, other = own_ref[kind], next_ref[kind]
         other = jnp.where(low, pltpu.roll(other, lat_rows, 1), pltpu.roll(other, NEAR, 1))
         both = jnp.where(lane < lat_rows, own, other)
         dep_ref[kind] = both
-        to_left_ref[0:NEAR, kind * LANES : (kind + 1) * LANES] = both[0:NEAR, :]
-        to_right_ref[0:NEAR, kind * LANES : (kind + 1) * LANES] = both[cols - NEAR : cols, :]
-    count = left_ref.shape[0]
-    more_left_ref[0:count, :] = left_ref[...]
-    more_right_ref[0:count, :] = right_ref[...]
+        left_a_ref[0:NEAR, kind * LANES : (kind + 1) * LANES] = both[0:NEAR, :]
+        right_a_ref[0:NEAR, kind * LANES : (kind + 1) * LANES] = both[cols - NEAR : cols, :]
+    some = left_a_ref.shape[0] - 8
+    rest = lat_rows * NEAR - some
+    left_a_ref[8 : 8 + some, :] = left_ref[0:some, :]
+    right_a_ref[8 : 8 + some, :] = right_ref[0:some, :]
+    left_b_ref[0:rest, :] = left_ref[some : some + rest, :]
+    right_b_ref[0:rest, :] = right_ref[some : some + rest, :]
     for r in range(NEAR):
-        more_left_ref[count + r * NEAR : count + r * NEAR + NEAR, :] = edge_ref[r, 0:NEAR, :]
-        more_right_ref[count + r * NEAR : count + r * NEAR + NEAR, :] = edge_ref[r, cols - NEAR : cols, :]
-
-
-def list_slots(bits_ref, which, rows, cols, firsts, list_ref, slots):
+        at = slice(rest + r * NEAR, rest + (r + 1) * NEAR)
+        left_b_ref[at, :] = edge_ref[r, 0:NEAR, :]
+        right_b_ref[at, :] = edge_ref[r, cols - NEAR : cols, :]
+
+
+def list_slots(bits_ref, which, rows, cols, firsts, list_ref):
     def row(m, counts):
         low, high = counts
         base = m * cols
         low_bits, high_bits = bits_ref[which, m], bits_ref[which + 1, m]
         for j in range(FAR):
-            list_ref[0, jnp.minimum(low, slots)] = base + (firsts[0][0] + firsts[0][1] * j)
-            list_ref[1, jnp.minimum(high, slots)] = base + (firsts[1][0] + firsts[1][1] * j)
+            list_ref[0, low] = base + (firsts[0][0] + firsts[0][1] * j)
+            list_ref[1, high] = base + (firsts[1][0] + firsts[1][1] * j)
             low = low + ((low_bits >> j) & 1)
             high = high + ((high_bits >> j) & 1)
         return low, high
 
-    low, high = lax.fori_loop(0, rows, row, (jnp.int32(0), jnp.int32(0)))
-    list_ref[0, slots + 1] = low
-    list_ref[1, slots + 1] = high
+    return lax.fori_loop(0, rows, row, (jnp.int32(0), jnp.int32(0)))
 
 
 def pack_kernel(
@@ -135,6 +139,7 @@
     low_ref,
     high_ref,
     flags,
+    sent,
     wide_ref,
     buf,
     heads,
@@ -151,8 +156,8 @@
     low = info_ref[0] == 0
     own, extra = lat_rows * cols, NEAR * cols
     fetch = [
-        pltpu.make_async_copy(from_left_ref, heads.at[0], sems.at[0]),
-        pltpu.make_async_copy(from_right_ref, heads.at[1], sems.at[1]),
+        pltpu.make_async_copy(from_left_ref.at[pl.ds(0, 8)], heads.at[0], sems.at[0]),
+        pltpu.make_async_copy(from_right_ref.at[pl.ds(0, 8)], heads.at[1], sems.at[1]),
         pltpu.make_async_copy(state_ref, buf.at[pl.ds(0, own)], sems.at[2]),
         pltpu.make_async_copy(edge_ref, buf.at[pl.ds(own, extra)], sems.at[3]),
     ]
@@ -183,24 +188,21 @@
         ([NEAR - r for r in reach], -1, -1),
         ([cols] * TRAJ, cols, 1),
     )
+    flags[...] = jnp.zeros_like(flags)
     for which, (first, anchor, sign) in enumerate(groups):
         total = jnp.zeros((1, LANES), jnp.int32)
-        hits = [jnp.zeros((1, LANES), bool) for _ in range(FAR)]
         for turn in range(TRAJ):
             for q in range(first[turn], first[turn] + NEAR + reach[turn]):
                 target = wide_ref[turn, q : q + 1, :].astype(jnp.int32) + (q - NEAR)
-                target = jnp.where(beyond <= reach[turn], target, -4 * LANES)
-                for j in range(FAR):
-                    hits[j] = hits[j] | (target == anchor + sign * (NEAR + j))
-        for j in range(FAR):
-            total = total + jnp.where(hits[j], 1 << j, 0)
+                j = sign * (target - anchor) - NEAR
+                hit = (j >= 0) & (j < FAR) & (beyond <= reach[turn])
+                total = total | jnp.where(hit, jnp.left_shift(1, jnp.maximum(j, 0)), 0)
         flags[which : which + 1, :] = total
-    flags[len(groups) : 8, :] = jnp.zeros((8 - len(groups), LANES), jnp.int32)
     copy = pltpu.make_async_copy(flags, bits, sems.at[4])
     copy.start()
     copy.wait()
 
-    list_slots(bits, 0, rows, cols, ((NEAR, 1), (cols - 1 - NEAR, -1)), lists, slots)
+    sent[0], sent[1] = list_slots(bits, 0, rows, cols, ((NEAR, 1), (cols - 1 - NEAR, -1)), lists)
     fetch[2].wait()
     fetch[3].wait()
 
@@ -214,13 +216,14 @@
     lax.fori_loop(0, slots // 8, gather, 0)
 
 
-def weights_kernel(bits_ref, wide_ref, pick_ref, frac_ref, taken, counts, sent, *, rows, slots):
+def weights_kernel(bits_ref, sent_ref, wide_ref, _, pick_ref, frac_ref, taken, counts, over, *, rows, slots):
     kinds, wide, _ = wide_ref.shape
     cols = wide - 2 * NEAR
-    list_slots(bits_ref, 2, rows, LANES, ((SIDE - 1 - NEAR, -1), (SIDE + cols + NEAR, 1)), taken, slots)
-    list_slots(bits_ref, 0, rows, LANES, ((0, 0), (0, 0)), sent, slots)
+    got = list_slots(bits_ref, 2, rows, LANES, ((SIDE - 1 - NEAR, -1), (SIDE + cols + NEAR, 1)), taken)
     for side in range(2):
-        counts[side] = jnp.maximum(taken[side, slots + 1], sent[side, slots + 1])
+        counts[side] = got[side]
+        counts[2 + side] = jnp.maximum(got[side], sent_ref[side])
+    over[0] = (jnp.maximum(counts[2], counts[3]) > slots).astype(jnp.int32)
     groups, band = wide // 8, wide - 2 * NEAR + 2 * SIDE
     place = lax.broadcasted_iota(jnp.int32, (8, LANES), 1)
     place = jnp.where(place < band, place, place - band).astype(jnp.float32)
@@ -311,7 +314,7 @@
         for k in range(groups):
             xa[f, rows, 8 * k : 8 * k + 8, :] = zero
             xb[f, rows, 8 * k : 8 * k + 8, :] = zero
-    half = low_a_ref.shape[0] // NEAR
+    half = (low_a_ref.shape[0] - 8) // NEAR
 
     def near(m, base, refs):
         e = jnp.where(m < lat_rows, own0 + m, ext0 + m - lat_rows)
@@ -323,7 +326,7 @@
                     ext[f, e + v, col : col + NEAR, :] = two[v * NEAR : (v + 1) * NEAR, f * LEV : (f + 1) * LEV]
 
     def near_a(group, _):
-        near(2 * group, group * 8, (low_a_ref, high_a_ref))
+        near(2 * group, 8 + group * 8, (low_a_ref, high_a_ref))
         return 0
 
     def near_b(group, _):
@@ -339,16 +342,16 @@
             for f in range(tiles):
                 ext[f, e, pl.ds(col, 1), :] = column[:, f * LEV : (f + 1) * LEV]
 
-        @pl.when(counts_ref[side] <= slots)
+        @pl.when(counts_ref[2 + side] <= slots)
         def _(side=side, far_ref=far_ref, put=put):
             def place(n, _):
                 address = lists_ref[side, n]
                 put(address >> 7, address & (LANES - 1), far_ref[pl.ds(n, 1), :])
                 return 0
 
-            lax.fori_loop(0, lists_ref[side, slots + 1], place, 0)
-
-        @pl.when(counts_ref[side] > slots)
+            lax.fori_loop(0, counts_ref[side], place, 0)
+
+        @pl.when(counts_ref[2 + side] > slots)
         def _(side=side, put=put):
             copy = pltpu.make_async_copy(full_ref.at[side], full, sems.at[2 * tiles + 2])
             copy.start()
@@ -452,75 +455,84 @@
     smem = pl.BlockSpec(memory_space=pltpu.SMEM)
     vmem = pl.BlockSpec(memory_space=pltpu.VMEM)
     anywhere = pl.BlockSpec(memory_space=pl.ANY)
-
-    half = shape((lat_rows // 2 * NEAR, width))
-    own, edge, left_a, left_b, right_a, right_b = pl.pallas_call(
+    hbm = pl.BlockSpec(memory_space=pltpu.HBM)
+
+    near = shape((lat_rows * NEAR, width))
+    own, edge, near_left, near_right = pl.pallas_call(
         start_kernel,
-        out_shape=(shape((kinds, cols, LANES)), shape((NEAR, cols, width)), half, half, half, half),
-        in_specs=[smem, vmem, vmem, anywhere],
-        out_specs=(vmem,) * 6,
+        out_shape=(shape((kinds, cols, LANES)), shape((NEAR, cols, width)), near, near),
+        in_specs=[smem] + [hbm] * 3,
+        out_specs=(vmem,) * 4,
         scratch_shapes=[
+            pltpu.VMEM(dep_shift.shape, jnp.int32),
+            pltpu.VMEM(dep_frac.shape, jnp.float32),
             pltpu.VMEM((LANES, LANES), jnp.float32),
             pltpu.VMEM((2, lat_rows, 8, width), jnp.float32),
-            pltpu.SemaphoreType.DMA((3,)),
+            pltpu.SemaphoreType.DMA((5,)),
         ],
         compiler_params=pltpu.CompilerParams(vmem_limit_bytes=16 * 2**20),
     )(info, dep_shift, dep_frac, state)
     other = lax.ppermute(own, "lat", swap)
     edge = lax.ppermute(edge, "lat", swap)
+    some = lat_rows // 4 * NEAR
+    first = shape((8 + some, width))
+    second = shape((lat_rows * NEAR - some + NEAR * NEAR, width))
+    left_a, right_a, left_b, right_b, dep = pl.pallas_call(
+        functools.partial(second_kernel, rows=rows),
+        out_shape=(first, first, second, second, shape((kinds, cols, LANES))),
+        in_specs=[smem] + [vmem] * 5,
+        out_specs=(vmem,) * 5,
+        compiler_params=pltpu.CompilerParams(vmem_limit_bytes=4 * 2**20),
+    )(info, own, other, edge, near_left, near_right)
     low_a = lax.ppermute(right_a, "lon", right)
     high_a = lax.ppermute(left_a, "lon", left)
-    head = shape((8, width))
-    more = shape((half.shape[0] + NEAR * NEAR, width))
-    to_left, to_right, left_b, right_b, dep = pl.pallas_call(
-        functools.partial(second_kernel, rows=rows),
-        out_shape=(head, head, more, more, shape((kinds, cols, LANES))),
-        in_specs=[smem] + [vmem] * 5,
-        out_specs=(vmem,) * 5,
-    )(info, own, other, edge, left_b, right_b)
-    from_left = lax.ppermute(to_right, "lon", right)
-    from_right = lax.ppermute(to_left, "lon", left)
     low_b = lax.ppermute(right_b, "lon", right)
     high_b = lax.ppermute(left_b, "lon", left)
 
     message = shape((SLOTS, width))
-    send_low, send_high, flags, around = pl.pallas_call(
+    size = -(-rows * FAR // 8) * 8
+    send_low, send_high, flags, sent, around = pl.pallas_call(
         functools.partial(pack_kernel, rows=rows, slots=SLOTS),
-        out_shape=(message, message, jax.ShapeDtypeStruct((8, LANES), jnp.int32), shape((kinds, wide, LANES))),
+        out_shape=(
+            message,
+            message,
+            jax.ShapeDtypeStruct((8, LANES), jnp.int32),
+            jax.ShapeDtypeStruct((2,), jnp.int32),
+            shape((kinds, wide, LANES)),
+        ),
         in_specs=[smem, vmem] + [anywhere] * 4,
-        out_specs=(vmem,) * 4,
+        out_specs=(vmem, vmem, vmem, smem, vmem),
         scratch_shapes=[
             pltpu.VMEM((rows * cols, width), jnp.float32),
             pltpu.VMEM((2, 8, width), jnp.float32),
             pltpu.SMEM((8, LANES), jnp.int32),
-            pltpu.SMEM((2, SLOTS + 8), jnp.int32),
+            pltpu.SMEM((2, size + 8), jnp.int32),
             pltpu.SemaphoreType.DMA((5,)),
         ],
         compiler_params=pltpu.CompilerParams(vmem_limit_bytes=16 * 2**20),
         cost_estimate=pl.CostEstimate(flops=0, bytes_accessed=4 * 2**20, transcendentals=0),
-    )(info, dep, state.reshape(lat_rows * cols, width), edge.reshape(NEAR * cols, width), from_left, from_right)
+    )(info, dep, state.reshape(lat_rows * cols, width), edge.reshape(NEAR * cols, width), low_a, high_a)
     far_high = lax.ppermute(send_low, "lon", left)
     far_low = lax.ppermute(send_high, "lon", right)
 
-    pick, frac, taken, counts = pl.pallas_call(
+    pick, frac, taken, counts, over = pl.pallas_call(
         functools.partial(weights_kernel, rows=rows, slots=SLOTS),
         out_shape=(
             shape((rows, TRAJ * wide, LANES)),
             shape((rows, TRAJ * wide, LANES)),
-            jax.ShapeDtypeStruct((2, SLOTS + 8), jnp.int32),
-            jax.ShapeDtypeStruct((2,), jnp.int32),
+            jax.ShapeDtypeStruct((2, size + 8), jnp.int32),
+            jax.ShapeDtypeStruct((4,), jnp.int32),
+            jax.ShapeDtypeStruct((1,), jnp.int32),
         ),
-        in_specs=[smem, vmem],
-        out_specs=(vmem, vmem, smem, smem),
-        scratch_shapes=[pltpu.SMEM((2, SLOTS + 8), jnp.int32)],
+        in_specs=[smem, smem, vmem, anywhere],
+        out_specs=(vmem, vmem, smem, smem, smem),
         compiler_params=pltpu.CompilerParams(vmem_limit_bytes=16 * 2**20),
-    )(flags, around)
-
-    over_left, over_right = counts[0] > SLOTS, counts[1] > SLOTS
-    size = -(-rows * FAR // 8) * 8
+    )(flags, sent, around, low_b)
+
     nothing = jnp.zeros((size, width), jnp.float32)
 
     def whole():
+        over_left, over_right = counts[2] > SLOTS, counts[3] > SLOTS
         field = jnp.concatenate([state, edge], axis=0)
         pad = ((0, size - rows * FAR), (0, 0))
         at_left = jnp.pad(field[:, NEAR : NEAR + FAR].reshape(rows * FAR, width), pad)
@@ -538,7 +550,7 @@
         )
         return jnp.where(even, jnp.stack([got_odd, got_even]), jnp.stack([got_even, got_odd]))
 
-    full = lax.cond(over_left | over_right, whole, lambda: jnp.stack([nothing, nothing]))
+    full = lax.cond(over[0] > 0, whole, lambda: jnp.stack([nothing, nothing]))
 
     return pl.pallas_call(
         functools.partial(main_kernel, rows, cols, SLOTS),

time: 62 us -> 51.7 us (0.83)
  waiting for transfers between devices: 11.1 us -> 5.72 us
  local copies, waits for them, and re-layouts: 7.4 us -> 2.69 us
  starting transfers between devices: 16 us -> 18.9 us
  Pallas kernels: 25.8 us -> 23.6 us
  between operations: 1.39 us -> 0.71 us
    ppermute x1, waiting for transfers between devices: 9.76 us -> 0.01 us  [shards(): high_a = lax.ppermute(left_a, 'lon', left)]
    ppermute x2 -> x0, starting transfers between devices: 5.94 us -> none  [the longest x1 3.05 us: shards(): from_right = lax.ppermute(to_left, 'lon', left)]
    ppermute x1, waiting for transfers between devices: 0.01 us -> 4.28 us  [shards(): far_high = lax.ppermute(send_low, 'lon', left)]
    unnamed x24 -> x10, local copies, waits for them, and re-layouts: 5.66 us -> 1.53 us
    ppermute x1, starting transfers between devices: 0.03 us -> 3.04 us  [shards(): high_a = lax.ppermute(left_a, 'lon', left)]
    ppermute x1, starting transfers between devices: 4.68 us -> 7.57 us  [shards(): far_high = lax.ppermute(send_low, 'lon', left)]
    ppermute x1, starting transfers between devices: 0.01 us -> 2.89 us  [shards(): low_a = lax.ppermute(right_a, 'lon', right)]
    pallas_call x1, Pallas kernels: 5.34 us -> 3.53 us  [shards(): pl.pallas_call(functools.partial(weights_kernel, rows=rows, slots=SLOTS),...]
  transfers between devices with their start and end apart: 10 -> 8, of which waited for: 2 -> 3; matrix products, arithmetic and copies ran while one was open for 3% -> 2% of each run, Pallas kernels for 15% -> 16%
where the time goes in v2:
time: 51.7 us; the launch traced here: 51.6 us
  Pallas kernels  23.6 us (46%)
  starting transfers between devices  18.9 us (37%)
  waiting for transfers between devices  5.72 us (11%)
  local copies, waits for them, and re-layouts  2.69 us (5%)
  between operations  0.71 us (1%)
    pallas_call x1, Pallas kernels, shards(): pl.pallas_call(functools.partial(main_kernel, rows, cols, SLOTS), out_sha...  12.9 us
    ppermute x1, starting transfers between devices, shards(): far_high = lax.ppermute(send_low, 'lon', left)  7.57 us
    ppermute x1, starting transfers between devices, shards(): high_b = lax.ppermute(left_b, 'lon', left)  4.72 us
    pallas_call x1, Pallas kernels, shards(): pl.pallas_call(functools.partial(pack_kernel, rows=rows, slots=SLOTS), ou...  4.64 us
    ppermute x1, waiting for transfers between devices, shards(): far_high = lax.ppermute(send_low, 'lon', left)  4.28 us
    pallas_call x1, Pallas kernels, shards(): pl.pallas_call(functools.partial(weights_kernel, rows=rows, slots=SLOTS),...  3.53 us
    ppermute x1, starting transfers between devices, shards(): high_a = lax.ppermute(left_a, 'lon', left)  3.04 us
    ppermute x1, starting transfers between devices, shards(): low_a = lax.ppermute(right_a, 'lon', right)  2.89 us
  transfers between devices with their start and end apart: 8, of which 3 were waited for; matrix products, arithmetic and copies ran while one was open for 2% of the time, Pallas kernels for 16%

profile of v2, /device:TPU:0, one launch (start us, length us, event | category | flops | bytes accessed | tf_op | source)
XLA Modules:
  0.0 51.6 jit_solution(5914429777568741689)
XLA Ops:
  0.0 0.0 copy-start
  0.0 0.8 %copy-done = s32[2,32,32]{2,1,0:T(8,128)S(1)} copy-done((s32[2,32,32]{2,1,0:T(8,128)S(1)}, s32[2,32,32]{2,1,0:T(8,128)}, u32[]{:S(2)}) %copy-start) | copy-done | bytes 8216
  0.8 0.0 copy-start.1
  0.8 0.8 %copy-done.1 = f32[2,32,32]{2,1,0:T(8,128)S(1)} copy-done((f32[2,32,32]{2,1,0:T(8,128)S(1)}, f32[2,32,32]{2,1,0:T(8,128)}, u32[]{:S(2)}) %copy-start.1) | copy-done | bytes 8216
  1.5 0.0 copy-start.2
  1.5 1.7 %shard_map.46 = (f32[4,32,128]{2,1,0:T(8,128)S(1)}, f32[4,32,640]{2,1,0:T(8,128)S(1)}, f32[128,640]{1,0:T(8,128)S(1)}, f32[128,640]{1,0:T(8,128)S(1)}) custom-call(s32[1]{0:T(128)} %bitcast.4.info_ref, s32[2,32,32]{2,1,0:T(8,128)S(1)} %copy-done, f32[2,32,32]{2,1,0:T(8,128)S(1)} %copy-done.1, f32[32,32,640]{2,1,0:T(8,128)} %state_ref.3), custom_call_target="tpu_custom_call" | custom-call | tf_op jit(solution)/shard_map/pallas_call | solution.py:461
  3.3 0.5 %collective-permute-start.3 = (f32[4,32,640]{2,1,0:T(8,128)S(1)}, f32[4,32,640]{2,1,0:T(8,128)S(1)}, u32[]{:S(2)}, u32[]{:S(2)}) collective-permute-start(f32[4,32,640]{2,1,0:T(8,128)S(1)} %get-tuple-element.63), channel_id=1, source_target_pairs={{0,1},{1,0},{2,3},{3,2},{4,5},{5,4},{6,7},{7,6},{8,9},{9,8},{10,11... | collective-permute-start | bytes 983048 | tf_op jit(solution)/shard_map/ppermute | solution.py:476
  3.8 0.1 collective-permute-start.2
  3.9 1.3 %collective-permute-done.2.next_ref = f32[4,32,128]{2,1,0:T(8,128)S(1)} collective-permute-done((f32[4,32,128]{2,1,0:T(8,128)S(1)}, f32[4,32,128]{2,1,0:T(8,128)S(1)}, u32[]{:S(2)}, u32[]{:S(2)}) %collective-permute-start.2) | collective-permute-done | bytes 65568 | tf_op jit(solution)/shard_map/ppermute | solution.py:475
  5.1 0.0 collective-permute-done.3.edge_ref
  5.1 0.0 copy-start.3
  5.1 0.9 %shard_map.47 = (f32[40,640]{1,0:T(8,128)S(1)}, f32[40,640]{1,0:T(8,128)S(1)}, f32[112,640]{1,0:T(8,128)}, f32[112,640]{1,0:T(8,128)S(1)}, f32[4,32,128]{2,1,0:T(8,128)S(1)}) custom-call(s32[1]{0:T(128)} %bitcast.4.info_ref, f32[4,32,128]{2,1,0:T(8,128)S(1)} %get-tuple-element.62.own_ref, f32[4,32,128]{2,1,0:T(8,128)S(1)} %collective-permute-done.2.next_ref, ...), custom_call_target="tpu_custom_call" | custom-call | tf_op jit(solution)/shard_map/pallas_call | solution.py:480
  6.0 2.9 %collective-permute-start.4 = (f32[40,640]{1,0:T(8,128)S(1)}, f32[40,640]{1,0:T(8,128)S(1)}, u32[]{:S(2)}, u32[]{:S(2)}) collective-permute-start(f32[40,640]{1,0:T(8,128)S(1)} %get-tuple-element.67), channel_id=1, source_target_pairs={{0,2},{2,4},{4,6},{6,8},{8,10},{10,12},{12,14},{14,0},{1,3},{3,5},... | collective-permute-start | bytes 307208 | tf_op jit(solution)/shard_map/ppermute | solution.py:487
  8.9 3.0 %collective-permute-start.5 = (f32[40,640]{1,0:T(8,128)S(1)}, f32[40,640]{1,0:T(8,128)S(1)}, u32[]{:S(2)}, u32[]{:S(2)}) collective-permute-start(f32[40,640]{1,0:T(8,128)S(1)} %get-tuple-element.68), channel_id=1, source_target_pairs={{0,14},{2,0},{4,2},{6,4},{8,6},{10,8},{12,10},{14,12},{1,15},{3,1}... | collective-permute-start | bytes 307208 | tf_op jit(solution)/shard_map/ppermute | solution.py:488
  11.9 0.0 collective-permute-start.6
  11.9 4.7 %collective-permute-start.7 = (f32[112,640]{1,0:T(8,128)}, f32[112,640]{1,0:T(8,128)}, u32[]{:S(2)}, u32[]{:S(2)}) collective-permute-start(f32[112,640]{1,0:T(8,128)} %get-tuple-element.74), channel_id=1, source_target_pairs={{0,14},{2,0},{4,2},{6,4},{8,6},{10,8},{12,10},{14,12},{1,15},{3,1}... | collective-permute-start | bytes 860168 | tf_op jit(solution)/shard_map/ppermute | solution.py:490
  16.6 0.0 collective-permute-done.4.from_left_ref.low_a_ref
  16.6 0.0 collective-permute-done.5.from_right_ref.high_a_ref
  16.6 0.0 copy-done.2
  16.7 0.0 copy-start.5
  16.7 4.6 %shard_map.48 = (f32[80,640]{1,0:T(8,128)}, f32[80,640]{1,0:T(8,128)}, s32[8,128]{1,0:T(8,128)S(1)}, s32[2]{0:T(128)S(1)}, f32[4,40,128]{2,1,0:T(8,128)S(1)}) custom-call(s32[1]{0:T(128)} %bitcast.4.info_ref, f32[4,32,128]{2,1,0:T(8,128)S(1)} %get-tuple-element.66.dep_ref, f32[1024,640]{1,0:T(8,128)S(1)} %bitcast.8, f32[128,640]{1,0:T(8,128)S(1)} %bitcast.9, ...), custom_call_target="tpu_custom_call" | custom-call | bytes 4194304 | tf_op jit(solution)/shard_map/pallas_call | solution.py:494
  21.3 0.0 copy-done.3
  21.3 0.1 collective-permute-start.8
  21.4 7.6 %collective-permute-start.9 = (f32[80,640]{1,0:T(8,128)}, f32[80,640]{1,0:T(8,128)}, u32[]{:S(2)}, u32[]{:S(2)}) collective-permute-start(f32[80,640]{1,0:T(8,128)} %get-tuple-element.76), channel_id=1, source_target_pairs={{0,14},{2,0},{4,2},{6,4},{8,6},{10,8},{12,10},{14,12},{1,15},{3,1}... | collective-permute-start | bytes 614408 | tf_op jit(solution)/shard_map/ppermute | solution.py:515
  29.0 0.0 copy-done.5
  29.0 0.0 collective-permute-done.6._.low_b_ref
  29.0 3.5 %shard_map.49 = (f32[36,80,128]{2,1,0:T(8,128)S(1)}, f32[36,80,128]{2,1,0:T(8,128)S(1)}, s32[2,264]{1,0:T(2,128)S(1)}, s32[4]{0:T(128)S(1)}, s32[1]{0:T(128)}) custom-call(s32[8,128]{1,0:T(8,128)S(1)} %get-tuple-element.69.bits_ref, s32[2]{0:T(128)S(1)} %get-tuple-element.70.sent_ref, f32[4,40,128]{2,1,0:T(8,128)S(1)} %get-tuple-element.71.wide_ref, ...), custom_call_target="tpu_custom_call" | custom-call | tf_op jit(solution)/shard_map/pallas_call | solution.py:518
  33.2 1.2 %conditional.3 = (f32[2,256,640]{2,1,0:T(8,128)}) conditional(s32[]{:T(128)} %bitcast.7, () %tuple.27, (s32[4]{0:T(128)S(1)}, f32[32,32,640]{2,1,0:T(8,128)}, f32[4,32,640]{2,1,0:T(8,128)}) %tuple.37), branch_computations={%region_0.0_spmd, %region_1.6_spmd} | conditional | flops 1310741 | bytes 26767752 | solution.py:553
  33.2 1.1 %broadcast.7 = f32[2,256,640]{2,1,0:T(8,128)} broadcast(f32[]{:T(128)} %constant.27.clone), dimensions={} | broadcast | bytes 1310724 | tf_op jit(solution)/shard_map/broadcast.1
  34.3 0.0 collective-permute-done.7.high_b_ref
  34.3 0.2 collective-permute-done.8.far_low_ref
  34.5 4.3 %collective-permute-done.9.far_high_ref = f32[80,640]{1,0:T(8,128)} collective-permute-done((f32[80,640]{1,0:T(8,128)}, f32[80,640]{1,0:T(8,128)}, u32[]{:S(2)}, u32[]{:S(2)}) %collective-permute-start.9) | collective-permute-done | bytes 204832 | tf_op jit(solution)/shard_map/ppermute | solution.py:515
  38.8 12.9 %shard_map.50 = f32[32,32,640]{2,1,0:T(8,128)} custom-call(s32[1]{0:T(128)} %bitcast.4.info_ref, s32[2,264]{1,0:T(2,128)S(1)} %get-tuple-element.73.lists_ref, f32[32,32,640]{2,1,0:T(8,128)} %state_ref.3, f32[4,32,640]{2,1,0:T(8,128)} %copy-done.3, f32[40,640]{1,0:T(8,128)S(1)} %collective-permute-done.4.from_left_ref.low_a_ref, ...), custom_call_target="tpu_custom_call" | custom-call | flops 200000000 | bytes 8388608 | tf_op jit(solution)/shard_map/pallas_call | solution.py:555
  (1 shorter events, 0.0 us)
Async XLA Ops:
  0.0 0.8 %copy-start = (s32[2,32,32]{2,1,0:T(8,128)S(1)}, s32[2,32,32]{2,1,0:T(8,128)}, u32[]{:S(2)}) copy-start(s32[2,32,32]{2,1,0:T(8,128)} %shift_ref.1) | copy-start | bytes 24580
  0.8 0.8 %copy-start.1 = (f32[2,32,32]{2,1,0:T(8,128)S(1)}, f32[2,32,32]{2,1,0:T(8,128)}, u32[]{:S(2)}) copy-start(f32[2,32,32]{2,1,0:T(8,128)} %frac_ref.1) | copy-start | bytes 24580
  1.5 15.1 %copy-start.2 = (f32[32,32,640]{2,1,0:T(8,128)S(1)}, f32[32,32,640]{2,1,0:T(8,128)}, u32[]{:S(2)}) copy-start(f32[32,32,640]{2,1,0:T(8,128)} %state_ref.3) | copy-start | bytes 7864324
  3.3 1.9 %collective-permute-start.3 = (f32[4,32,640]{2,1,0:T(8,128)S(1)}, f32[4,32,640]{2,1,0:T(8,128)S(1)}, u32[]{:S(2)}, u32[]{:S(2)}) collective-permute-start(f32[4,32,640]{2,1,0:T(8,128)S(1)} %get-tuple-element.63), channel_id=1, source_target_pairs={{0,1},{1,0},{2,3},{3,2},{4,5},{5,4},{6,7},{7,6},{8,9},{9,8},{10,11... | collective-permute-start | bytes 983048 | tf_op jit(solution)/shard_map/ppermute | solution.py:476
  3.8 1.3 %collective-permute-start.2 = (f32[4,32,128]{2,1,0:T(8,128)S(1)}, f32[4,32,128]{2,1,0:T(8,128)S(1)}, u32[]{:S(2)}, u32[]{:S(2)}) collective-permute-start(f32[4,32,128]{2,1,0:T(8,128)S(1)} %get-tuple-element.62.own_ref), channel_id=1, source_target_pairs={{0,1},{1,0},{2,3},{3,2},{4,5},{5,4},{6,7},{7,6},{8,9},{9,8},{10,11... | collective-permute-start | bytes 196616 | tf_op jit(solution)/shard_map/ppermute | solution.py:475
  5.1 16.2 %copy-start.3 = (f32[4,32,640]{2,1,0:T(8,128)}, f32[4,32,640]{2,1,0:T(8,128)S(1)}, u32[]{:S(2)}) copy-start(f32[4,32,640]{2,1,0:T(8,128)S(1)} %collective-permute-done.3.edge_ref) | copy-start | bytes 983044
  6.0 10.7 %collective-permute-start.4 = (f32[40,640]{1,0:T(8,128)S(1)}, f32[40,640]{1,0:T(8,128)S(1)}, u32[]{:S(2)}, u32[]{:S(2)}) collective-permute-start(f32[40,640]{1,0:T(8,128)S(1)} %get-tuple-element.67), channel_id=1, source_target_pairs={{0,2},{2,4},{4,6},{6,8},{8,10},{10,12},{12,14},{14,0},{1,3},{3,5},... | collective-permute-start | bytes 307208 | tf_op jit(solution)/shard_map/ppermute | solution.py:487
  8.9 7.8 %collective-permute-start.5 = (f32[40,640]{1,0:T(8,128)S(1)}, f32[40,640]{1,0:T(8,128)S(1)}, u32[]{:S(2)}, u32[]{:S(2)}) collective-permute-start(f32[40,640]{1,0:T(8,128)S(1)} %get-tuple-element.68), channel_id=1, source_target_pairs={{0,14},{2,0},{4,2},{6,4},{8,6},{10,8},{12,10},{14,12},{1,15},{3,1}... | collective-permute-start | bytes 307208 | tf_op jit(solution)/shard_map/ppermute | solution.py:488
  11.9 17.1 %collective-permute-start.6 = (f32[112,640]{1,0:T(8,128)S(1)}, f32[112,640]{1,0:T(8,128)S(1)}, u32[]{:S(2)}, u32[]{:S(2)}) collective-permute-start(f32[112,640]{1,0:T(8,128)S(1)} %get-tuple-element.72), channel_id=1, source_target_pairs={{0,2},{2,4},{4,6},{6,8},{8,10},{10,12},{12,14},{14,0},{1,3},{3,5},... | collective-permute-start | bytes 860168 | tf_op jit(solution)/shard_map/ppermute | solution.py:489
  11.9 22.4 %collective-permute-start.7 = (f32[112,640]{1,0:T(8,128)}, f32[112,640]{1,0:T(8,128)}, u32[]{:S(2)}, u32[]{:S(2)}) collective-permute-start(f32[112,640]{1,0:T(8,128)} %get-tuple-element.74), channel_id=1, source_target_pairs={{0,14},{2,0},{4,2},{6,4},{8,6},{10,8},{12,10},{14,12},{1,15},{3,1}... | collective-permute-start | bytes 860168 | tf_op jit(solution)/shard_map/ppermute | solution.py:490
  16.7 12.3 %copy-start.5 = (f32[640]{0:T(1024)S(1)}, f32[640]{0:T(1024)}, u32[]{:S(2)}) copy-start(f32[640]{0:T(1024)} %param.13) | copy-start | bytes 7684
  21.3 13.2 %collective-permute-start.8 = (f32[80,640]{1,0:T(8,128)}, f32[80,640]{1,0:T(8,128)}, u32[]{:S(2)}, u32[]{:S(2)}) collective-permute-start(f32[80,640]{1,0:T(8,128)} %get-tuple-element.75), channel_id=1, source_target_pairs={{0,2},{2,4},{4,6},{6,8},{8,10},{10,12},{12,14},{14,0},{1,3},{3,5},... | collective-permute-start | bytes 614408 | tf_op jit(solution)/shard_map/ppermute | solution.py:516
  21.4 17.4 %collective-permute-start.9 = (f32[80,640]{1,0:T(8,128)}, f32[80,640]{1,0:T(8,128)}, u32[]{:S(2)}, u32[]{:S(2)}) collective-permute-start(f32[80,640]{1,0:T(8,128)} %get-tuple-element.76), channel_id=1, source_target_pairs={{0,14},{2,0},{4,2},{6,4},{8,6},{10,8},{12,10},{14,12},{1,15},{3,1}... | collective-permute-start | bytes 614408 | tf_op jit(solution)/shard_map/ppermute | solution.py:515

commit v3 on v2

v3 whole, which is shorter than its diff:
```python
import functools

import jax
import jax.numpy as jnp
from jax import lax
from jax.experimental import pallas as pl
from jax.experimental.pallas import tpu as pltpu
from jax.sharding import PartitionSpec as P

LEV = 128
TRAJ = 2
REACH = 8
OMEGAS = (0.4227, 0.8104)

NEAR = 2 * TRAJ
FAR = REACH - 1
SLOTS = 80
LANES = 128
SIDE = 8
UP_ROWS = 6
SWEEP_ROWS = 6


def ring(axis, step):
    count = lax.axis_size(axis)
    return [(i, (i + step) % count) for i in range(count)]


def pairs(axis, start):
    count = lax.axis_size(axis)
    edges = [(i, (i + 1) % count) for i in range(start, count, 2)]
    return edges + [(b, a) for a, b in edges]


def start_kernel(
    info_ref,
    dep_ref,
    state_ref,
    own_ref,
    edge_ref,
    left_ref,
    right_ref,
    pad,
    sides,
    sems,
):
    kinds, rows, cols = dep_ref.shape
    edge_row = jnp.where(info_ref[0] == 0, rows - NEAR, 0)
    fetch = [
        pltpu.make_async_copy(state_ref.at[:, pl.ds(0, 8), :], sides.at[0], sems.at[0]),
        pltpu.make_async_copy(state_ref.at[:, pl.ds(cols - 8, 8), :], sides.at[1], sems.at[1]),
        pltpu.make_async_copy(state_ref.at[pl.ds(edge_row, NEAR)], edge_ref, sems.at[2]),
    ]
    for copy in fetch:
        copy.start()
    pad[...] = jnp.zeros_like(pad)
    for kind in range(kinds):
        pad[0:rows, 0:cols] = dep_ref[kind]
        own_ref[kind] = jnp.transpose(pad[...])[0:cols, :]
    for side, (first, ref) in enumerate(((0, left_ref), (8 - NEAR, right_ref))):
        fetch[side].wait()
        for r in range(0, rows, 2):
            two = jnp.concatenate([sides[side, r + v, first : first + NEAR, :] for v in range(2)], axis=0)
            ref[r * NEAR : (r + 2) * NEAR, :] = two
    fetch[2].wait()


def second_kernel(
    info_ref,
    own_ref,
    next_ref,
    edge_ref,
    left_ref,
    right_ref,
    left_a_ref,
    right_a_ref,
    left_b_ref,
    right_b_ref,
    dep_ref,
    *,
    rows,
):
    kinds, cols, _ = own_ref.shape
    low = info_ref[0] == 0
    lat_rows = rows - NEAR
    lane = lax.broadcasted_iota(jnp.int32, (cols, LANES), 1)
    head = jnp.zeros((8, left_ref.shape[1]), jnp.float32)
    left_a_ref[0:8, :] = head
    right_a_ref[0:8, :] = head
    for kind in range(kinds):
        own, other = own_ref[kind], next_ref[kind]
        other = jnp.where(low, pltpu.roll(other, lat_rows, 1), pltpu.roll(other, NEAR, 1))
        both = jnp.where(lane < lat_rows, own, other)
        dep_ref[kind] = both
        left_a_ref[0:NEAR, kind * LANES : (kind + 1) * LANES] = both[0:NEAR, :]
        right_a_ref[0:NEAR, kind * LANES : (kind + 1) * LANES] = both[cols - NEAR : cols, :]
    some = left_a_ref.shape[0] - 8
    rest = lat_rows * NEAR - some
    left_a_ref[8 : 8 + some, :] = left_ref[0:some, :]
    right_a_ref[8 : 8 + some, :] = right_ref[0:some, :]
    left_b_ref[0:rest, :] = left_ref[some : some + rest, :]
    right_b_ref[0:rest, :] = right_ref[some : some + rest, :]
    for r in range(NEAR):
        at = slice(rest + r * NEAR, rest + (r + 1) * NEAR)
        left_b_ref[at, :] = edge_ref[r, 0:NEAR, :]
        right_b_ref[at, :] = edge_ref[r, cols - NEAR : cols, :]


def pack_kernel(
    info_ref,
    dep_ref,
    state_ref,
    edge_ref,
    from_left_ref,
    from_right_ref,
    low_ref,
    high_ref,
    notes_ref,
    over,
    wide_ref,
    notes,
    sem,
    *,
    rows,
    slots,
):
    kinds, cols, _ = dep_ref.shape
    wide = cols + 2 * NEAR
    lat_rows = rows - NEAR
    low = info_ref[0] == 0
    for kind in range(kinds):
        lanes = slice(kind * LANES, (kind + 1) * LANES)
        wide_ref[kind, 0:NEAR, :] = from_left_ref[0:NEAR, lanes]
        wide_ref[kind, NEAR : NEAR + cols, :] = dep_ref[kind]
        wide_ref[kind, NEAR + cols : wide, :] = from_right_ref[0:NEAR, lanes]

    lane = lax.broadcasted_iota(jnp.int32, (1, LANES), 1)
    beyond = jnp.where(low, lane - lat_rows + 1, rows - lane)
    beyond = jnp.where(lane < lat_rows, 0, jnp.where(lane < rows, beyond, rows))
    reach = [NEAR - 1 - 2 * turn for turn in range(TRAJ)]
    groups = (
        ([0] * TRAJ, 0, 1),
        ([cols + NEAR - r for r in reach], cols - 1, -1),
        ([NEAR - r for r in reach], -1, -1),
        ([cols] * TRAJ, cols, 1),
    )
    totals = []
    for first, anchor, sign in groups:
        total = jnp.zeros((1, LANES), jnp.int32)
        for turn in range(TRAJ):
            for q in range(first[turn], first[turn] + NEAR + reach[turn]):
                target = wide_ref[turn, q : q + 1, :].astype(jnp.int32) + (q - NEAR)
                j = sign * (target - anchor) - NEAR
                hit = (j >= 0) & (j < FAR) & (beyond <= reach[turn])
                total = total | jnp.where(hit, jnp.left_shift(1, jnp.maximum(j, 0)), 0)
        totals.append(total)
    totals = jnp.concatenate(totals + [jnp.zeros((8 - len(groups), LANES), jnp.int32)], axis=0)

    hits = [(totals >> j) & 1 for j in range(FAR)]
    in_row = sum(hits[1:], hits[0])
    upto, lanes8 = in_row, lax.broadcasted_iota(jnp.int32, (8, LANES), 1)
    for d in (1, 2, 4, 8, 16, 32, 64):
        upto = upto + jnp.where(lanes8 >= d, pltpu.roll(upto, d, 1), 0)
    place, places = upto - in_row, []
    for hit in hits:
        places.append(jnp.where(hit == 1, place, -1))
        place = place + hit
    n = lax.broadcasted_iota(jnp.int32, (slots, LANES), 0)
    diagonal = n == lax.broadcasted_iota(jnp.int32, (slots, LANES), 1)
    addresses = (
        (2, 8, 0, 1),
        (3, 8, 0, 1),
        (0, cols, NEAR, 1),
        (1, cols, cols - 1 - NEAR, -1),
    )
    notes_ref[0 : len(groups), :] = upto[0 : len(groups)]
    for i, (which, stride, first, sign) in enumerate(addresses):
        found = jnp.zeros((slots, LANES), jnp.float32)
        for j in range(FAR):
            address = (lane * stride + (first + sign * j)).astype(jnp.float32)
            found = found + jnp.where(places[j][which : which + 1] == n, address, 0.0)
        found = jnp.where(diagonal, jnp.sum(found, axis=1, keepdims=True), 0.0)
        notes_ref[len(groups) + i : len(groups) + i + 1, :] = jnp.sum(found, axis=0, keepdims=True).astype(jnp.int32)
    copy = pltpu.make_async_copy(notes_ref, notes, sem)
    copy.start()
    copy.wait()
    sent = [notes[side, LANES - 1] for side in range(2)]
    most = jnp.maximum(jnp.maximum(sent[0], sent[1]), jnp.maximum(notes[2, LANES - 1], notes[3, LANES - 1]))
    over[0] = (most > slots).astype(jnp.int32)
    own = lat_rows * cols

    def gather(group, _):
        for u in range(8):
            n = group * 8 + u
            for side, ref in enumerate((low_ref, high_ref)):
                address = jnp.minimum(notes[6 + side, n], own - 1)
                ref[pl.ds(n, 1), :] = state_ref[pl.ds(address, 1), :]
        return 0

    lax.fori_loop(0, slots // 8, gather, 0)

    def gather_edge(side, ref):
        def body(n):
            ref[pl.ds(n, 1), :] = edge_ref[pl.ds(notes[6 + side, n] - own, 1), :]
            return n - 1

        start = jnp.minimum(sent[side], slots) - 1
        lax.while_loop(lambda n: (n >= 0) & (notes[6 + side, jnp.maximum(n, 0)] >= own), body, start)

    gather_edge(0, low_ref)
    gather_edge(1, high_ref)


def arranged(ref, index, start, groups):
    middle = groups - 2
    parts = [ref[index + (pl.ds(start, 8), slice(None))]]
    parts += [ref[index + (pl.ds(start + 8 + k, 8, stride=middle), slice(None))] for k in range(middle)]
    return parts + [ref[index + (pl.ds(start + 8 * (groups - 1), 8), slice(None))]]


def weights_kernel(wide_ref, pick_ref, frac_ref, far_ref, kept_ref, sem, *, rows):
    kinds, wide, _ = wide_ref.shape
    cols = wide - 2 * NEAR
    keep = pltpu.make_async_copy(wide_ref, kept_ref, sem)
    keep.start()
    groups, band = wide // 8, cols + 2 * SIDE
    place = lax.broadcasted_iota(jnp.int32, (8, LANES), 1)
    place = jnp.where(place < band, place, place - band)
    place = jnp.where(place < band, place, -LANES).astype(jnp.float32)
    sub = lax.broadcasted_iota(jnp.int32, (8, LANES), 0)
    firsts = [sub] + [8 + k + sub * (groups - 2) for k in range(groups - 2)] + [8 * (groups - 1) + sub]
    parts = []
    for turn in range(TRAJ):
        for k, shift in enumerate(arranged(wide_ref, (turn,), 0, groups)):
            parts.append(shift + (firsts[k] - NEAR).astype(jnp.float32))
    fracs = [frac for turn in range(TRAJ) for frac in arranged(wide_ref, (TRAJ + turn,), 0, groups)]
    highs = [frac.astype(jnp.bfloat16).astype(jnp.float32) for frac in fracs]
    parts += highs + [frac - high for frac, high in zip(fracs, highs)]
    table = jnp.concatenate(parts, axis=0).astype(jnp.bfloat16)
    row = lax.broadcasted_iota(jnp.int32, (LANES, LANES), 0)
    count = TRAJ * wide
    for m in range(rows):
        spread = jnp.dot(table, jnp.where(row == m, 1.0, 0.0).astype(jnp.bfloat16), preferred_element_type=jnp.float32)
        frac_ref[m] = spread[count : 2 * count] + spread[2 * count :]
        for n in range(TRAJ * groups):
            column = spread[8 * n : 8 * n + 8]
            pick_ref[m, 8 * n : 8 * n + 8, :] = jnp.where(column + SIDE == place, 1.0, 0.0)
            turn, k = divmod(n, groups)
            if k == 0:
                far_ref[0, turn, m] = -1 - NEAR - column
            if k == groups - 1:
                far_ref[1, turn, m] = column - (cols + NEAR)
    keep.wait()


def gather_kernel(
    info_ref,
    state_ref,
    edge_ref,
    low_a_ref,
    high_a_ref,
    low_b_ref,
    high_b_ref,
    pick_ref,
    frac_ref,
    rhs,
    x_ref,
    *rest,
):
    *kept, ext, sems = rest
    lat_rows, cols, width = state_ref.shape
    tiles = width // LEV
    rows = lat_rows + NEAR
    wide = cols + 2 * NEAR
    groups, band = wide // 8, cols + 2 * SIDE
    own0 = jnp.where(info_ref[0] == 0, 0, NEAR)
    ext0 = jnp.where(info_ref[0] == 0, lat_rows, 0)
    copies = []
    for f in range(tiles):
        lanes = pl.ds(f * LEV, LEV)
        for i, (ref, first, count) in enumerate(((state_ref, own0, lat_rows), (edge_ref, ext0, NEAR))):
            copies.append(
                pltpu.make_async_copy(
                    ref.at[:, :, lanes],
                    ext.at[f, pl.ds(first, count), pl.ds(SIDE, cols), :],
                    sems.at[2 * f + i],
                )
            )
            copies[-1].start()
    keeps = []
    for i, (source, target) in enumerate(zip((edge_ref, low_a_ref, high_a_ref, low_b_ref, high_b_ref), kept)):
        keeps.append(pltpu.make_async_copy(source, target, sems.at[2 * tiles + i]))
        keeps[-1].start()
    zero = jnp.zeros((8, LEV), jnp.float32)
    for f in range(tiles):
        for k in range(groups):
            x_ref[f, rows, 8 * k : 8 * k + 8, :] = zero

    first = (low_a_ref.shape[0] - 8) // NEAR
    blank = jnp.zeros((SIDE - NEAR, LEV), jnp.float32)

    def near(m, start, low, high):
        e = jnp.where(m < lat_rows, own0 + m, ext0 + m - lat_rows)
        at = pl.ds(pl.multiple_of(start, 8), 2 * NEAR)
        west, east = low[at, :], high[at, :]
        for f in range(tiles):
            for v in range(2):
                part = (slice(v * NEAR, (v + 1) * NEAR), slice(f * LEV, (f + 1) * LEV))
                ext[f, e + v, 0:SIDE, :] = jnp.concatenate([blank, west[part]], axis=0)
                ext[f, e + v, SIDE + cols : band, :] = jnp.concatenate([east[part], blank], axis=0)

    def near_a(n, _):
        near(2 * n, 8 + 2 * NEAR * n, low_a_ref, high_a_ref)
        return 0

    def near_b(n, _):
        near(first + 2 * n, 2 * NEAR * n, low_b_ref, high_b_ref)
        return 0

    lax.fori_loop(0, first // 2, near_a, 0)
    lax.fori_loop(0, (rows - first) // 2, near_b, 0)
    for copy in copies:
        copy.wait()

    top = lax.broadcasted_iota(jnp.int32, (wide, LEV), 1) == LEV - 1

    def upstream(group, _):
        for v in range(UP_ROWS):
            e = group * UP_ROWS + v
            own = (e >= own0) & (e < own0 + lat_rows)
            m = jnp.where(own, e - own0, e - ext0 + lat_rows)
            his, los = [], []
            for f in range(tiles):
                value = ext[f, e]
                hi = value.astype(jnp.bfloat16)
                his.append(hi)
                los.append((value - hi.astype(jnp.float32)).astype(jnp.bfloat16))
                for k, part in enumerate(arranged(ext, (f, e), SIDE - NEAR, groups)):
                    x_ref[f, e, 8 * k : 8 * k + 8, :] = part
            field = jnp.concatenate([jnp.concatenate(his, axis=1), jnp.concatenate(los, axis=1)], axis=0)
            pick = pick_ref[m].astype(jnp.bfloat16)[:, : 2 * band]
            got = jnp.dot(pick, field, preferred_element_type=jnp.float32)
            for turn in range(TRAJ):
                frac = frac_ref[m, turn * wide : (turn + 1) * wide, :]
                for f in range(tiles):
                    u = got[turn * wide : (turn + 1) * wide, f * LEV : (f + 1) * LEV]
                    up = jnp.where(top, u, pltpu.roll(u, LEV - 1, 1))
                    rhs[turn, f, e] = u + frac * (up - u)
        return 0

    lax.fori_loop(0, rows // UP_ROWS, upstream, 0)
    for keep in keeps:
        keep.wait()


def main_kernel(
    info_ref,
    notes_ref,
    far_low_ref,
    far_high_ref,
    met_ref,
    frac_ref,
    stiff_ref,
    x_ref,
    rhs_in,
    out_any,
    rhs,
    low_kept,
    high_kept,
    ups,
    xa,
    xb,
    nat,
    sems,
    *,
    slots,
):
    lat_rows, cols, width = out_any.shape
    tiles = width // LEV
    rows = lat_rows + NEAR
    wide = cols + 2 * NEAR
    groups = wide // 8
    own0 = jnp.where(info_ref[0] == 0, 0, NEAR)
    ext0 = jnp.where(info_ref[0] == 0, lat_rows, 0)
    keeps = [
        pltpu.make_async_copy(far_low_ref, low_kept, sems.at[tiles]),
        pltpu.make_async_copy(far_high_ref, high_kept, sems.at[tiles + 1]),
    ]
    for keep in keeps:
        keep.start()
    zero = jnp.zeros((8, LEV), jnp.float32)
    for f in range(tiles):
        for k in range(groups):
            xa[f, rows, 8 * k : 8 * k + 8, :] = zero
            xb[f, rows, 8 * k : 8 * k + 8, :] = zero

    def lift(source, count):
        def block(n, _):
            at = pl.ds(pl.multiple_of(n * 8, 8), 8)
            lane = lax.broadcasted_iota(jnp.int32, (8, LEV), 1)
            for f in range(tiles):
                lanes = slice(f * LEV, (f + 1) * LEV)
                u = source[at, lanes]
                ups[at, lanes] = jnp.where(lane == LEV - 1, u, pltpu.roll(u, LEV - 1, 1))
            return 0

        lax.fori_loop(0, count // 8, block, 0)

    def put(side, m, j, source, n):
        k = 0 if side == 0 else groups - 1
        e = jnp.where(m < lat_rows, own0 + m, ext0 + m - lat_rows)
        column, up = source[pl.ds(n, 1), :], ups[pl.ds(n, 1), :]
        for turn in range(TRAJ):
            hit = met_ref[side, turn, m] == j.astype(jnp.float32)
            frac = frac_ref[m, turn * wide + 8 * k : turn * wide + 8 * k + 8, :]
            for f in range(tiles):
                u, v = column[:, f * LEV : (f + 1) * LEV], up[:, f * LEV : (f + 1) * LEV]
                mixed = u + frac * (v - u)
                at = (turn, f, e, slice(8 * k, 8 * k + 8), slice(None))
                rhs[at] = jnp.where(hit, mixed, rhs[at])

    for side, far_ref in enumerate((far_low_ref, far_high_ref)):
        lift(far_ref, slots)

        def place(n, _, side=side, far_ref=far_ref):
            address = notes_ref[4 + side * -(-slots // LANES) + n // LANES, n % LANES]
            put(side, address >> 3, address & 7, far_ref, n)
            return 0

        lax.fori_loop(0, jnp.minimum(notes_ref[2 + side, LANES - 1], slots), place, 0)

    sub = lax.broadcasted_iota(jnp.int32, (8, LEV), 0)
    bottom, last = sub == 0, sub == 7

    def tile(f, _):
        s = stiff_ref[f]
        prev = 1.0
        for sweep in range(2 * TRAJ):
            omega = OMEGAS[sweep % 2]
            alpha = jnp.broadcast_to((1.0 - omega - 4.0 * omega * s) * (prev / omega), (8, LEV))
            beta = jnp.broadcast_to(s * prev, (8, LEV))
            prev = omega
            turn = sweep // 2
            src, dst = (x_ref, xa, xb, xa)[sweep], (xa, xb, xa, None)[sweep]

            def load(e, src=src):
                return [src[f, e, 8 * k : 8 * k + 8, :] for k in range(groups)]

            def block(group, carry, load=load, dst=dst, alpha=alpha, beta=beta, turn=turn, omega=omega):
                south, mid = carry
                for v in range(SWEEP_ROWS):
                    e = group * SWEEP_ROWS + v
                    north = load(e + 1)
                    left, right = mid[0], mid[groups - 1]
                    first, final = mid[1], mid[groups - 2]
                    from_west = [pltpu.roll(x, 1, 0) for x in (left, final, right)]
                    from_east = [pltpu.roll(x, 7, 0) for x in (left, first, right)]
                    wests = [from_west[0], jnp.where(bottom, from_west[0], from_west[1])]
                    wests += mid[1 : groups - 2] + [jnp.where(bottom, from_west[1], from_west[2])]
                    easts = [jnp.where(last, from_east[1], from_east[0])] + mid[2 : groups - 1]
                    easts += [jnp.where(last, from_east[2], from_east[1]), from_east[2]]
                    for k in range(groups):
                        around = (south[k] + north[k]) + (wests[k] + easts[k])
                        new = alpha * mid[k] + beta * around + rhs[turn, f, e, 8 * k : 8 * k + 8, :]
                        if dst is not None:
                            dst[f, e, 8 * k : 8 * k + 8, :] = new
                        elif k in (0, groups - 1):
                            nat[f, e, 8 * k : 8 * k + 8, :] = new * omega
                        else:
                            nat[f, e, pl.ds(8 + k - 1, 8, stride=groups - 2), :] = new * omega
                    south, mid = mid, north
                return south, mid

            lax.fori_loop(0, rows // SWEEP_ROWS, block, ([zero] * groups, load(0)))

        lanes = pl.ds(pl.multiple_of(f * LEV, LEV), LEV)
        part = nat.at[f, pl.ds(own0, lat_rows), pl.ds(NEAR, cols), :]
        pltpu.make_async_copy(part, out_any.at[:, :, lanes], sems.at[f]).start()
        return 0

    lax.fori_loop(0, tiles, tile, 0)
    for f in range(tiles):
        part = nat.at[f, pl.ds(own0, lat_rows), pl.ds(NEAR, cols), :]
        pltpu.make_async_copy(part, out_any.at[:, :, pl.ds(f * LEV, LEV)], sems.at[f]).wait()
    for keep in keeps:
        keep.wait()


def shards(state, dep_shift, dep_frac, stiff):
    lat_rows, cols, width = state.shape
    tiles = width // LEV
    rows = lat_rows + NEAR
    wide = cols + 2 * NEAR
    band = cols + 2 * SIDE
    kinds = 2 * TRAJ
    lat = lax.axis_index("lat")
    low = lat == 0
    right, left = ring("lon", 1), ring("lon", -1)
    swap = ring("lat", 1)
    info = lat[None]
    shape = functools.partial(jax.ShapeDtypeStruct, dtype=jnp.float32)
    smem = pl.BlockSpec(memory_space=pltpu.SMEM)
    vmem = pl.BlockSpec(memory_space=pltpu.VMEM)
    anywhere = pl.BlockSpec(memory_space=pl.ANY)
    hbm = pl.BlockSpec(memory_space=pltpu.HBM)

    is_shift = jnp.arange(2)[:, None, None, None] == 0
    dep = jnp.where(is_shift, dep_shift[None].astype(jnp.float32), dep_frac[None]).reshape(kinds, lat_rows, cols)
    near = shape((lat_rows * NEAR, width))
    own, edge, near_left, near_right = pl.pallas_call(
        start_kernel,
        out_shape=(shape((kinds, cols, LANES)), shape((NEAR, cols, width)), near, near),
        in_specs=[smem, vmem, hbm],
        out_specs=(vmem,) * 4,
        scratch_shapes=[
            pltpu.VMEM((LANES, LANES), jnp.float32),
            pltpu.VMEM((2, lat_rows, 8, width), jnp.float32),
            pltpu.SemaphoreType.DMA((3,)),
        ],
        compiler_params=pltpu.CompilerParams(vmem_limit_bytes=16 * 2**20),
    )(info, dep, state)
    other = lax.ppermute(own, "lat", swap)
    edge = lax.ppermute(edge, "lat", swap)
    some = lat_rows // 4 * NEAR
    first = shape((8 + some, width))
    second = shape((rows * NEAR - some, width))
    left_a, right_a, left_b, right_b, dep = pl.pallas_call(
        functools.partial(second_kernel, rows=rows),
        out_shape=(first, first, second, second, shape((kinds, cols, LANES))),
        in_specs=[smem] + [vmem] * 5,
        out_specs=(vmem,) * 5,
        compiler_params=pltpu.CompilerParams(vmem_limit_bytes=4 * 2**20),
    )(info, own, other, edge, near_left, near_right)
    low_a = lax.ppermute(right_a, "lon", right)
    high_a = lax.ppermute(left_a, "lon", left)
    low_b = lax.ppermute(right_b, "lon", right)
    high_b = lax.ppermute(left_b, "lon", left)

    few = shape((SLOTS, width))
    size = rows * 8
    send_low, send_high, notes, over, around = pl.pallas_call(
        functools.partial(pack_kernel, rows=rows, slots=SLOTS),
        out_shape=(
            few,
            few,
            jax.ShapeDtypeStruct((8, LANES), jnp.int32),
            jax.ShapeDtypeStruct((1,), jnp.int32),
            shape((kinds, wide, LANES)),
        ),
        in_specs=[smem] + [vmem] * 5,
        out_specs=(vmem, vmem, vmem, smem, vmem),
        scratch_shapes=[pltpu.SMEM((8, LANES), jnp.int32), pltpu.SemaphoreType.DMA(())],
        compiler_params=pltpu.CompilerParams(vmem_limit_bytes=4 * 2**20),
        cost_estimate=pl.CostEstimate(flops=0, bytes_accessed=40 * 2**20, transcendentals=0),
    )(info, dep, state.reshape(lat_rows * cols, width), edge.reshape(NEAR * cols, width), low_a, high_a)
    far_high = lax.ppermute(send_low, "lon", left)
    far_low = lax.ppermute(send_high, "lon", right)

    per_row = shape((rows, TRAJ * wide, LANES))
    def weights(around):
        return pl.pallas_call(
            functools.partial(weights_kernel, rows=rows),
            out_shape=(per_row, per_row, shape((2, TRAJ, rows, 8, LANES)), shape(around.shape)),
            in_specs=[vmem],
            out_specs=(vmem, vmem, vmem, hbm),
            scratch_shapes=[pltpu.SemaphoreType.DMA(())],
            compiler_params=pltpu.CompilerParams(vmem_limit_bytes=8 * 2**20),
        )(around)

    pick, frac, met, around = weights(around)
    low_b, high_b, pick = lax.optimization_barrier((low_b, high_b, pick))

    rhs_shape = shape((TRAJ, tiles, rows, wide, LEV))
    x_shape = (tiles, rows + 1, wide, LEV)

    def gather(state, edge, low_a, high_a, low_b, high_b, pick, frac):
        return pl.pallas_call(
            gather_kernel,
            out_shape=(rhs_shape, shape(x_shape)) + tuple(shape(x.shape) for x in (edge, low_a, high_a, low_b, high_b)),
            in_specs=[smem, hbm, anywhere] + [vmem] * 6,
            out_specs=(vmem, vmem) + (hbm,) * 5,
            scratch_shapes=[
                pltpu.VMEM((tiles, rows, cols + 2 * SIDE, LEV), jnp.float32),
                pltpu.SemaphoreType.DMA((2 * tiles + 5,)),
            ],
            compiler_params=pltpu.CompilerParams(vmem_limit_bytes=12 * 2**20),
            cost_estimate=pl.CostEstimate(flops=0, bytes_accessed=2**20, transcendentals=0),
        )(info, state, edge, low_a, high_a, low_b, high_b, pick, frac)

    def finish(slots, notes, far_low, far_high, met, frac, x, rhs):
        return pl.pallas_call(
            functools.partial(main_kernel, slots=slots),
            out_shape=(shape(state.shape), rhs_shape, shape(far_low.shape), shape(far_high.shape)),
            in_specs=[smem] * 2 + [vmem] * 7,
            out_specs=(hbm, vmem, hbm, hbm),
            scratch_shapes=[
                pltpu.VMEM((slots, width), jnp.float32),
                pltpu.VMEM(x_shape, jnp.float32),
                pltpu.VMEM(x_shape, jnp.float32),
                pltpu.VMEM((tiles, rows, wide, LEV), jnp.float32),
                pltpu.SemaphoreType.DMA((tiles + 2,)),
            ],
            input_output_aliases={8: 1},
            compiler_params=pltpu.CompilerParams(vmem_limit_bytes=16 * 2**20),
        )(info, notes, far_low, far_high, met, frac, stiff.reshape(tiles, 1, LEV), x, rhs)

    rhs, x, *messages = gather(state, edge, low_a, high_a, low_b, high_b, pick, frac)
    out, _, far_low, far_high = finish(SLOTS, notes, far_low, far_high, met, frac, x, rhs)

    def whole():
        counts = notes[:4, LANES - 1]
        most = jnp.maximum(counts[:2], counts[2:])
        over_left, over_right = most[0] > SLOTS, most[1] > SLOTS
        field = jnp.concatenate([state, messages[0]], axis=0)
        at_left = field[:, NEAR : NEAR + 8].reshape(size, width)
        at_right = field[:, cols - NEAR - 8 : cols - NEAR][:, ::-1].reshape(size, width)
        even = lax.axis_index("lon") % 2 == 0
        nothing = jnp.zeros((size, width), jnp.float32)
        got_even = lax.cond(
            jnp.where(even, over_right, over_left),
            lambda: lax.ppermute(jnp.where(even, at_right, at_left), "lon", pairs("lon", 0)),
            lambda: nothing,
        )
        got_odd = lax.cond(
            jnp.where(even, over_left, over_right),
            lambda: lax.ppermute(jnp.where(even, at_left, at_right), "lon", pairs("lon", 1)),
            lambda: nothing,
        )
        lists = -(-size // LANES)
        every = jnp.arange(lists * LANES, dtype=jnp.int32).reshape(lists, LANES)
        more, got = [], []
        for side, (over_side, some) in enumerate(((over_left, far_low), (over_right, far_high))):
            complete = jnp.where((side == 1) == even, got_even, got_odd)
            few = jnp.pad(notes[4 + side : 5 + side], ((0, lists - 1), (0, 0)))
            more.append(jnp.where(over_side, every, few))
            got.append(jnp.where(over_side, complete, jnp.pad(some, ((0, size - SLOTS), (0, 0)))))
        many = jnp.where(jnp.stack([over_left, over_right]), size, counts[2:])
        many = jnp.broadcast_to(jnp.concatenate([counts[:2], many])[:, None], (4, LANES))
        pick, frac, met, _ = weights(around)
        rhs, x, *_ = gather(state, *messages, pick, frac)
        return finish(size, jnp.concatenate([many] + more), got[0], got[1], met, frac, x, rhs)[0]

    return lax.cond(over[0] > 0, whole, lambda: out)


def solution(mesh):
    in_specs = (
        P(("member", "lat"), "lon", None),
        P(None, ("member", "lat"), "lon"),
        P(None, ("member", "lat"), "lon"),
        P(),
    )
    out_specs = P(("member", "lat"), "lon", None)
    return jax.shard_map(shards, mesh=mesh, in_specs=in_specs, out_specs=out_specs, check_vma=False)
```

time: 51.7 us -> 47.3 us (0.915); the launches traced: 51.6 us -> 47.9 us
  local copies, waits for them, and re-layouts: 2.69 us -> 0.18 us
  Pallas kernels: 23.6 us -> 21.8 us
  other arithmetic: 0 us -> 1.75 us
  waiting for transfers between devices: 5.72 us -> 4.57 us
    ppermute x1, waiting for transfers between devices: 4.28 us -> 0.01 us  [shards(): far_high = lax.ppermute(send_low, 'lon', left)]
    ppermute x1, waiting for transfers between devices: 0.01 us -> 3.28 us  [shards(): high_b = lax.ppermute(left_b, 'lon', left)]
    pallas_call x1, Pallas kernels: 4.64 us -> 2.92 us  [shards(): pl.pallas_call(functools.partial(pack_kernel, rows=rows, slots=SLOTS), ou...]
    unnamed x10 -> x4, local copies, waits for them, and re-layouts: 1.53 us -> 0.01 us
    another operation x1 -> x0, local copies, waits for them, and re-layouts: 1.15 us -> none
    pallas_call x2 -> x3, Pallas kernels: 16.4 us -> 17.3 us  [the longest x1 10.4 us: finish(): pl.pallas_call(functools.partial(main_kernel, slots=slots), out_shape=(sh...]
    convert_element_type x0 -> x1, other arithmetic: none -> 0.91 us  [shards(): dep_shift[None].astype(jnp.float32)]
    select_n x0 -> x1, other arithmetic: none -> 0.83 us  [shards(): jnp.where(is_shift, dep_shift[None].astype(jnp.float32), dep_frac[None])]
  transfers between devices with their start and end apart: 8 -> 8, of which waited for: 3 -> 2; matrix products, arithmetic and copies ran while one was open for 2% -> 0% of each run, Pallas kernels for 16% -> 21%
where the time goes in v3:
time: 47.3 us; the launch traced here: 47.9 us
  Pallas kernels  21.8 us (46%)
  starting transfers between devices  18.9 us (40%)
  waiting for transfers between devices  4.57 us (10%)
  other arithmetic  1.75 us (4%)
  between operations  0.74 us (2%)
    pallas_call x1, Pallas kernels, finish(): pl.pallas_call(functools.partial(main_kernel, slots=slots), out_shape=(sh...  10.4 us
    ppermute x1, starting transfers between devices, shards(): far_high = lax.ppermute(send_low, 'lon', left)  7.44 us
    pallas_call x1, Pallas kernels, gather(): pl.pallas_call(gather_kernel, out_shape=(rhs_shape, shape(x_shape)) + tup...  5.67 us
    ppermute x1, starting transfers between devices, shards(): high_b = lax.ppermute(left_b, 'lon', left)  4.72 us
    ppermute x1, waiting for transfers between devices, shards(): high_b = lax.ppermute(left_b, 'lon', left)  3.28 us
    ppermute x1, starting transfers between devices, shards(): high_a = lax.ppermute(left_a, 'lon', left)  3.1 us
    ppermute x1, starting transfers between devices, shards(): low_a = lax.ppermute(right_a, 'lon', right)  2.94 us
    pallas_call x1, Pallas kernels, shards(): pl.pallas_call(functools.partial(pack_kernel, rows=rows, slots=SLOTS), ou...  2.92 us
  transfers between devices with their start and end apart: 8, of which 2 were waited for; matrix products, arithmetic and copies ran while one was open for 0% of the time, Pallas kernels for 21%

profile of v3, /device:TPU:0, one launch (start us, length us, event | category | flops | bytes accessed | tf_op | source)
XLA Modules:
  0.0 47.9 jit_solution(13711929173181392423)
XLA Ops:
  0.0 0.1 broadcast_in_dim.49
  0.1 0.1 broadcast_in_dim.50
  0.2 0.0 copy-start
  0.2 0.9 %convert_element_type.19 = f32[2,32,32]{2,1,0:T(8,128)S(1)} convert(s32[2,32,32]{2,1,0:T(8,128)} %param.11) | non-fusion elementwise | flops 2048 | bytes 16384 | tf_op jit(solution)/shard_map/convert_element_type | solution.py:508
  1.1 0.8 %bitcast_select_fusion.dep_ref = f32[4,32,32]{2,1,0:T(8,128)S(1)} fusion(f32[2,32,32]{2,1,0:T(8,128)} %param.12, f32[2,32,32]{2,1,0:T(8,128)S(1)} %convert_element_type.19, pred[4]{0:T(512)(128)(4,1)S(1)} %broadcast_in_dim.50), kind=kLoop, calls=%fused_computation.15 | loop fusion | flops 4096 | bytes 32772 | tf_op jit(solution)/shard_map/jit(_where)/select_n | solution.py:508
  1.9 0.0 copy-start.9
  1.9 1.4 %shard_map.48 = (f32[4,32,128]{2,1,0:T(8,128)S(1)}, f32[4,32,640]{2,1,0:T(8,128)S(1)}, f32[128,640]{1,0:T(8,128)S(1)}, f32[128,640]{1,0:T(8,128)S(1)}) custom-call(s32[1]{0:T(128)} %bitcast.4.info_ref, f32[4,32,32]{2,1,0:T(8,128)S(1)} %bitcast_select_fusion.dep_ref, f32[32,32,640]{2,1,0:T(8,128)} %state_ref.3), custom_call_target="tpu_custom_call" | custom-call | tf_op jit(solution)/shard_map/pallas_call | solution.py:510
  3.3 0.5 %collective-permute-start.3 = (f32[4,32,640]{2,1,0:T(8,128)S(1)}, f32[4,32,640]{2,1,0:T(8,128)S(1)}, u32[]{:S(2)}, u32[]{:S(2)}) collective-permute-start(f32[4,32,640]{2,1,0:T(8,128)S(1)} %get-tuple-element.107), channel_id=1, source_target_pairs={{0,1},{1,0},{2,3},{3,2},{4,5},{5,4},{6,7},{7,6},{8,9},{9,8},{10,11... | collective-permute-start | bytes 983048 | tf_op jit(solution)/shard_map/ppermute | solution.py:523
  3.9 0.1 collective-permute-start.2
  3.9 1.3 %collective-permute-done.2.next_ref = f32[4,32,128]{2,1,0:T(8,128)S(1)} collective-permute-done((f32[4,32,128]{2,1,0:T(8,128)S(1)}, f32[4,32,128]{2,1,0:T(8,128)S(1)}, u32[]{:S(2)}, u32[]{:S(2)}) %collective-permute-start.2) | collective-permute-done | bytes 65568 | tf_op jit(solution)/shard_map/ppermute | solution.py:522
  5.2 0.0 collective-permute-done.3.edge_ref
  5.2 0.1 shard_map.49
  5.3 2.9 %collective-permute-start.4 = (f32[40,640]{1,0:T(8,128)S(1)}, f32[40,640]{1,0:T(8,128)S(1)}, u32[]{:S(2)}, u32[]{:S(2)}) collective-permute-start(f32[40,640]{1,0:T(8,128)S(1)} %get-tuple-element.111), channel_id=1, source_target_pairs={{0,2},{2,4},{4,6},{6,8},{8,10},{10,12},{12,14},{14,0},{1,3},{3,5},... | collective-permute-start | bytes 307208 | tf_op jit(solution)/shard_map/ppermute | solution.py:534
  8.3 3.1 %collective-permute-start.5 = (f32[40,640]{1,0:T(8,128)S(1)}, f32[40,640]{1,0:T(8,128)S(1)}, u32[]{:S(2)}, u32[]{:S(2)}) collective-permute-start(f32[40,640]{1,0:T(8,128)S(1)} %get-tuple-element.112), channel_id=1, source_target_pairs={{0,14},{2,0},{4,2},{6,4},{8,6},{10,8},{12,10},{14,12},{1,15},{3,1}... | collective-permute-start | bytes 307208 | tf_op jit(solution)/shard_map/ppermute | solution.py:535
  11.4 0.0 collective-permute-start.8
  11.4 4.7 %collective-permute-start.9 = (f32[112,640]{1,0:T(8,128)S(1)}, f32[112,640]{1,0:T(8,128)S(1)}, u32[]{:S(2)}, u32[]{:S(2)}) collective-permute-start(f32[112,640]{1,0:T(8,128)S(1)} %get-tuple-element.121), channel_id=1, source_target_pairs={{0,14},{2,0},{4,2},{6,4},{8,6},{10,8},{12,10},{14,12},{1,15},{3,1}... | collective-permute-start | bytes 860168 | tf_op jit(solution)/shard_map/ppermute | solution.py:537
  16.1 0.0 collective-permute-done.4.from_left_ref.low_a_ref
  16.1 0.0 collective-permute-done.5.from_right_ref.high_a_ref
  16.1 0.0 copy-done
  16.1 2.9 %shard_map.50 = (f32[80,640]{1,0:T(8,128)S(1)}, f32[80,640]{1,0:T(8,128)S(1)}, s32[8,128]{1,0:T(8,128)S(1)}, s32[1]{0:T(128)}, f32[4,40,128]{2,1,0:T(8,128)S(1)}) custom-call(s32[1]{0:T(128)} %bitcast.4.info_ref, f32[4,32,128]{2,1,0:T(8,128)S(1)} %get-tuple-element.110.dep_ref, f32[1024,640]{1,0:T(8,128)S(1)} %bitcast.14, f32[128,640]{1,0:T(8,128)S(1)} %bitcast.13, ...), custom_call_target="tpu_custom_call" | custom-call | bytes 41943040 | tf_op jit(solution)/shard_map/pallas_call | solution.py:541
  19.0 0.1 collective-permute-start.6
  19.1 7.4 %collective-permute-start.7 = (f32[80,640]{1,0:T(8,128)S(1)}, f32[80,640]{1,0:T(8,128)S(1)}, u32[]{:S(2)}, u32[]{:S(2)}) collective-permute-start(f32[80,640]{1,0:T(8,128)S(1)} %get-tuple-element.116), channel_id=1, source_target_pairs={{0,14},{2,0},{4,2},{6,4},{8,6},{10,8},{12,10},{14,12},{1,15},{3,1}... | collective-permute-start | bytes 614408 | tf_op jit(solution)/shard_map/ppermute | solution.py:556
  26.5 0.0 copy-done.9
  27.2 1.3 %shard_map.51 = (f32[36,80,128]{2,1,0:T(8,128)S(1)}, f32[36,80,128]{2,1,0:T(8,128)S(1)}, f32[2,2,36,8,128]{4,3,2,1,0:T(8,128)S(1)}, f32[4,40,128]{2,1,0:T(8,128)}) custom-call(f32[4,40,128]{2,1,0:T(8,128)S(1)} %get-tuple-element.117.wide_ref), custom_call_target="tpu_custom_call" | custom-call | tf_op jit(solution)/shard_map/pallas_call | solution.py:561
  28.5 0.0 collective-permute-done.8.low_b_ref
  28.5 3.3 %collective-permute-done.9.high_b_ref = f32[112,640]{1,0:T(8,128)S(1)} collective-permute-done((f32[112,640]{1,0:T(8,128)S(1)}, f32[112,640]{1,0:T(8,128)S(1)}, u32[]{:S(2)}, u32[]{:S(2)}) %collective-permute-start.9) | collective-permute-done | bytes 286752 | tf_op jit(solution)/shard_map/ppermute | solution.py:537
  31.8 5.7 %shard_map.52 = (f32[2,5,36,40,128]{4,3,2,1,0:T(8,128)S(1)}, f32[5,37,40,128]{3,2,1,0:T(8,128)S(1)}, f32[4,32,640]{2,1,0:T(8,128)S(1)}, f32[40,640]{1,0:T(8,128)...) custom-call(s32[1]{0:T(128)} %bitcast.4.info_ref, f32[32,32,640]{2,1,0:T(8,128)} %state_ref.3, ...), custom_call_target="tpu_custom_call" | custom-call | bytes 1048576 | tf_op jit(solution)/shard_map/pallas_call | solution.py:577
  37.5 0.0 collective-permute-done.6.far_low_ref
  37.5 0.0 collective-permute-done.7.far_high_ref
  37.5 10.4 %shard_map.53 = (f32[32,32,640]{2,1,0:T(8,128)}, f32[2,5,36,40,128]{4,3,2,1,0:T(8,128)S(1)}, f32[80,640]{1,0:T(8,128)}, f32[80,640]{1,0:T(8,128)}) custom-call(s32[1]{0:T(128)} %bitcast.4.info_ref, s32[8,128]{1,0:T(8,128)S(1)} %get-tuple-element.114.notes_ref, f32[80,640]{1,0:T(8,128)S(1)} %collective-permute-done.6.far_low_ref, ...), custom_call_target="tpu_custom_call", output_to_operand_aliasing={{1}: (8, {})} | custom-call | tf_op jit(solution)/shard_map/pallas_call | solution.py:591
  (3 shorter events, 0.0 us)
Async XLA Ops:
  0.2 15.9 %copy-start = (f32[32,32,640]{2,1,0:T(8,128)S(1)}, f32[32,32,640]{2,1,0:T(8,128)}, u32[]{:S(2)}) copy-start(f32[32,32,640]{2,1,0:T(8,128)} %state_ref.3) | copy-start | bytes 7864324
  1.9 24.6 %copy-start.9 = (f32[640]{0:T(1024)S(1)}, f32[640]{0:T(1024)}, u32[]{:S(2)}) copy-start(f32[640]{0:T(1024)} %param.13) | copy-start | bytes 7684
  3.3 1.9 %collective-permute-start.3 = (f32[4,32,640]{2,1,0:T(8,128)S(1)}, f32[4,32,640]{2,1,0:T(8,128)S(1)}, u32[]{:S(2)}, u32[]{:S(2)}) collective-permute-start(f32[4,32,640]{2,1,0:T(8,128)S(1)} %get-tuple-element.107), channel_id=1, source_target_pairs={{0,1},{1,0},{2,3},{3,2},{4,5},{5,4},{6,7},{7,6},{8,9},{9,8},{10,11... | collective-permute-start | bytes 983048 | tf_op jit(solution)/shard_map/ppermute | solution.py:523
  3.9 1.3 %collective-permute-start.2 = (f32[4,32,128]{2,1,0:T(8,128)S(1)}, f32[4,32,128]{2,1,0:T(8,128)S(1)}, u32[]{:S(2)}, u32[]{:S(2)}) collective-permute-start(f32[4,32,128]{2,1,0:T(8,128)S(1)} %get-tuple-element.106.own_ref), channel_id=1, source_target_pairs={{0,1},{1,0},{2,3},{3,2},{4,5},{5,4},{6,7},{7,6},{8,9},{9,8},{10,11... | collective-permute-start | bytes 196616 | tf_op jit(solution)/shard_map/ppermute | solution.py:522
  5.3 10.8 %collective-permute-start.4 = (f32[40,640]{1,0:T(8,128)S(1)}, f32[40,640]{1,0:T(8,128)S(1)}, u32[]{:S(2)}, u32[]{:S(2)}) collective-permute-start(f32[40,640]{1,0:T(8,128)S(1)} %get-tuple-element.111), channel_id=1, source_target_pairs={{0,2},{2,4},{4,6},{6,8},{8,10},{10,12},{12,14},{14,0},{1,3},{3,5},... | collective-permute-start | bytes 307208 | tf_op jit(solution)/shard_map/ppermute | solution.py:534
  8.3 7.8 %collective-permute-start.5 = (f32[40,640]{1,0:T(8,128)S(1)}, f32[40,640]{1,0:T(8,128)S(1)}, u32[]{:S(2)}, u32[]{:S(2)}) collective-permute-start(f32[40,640]{1,0:T(8,128)S(1)} %get-tuple-element.112), channel_id=1, source_target_pairs={{0,14},{2,0},{4,2},{6,4},{8,6},{10,8},{12,10},{14,12},{1,15},{3,1}... | collective-permute-start | bytes 307208 | tf_op jit(solution)/shard_map/ppermute | solution.py:535
  11.4 17.2 %collective-permute-start.8 = (f32[112,640]{1,0:T(8,128)S(1)}, f32[112,640]{1,0:T(8,128)S(1)}, u32[]{:S(2)}, u32[]{:S(2)}) collective-permute-start(f32[112,640]{1,0:T(8,128)S(1)} %get-tuple-element.120), channel_id=1, source_target_pairs={{0,2},{2,4},{4,6},{6,8},{8,10},{10,12},{12,14},{14,0},{1,3},{3,5},... | collective-permute-start | bytes 860168 | tf_op jit(solution)/shard_map/ppermute | solution.py:536
  11.4 20.4 %collective-permute-start.9 = (f32[112,640]{1,0:T(8,128)S(1)}, f32[112,640]{1,0:T(8,128)S(1)}, u32[]{:S(2)}, u32[]{:S(2)}) collective-permute-start(f32[112,640]{1,0:T(8,128)S(1)} %get-tuple-element.121), channel_id=1, source_target_pairs={{0,14},{2,0},{4,2},{6,4},{8,6},{10,8},{12,10},{14,12},{1,15},{3,1}... | collective-permute-start | bytes 860168 | tf_op jit(solution)/shard_map/ppermute | solution.py:537
  19.0 18.5 %collective-permute-start.6 = (f32[80,640]{1,0:T(8,128)S(1)}, f32[80,640]{1,0:T(8,128)S(1)}, u32[]{:S(2)}, u32[]{:S(2)}) collective-permute-start(f32[80,640]{1,0:T(8,128)S(1)} %get-tuple-element.115), channel_id=1, source_target_pairs={{0,2},{2,4},{4,6},{6,8},{8,10},{10,12},{12,14},{14,0},{1,3},{3,5},... | collective-permute-start | bytes 614408 | tf_op jit(solution)/shard_map/ppermute | solution.py:557
  19.1 18.4 %collective-permute-start.7 = (f32[80,640]{1,0:T(8,128)S(1)}, f32[80,640]{1,0:T(8,128)S(1)}, u32[]{:S(2)}, u32[]{:S(2)}) collective-permute-start(f32[80,640]{1,0:T(8,128)S(1)} %get-tuple-element.116), channel_id=1, source_target_pairs={{0,14},{2,0},{4,2},{6,4},{8,6},{10,8},{12,10},{14,12},{1,15},{3,1}... | collective-permute-start | bytes 614408 | tf_op jit(solution)/shard_map/ppermute | solution.py:556

commit v4 on v3

--- a/solution.py
+++ b/solution.py
@@ -18,7 +18,7 @@
 LANES = 128
 SIDE = 8
 UP_ROWS = 6
-SWEEP_ROWS = 6
+SWEEP_ROWS = 17
 
 
 def ring(axis, step):
@@ -32,19 +32,17 @@
     return edges + [(b, a) for a, b in edges]
 
 
-def start_kernel(
-    info_ref,
-    dep_ref,
-    state_ref,
-    own_ref,
-    edge_ref,
-    left_ref,
-    right_ref,
-    pad,
-    sides,
-    sems,
-):
-    kinds, rows, cols = dep_ref.shape
+def turn_kernel(shift_ref, frac_ref, own_ref, pad):
+    turns, rows, cols = shift_ref.shape
+    pad[...] = jnp.zeros_like(pad)
+    for kind in range(2 * turns):
+        value = shift_ref[kind].astype(jnp.float32) if kind < turns else frac_ref[kind - turns]
+        pad[0:rows, 0:cols] = value
+        own_ref[kind] = jnp.transpose(pad[...])[0:cols, :]
+
+
+def start_kernel(info_ref, state_ref, edge_ref, left_ref, right_ref, sides, sems):
+    rows, cols, _ = state_ref.shape
     edge_row = jnp.where(info_ref[0] == 0, rows - NEAR, 0)
     fetch = [
         pltpu.make_async_copy(state_ref.at[:, pl.ds(0, 8), :], sides.at[0], sems.at[0]),
@@ -53,10 +51,6 @@
     ]
     for copy in fetch:
         copy.start()
-    pad[...] = jnp.zeros_like(pad)
-    for kind in range(kinds):
-        pad[0:rows, 0:cols] = dep_ref[kind]
-        own_ref[kind] = jnp.transpose(pad[...])[0:cols, :]
     for side, (first, ref) in enumerate(((0, left_ref), (8 - NEAR, right_ref))):
         fetch[side].wait()
         for r in range(0, rows, 2):
@@ -394,7 +388,7 @@
             xa[f, rows, 8 * k : 8 * k + 8, :] = zero
             xb[f, rows, 8 * k : 8 * k + 8, :] = zero
 
-    def lift(source, count):
+    def lift(source, ups, count):
         def block(n, _):
             at = pl.ds(pl.multiple_of(n * 8, 8), 8)
             lane = lax.broadcasted_iota(jnp.int32, (8, LEV), 1)
@@ -406,10 +400,10 @@
 
         lax.fori_loop(0, count // 8, block, 0)
 
-    def put(side, m, j, source, n):
+    def put(side, m, j, n):
         k = 0 if side == 0 else groups - 1
         e = jnp.where(m < lat_rows, own0 + m, ext0 + m - lat_rows)
-        column, up = source[pl.ds(n, 1), :], ups[pl.ds(n, 1), :]
+        column, up = (far_low_ref, far_high_ref)[side][pl.ds(n, 1), :], ups[side, pl.ds(n, 1), :]
         for turn in range(TRAJ):
             hit = met_ref[side, turn, m] == j.astype(jnp.float32)
             frac = frac_ref[m, turn * wide + 8 * k : turn * wide + 8 * k + 8, :]
@@ -419,15 +413,18 @@
                 at = (turn, f, e, slice(8 * k, 8 * k + 8), slice(None))
                 rhs[at] = jnp.where(hit, mixed, rhs[at])
 
-    for side, far_ref in enumerate((far_low_ref, far_high_ref)):
-        lift(far_ref, slots)
-
-        def place(n, _, side=side, far_ref=far_ref):
+    fars = (far_low_ref, far_high_ref)
+    counts = [jnp.minimum(notes_ref[2 + side, LANES - 1], slots) for side in range(2)]
+    for side in range(2):
+        lift(fars[side], ups.at[side], slots)
+
+    def place(n, _):
+        for side in range(2):
             address = notes_ref[4 + side * -(-slots // LANES) + n // LANES, n % LANES]
-            put(side, address >> 3, address & 7, far_ref, n)
-            return 0
-
-        lax.fori_loop(0, jnp.minimum(notes_ref[2 + side, LANES - 1], slots), place, 0)
+            put(side, address >> 3, jnp.where(n < counts[side], address & 7, -LANES), n)
+        return 0
+
+    lax.fori_loop(0, jnp.maximum(counts[0], counts[1]), place, 0)
 
     sub = lax.broadcasted_iota(jnp.int32, (8, LEV), 0)
     bottom, last = sub == 0, sub == 7
@@ -442,14 +439,19 @@
             prev = omega
             turn = sweep // 2
             src, dst = (x_ref, xa, xb, xa)[sweep], (xa, xb, xa, None)[sweep]
+            beyond = 2 * TRAJ - 1 - sweep
+            start = jnp.maximum(own0 - beyond, 0)
+            step = max(d for d in range(1, SWEEP_ROWS + 1) if (lat_rows + beyond) % d == 0)
 
             def load(e, src=src):
                 return [src[f, e, 8 * k : 8 * k + 8, :] for k in range(groups)]
 
-            def block(group, carry, load=load, dst=dst, alpha=alpha, beta=beta, turn=turn, omega=omega):
+            def block(
+                group, carry, load=load, dst=dst, alpha=alpha, beta=beta, turn=turn, omega=omega, start=start, step=step
+            ):
                 south, mid = carry
-                for v in range(SWEEP_ROWS):
-                    e = group * SWEEP_ROWS + v
+                for v in range(step):
+                    e = start + group * step + v
                     north = load(e + 1)
                     left, right = mid[0], mid[groups - 1]
                     first, final = mid[1], mid[groups - 2]
@@ -471,7 +473,8 @@
                     south, mid = mid, north
                 return south, mid
 
-            lax.fori_loop(0, rows // SWEEP_ROWS, block, ([zero] * groups, load(0)))
+            before = [jnp.where(start == 0, 0.0, v) for v in load(jnp.maximum(start - 1, 0))]
+            lax.fori_loop(0, (lat_rows + beyond) // step, block, (before, load(start)))
 
         lanes = pl.ds(pl.multiple_of(f * LEV, LEV), LEV)
         part = nat.at[f, pl.ds(own0, lat_rows), pl.ds(NEAR, cols), :]
@@ -504,21 +507,26 @@
     anywhere = pl.BlockSpec(memory_space=pl.ANY)
     hbm = pl.BlockSpec(memory_space=pltpu.HBM)
 
-    is_shift = jnp.arange(2)[:, None, None, None] == 0
-    dep = jnp.where(is_shift, dep_shift[None].astype(jnp.float32), dep_frac[None]).reshape(kinds, lat_rows, cols)
     near = shape((lat_rows * NEAR, width))
-    own, edge, near_left, near_right = pl.pallas_call(
+    edge, near_left, near_right = pl.pallas_call(
         start_kernel,
-        out_shape=(shape((kinds, cols, LANES)), shape((NEAR, cols, width)), near, near),
-        in_specs=[smem, vmem, hbm],
-        out_specs=(vmem,) * 4,
+        out_shape=(shape((NEAR, cols, width)), near, near),
+        in_specs=[smem, hbm],
+        out_specs=(vmem,) * 3,
         scratch_shapes=[
-            pltpu.VMEM((LANES, LANES), jnp.float32),
             pltpu.VMEM((2, lat_rows, 8, width), jnp.float32),
             pltpu.SemaphoreType.DMA((3,)),
         ],
         compiler_params=pltpu.CompilerParams(vmem_limit_bytes=16 * 2**20),
-    )(info, dep, state)
+    )(info, state)
+    own = pl.pallas_call(
+        turn_kernel,
+        out_shape=shape((kinds, cols, LANES)),
+        in_specs=[vmem] * 2,
+        out_specs=vmem,
+        scratch_shapes=[pltpu.VMEM((LANES, LANES), jnp.float32)],
+        compiler_params=pltpu.CompilerParams(vmem_limit_bytes=4 * 2**20),
+    )(dep_shift, dep_frac)
     other = lax.ppermute(own, "lat", swap)
     edge = lax.ppermute(edge, "lat", swap)
     some = lat_rows // 4 * NEAR
@@ -594,7 +602,7 @@
             in_specs=[smem] * 2 + [vmem] * 7,
             out_specs=(hbm, vmem, hbm, hbm),
             scratch_shapes=[
-                pltpu.VMEM((slots, width), jnp.float32),
+                pltpu.VMEM((2, slots, width), jnp.float32),
                 pltpu.VMEM(x_shape, jnp.float32),
                 pltpu.VMEM(x_shape, jnp.float32),
                 pltpu.VMEM((tiles, rows, wide, LEV), jnp.float32),

time: 47.3 us -> 45.3 us (0.958); the launches traced: 47.9 us -> 45.3 us
  other arithmetic: 1.75 us -> 0 us
  waiting for transfers between devices: 4.57 us -> 3.14 us
  local copies, waits for them, and re-layouts: 0.18 us -> 1.53 us
  Pallas kernels: 21.8 us -> 20.9 us
    ppermute x1, waiting for transfers between devices: 3.28 us -> 0.01 us  [shards(): high_b = lax.ppermute(left_b, 'lon', left)]
    ppermute x1, waiting for transfers between devices: 0.01 us -> 1.93 us  [shards(): far_high = lax.ppermute(send_low, 'lon', left)]
    unnamed x4 -> x8, local copies, waits for them, and re-layouts: 0.01 us -> 1.52 us
    pallas_call x1, Pallas kernels: 10.4 us -> 9.33 us  [finish(): pl.pallas_call(functools.partial(main_kernel, slots=slots), out_shape=(sh...]
    convert_element_type x1 -> x0, other arithmetic: 0.91 us -> none  [shards(): dep_shift[None].astype(jnp.float32)]
    select_n x1 -> x0, other arithmetic: 0.83 us -> none  [shards(): jnp.where(is_shift, dep_shift[None].astype(jnp.float32), dep_frac[None])]
    pallas_call x1 -> x2, Pallas kernels: 1.41 us -> 1.65 us  [the longest x1 1.55 us: shards(): pl.pallas_call(start_kernel, out_shape=(shape((NEAR, cols, width)), near,...]
  transfers between devices with their start and end apart: 8 -> 8, of which waited for: 2 -> 2; matrix products, arithmetic and copies ran while one was open for 0% -> 0% of each run, Pallas kernels for 21% -> 22%
where the time goes in v4:
time: 45.3 us
  Pallas kernels  20.9 us (46%)
  starting transfers between devices  19 us (42%)
  waiting for transfers between devices  3.14 us (7%)
  local copies, waits for them, and re-layouts  1.53 us (3%)
  between operations  0.74 us (2%)
    pallas_call x1, Pallas kernels, finish(): pl.pallas_call(functools.partial(main_kernel, slots=slots), out_shape=(sh...  9.33 us
    ppermute x1, starting transfers between devices, shards(): far_high = lax.ppermute(send_low, 'lon', left)  7.78 us
    pallas_call x1, Pallas kernels, gather(): pl.pallas_call(gather_kernel, out_shape=(rhs_shape, shape(x_shape)) + tup...  5.66 us
    ppermute x1, starting transfers between devices, shards(): high_b = lax.ppermute(left_b, 'lon', left)  4.72 us
    ppermute x1, starting transfers between devices, shards(): high_a = lax.ppermute(left_a, 'lon', left)  3.1 us
    pallas_call x1, Pallas kernels, shards(): pl.pallas_call(functools.partial(pack_kernel, rows=rows, slots=SLOTS), ou...  2.82 us
    ppermute x1, starting transfers between devices, shards(): low_a = lax.ppermute(right_a, 'lon', right)  2.72 us
    ppermute x1, waiting for transfers between devices, shards(): far_high = lax.ppermute(send_low, 'lon', left)  1.93 us
  transfers between devices with their start and end apart: 8, of which 2 were waited for; matrix products, arithmetic and copies ran while one was open for 0% of the time, Pallas kernels for 22%

profile of v4, /device:TPU:0, one launch (start us, length us, event | category | flops | bytes accessed | tf_op | source)
XLA Modules:
  0.0 45.3 jit_solution(17350422382427399262)
XLA Ops:
  0.0 0.0 copy-start.2
  0.0 0.0 copy-start.11
  0.0 1.5 %shard_map.49 = (f32[4,32,640]{2,1,0:T(8,128)S(1)}, f32[128,640]{1,0:T(8,128)S(1)}, f32[128,640]{1,0:T(8,128)S(1)}) custom-call(s32[1]{0:T(128)} %bitcast.4.info_ref, f32[32,32,640]{2,1,0:T(8,128)} %state_ref.3), custom_call_target="tpu_custom_call" | custom-call | tf_op jit(solution)/shard_map/pallas_call | solution.py:511
  1.6 0.5 %collective-permute-start.3 = (f32[4,32,640]{2,1,0:T(8,128)S(1)}, f32[4,32,640]{2,1,0:T(8,128)S(1)}, u32[]{:S(2)}, u32[]{:S(2)}) collective-permute-start(f32[4,32,640]{2,1,0:T(8,128)S(1)} %get-tuple-element.105), channel_id=1, source_target_pairs={{0,1},{1,0},{2,3},{3,2},{4,5},{5,4},{6,7},{7,6},{8,9},{9,8},{10,11... | collective-permute-start | bytes 983048 | tf_op jit(solution)/shard_map/ppermute | solution.py:531
  2.1 0.0 copy-start
  2.1 0.8 %copy-done = s32[2,32,32]{2,1,0:T(8,128)S(1)} copy-done((s32[2,32,32]{2,1,0:T(8,128)S(1)}, s32[2,32,32]{2,1,0:T(8,128)}, u32[]{:S(2)}) %copy-start) | copy-done | bytes 8216
  2.8 0.0 copy-start.1
  2.8 0.8 %copy-done.1 = f32[2,32,32]{2,1,0:T(8,128)S(1)} copy-done((f32[2,32,32]{2,1,0:T(8,128)S(1)}, f32[2,32,32]{2,1,0:T(8,128)}, u32[]{:S(2)}) %copy-start.1) | copy-done | bytes 8216
  3.6 0.1 shard_map.48.own_ref
  3.7 0.1 collective-permute-start.2
  3.8 1.2 %collective-permute-done.2.next_ref = f32[4,32,128]{2,1,0:T(8,128)S(1)} collective-permute-done((f32[4,32,128]{2,1,0:T(8,128)S(1)}, f32[4,32,128]{2,1,0:T(8,128)S(1)}, u32[]{:S(2)}, u32[]{:S(2)}) %collective-permute-start.2) | collective-permute-done | bytes 65568 | tf_op jit(solution)/shard_map/ppermute | solution.py:530
  5.0 0.0 collective-permute-done.3.edge_ref
  5.0 0.1 shard_map.50
  5.1 2.7 %collective-permute-start.4 = (f32[40,640]{1,0:T(8,128)S(1)}, f32[40,640]{1,0:T(8,128)S(1)}, u32[]{:S(2)}, u32[]{:S(2)}) collective-permute-start(f32[40,640]{1,0:T(8,128)S(1)} %get-tuple-element.109), channel_id=1, source_target_pairs={{0,2},{2,4},{4,6},{6,8},{8,10},{10,12},{12,14},{14,0},{1,3},{3,5},... | collective-permute-start | bytes 307208 | tf_op jit(solution)/shard_map/ppermute | solution.py:542
  7.9 3.1 %collective-permute-start.5 = (f32[40,640]{1,0:T(8,128)S(1)}, f32[40,640]{1,0:T(8,128)S(1)}, u32[]{:S(2)}, u32[]{:S(2)}) collective-permute-start(f32[40,640]{1,0:T(8,128)S(1)} %get-tuple-element.110), channel_id=1, source_target_pairs={{0,14},{2,0},{4,2},{6,4},{8,6},{10,8},{12,10},{14,12},{1,15},{3,1}... | collective-permute-start | bytes 307208 | tf_op jit(solution)/shard_map/ppermute | solution.py:543
  11.0 0.0 collective-permute-start.8
  11.0 4.7 %collective-permute-start.9 = (f32[112,640]{1,0:T(8,128)S(1)}, f32[112,640]{1,0:T(8,128)S(1)}, u32[]{:S(2)}, u32[]{:S(2)}) collective-permute-start(f32[112,640]{1,0:T(8,128)S(1)} %get-tuple-element.119), channel_id=1, source_target_pairs={{0,14},{2,0},{4,2},{6,4},{8,6},{10,8},{12,10},{14,12},{1,15},{3,1}... | collective-permute-start | bytes 860168 | tf_op jit(solution)/shard_map/ppermute | solution.py:545
  15.7 0.0 collective-permute-done.4.from_left_ref.low_a_ref
  15.7 0.0 collective-permute-done.5.from_right_ref.high_a_ref
  15.7 0.0 copy-done.2
  15.7 2.8 %shard_map.51 = (f32[80,640]{1,0:T(8,128)S(1)}, f32[80,640]{1,0:T(8,128)S(1)}, s32[8,128]{1,0:T(8,128)S(1)}, s32[1]{0:T(128)}, f32[4,40,128]{2,1,0:T(8,128)S(1)}) custom-call(s32[1]{0:T(128)} %bitcast.4.info_ref, f32[4,32,128]{2,1,0:T(8,128)S(1)} %get-tuple-element.108.dep_ref, f32[1024,640]{1,0:T(8,128)S(1)} %bitcast.10, f32[128,640]{1,0:T(8,128)S(1)} %bitcast.9, ...), custom_call_target="tpu_custom_call" | custom-call | bytes 41943040 | tf_op jit(solution)/shard_map/pallas_call | solution.py:549
  18.5 0.1 collective-permute-start.6
  18.6 7.8 %collective-permute-start.7 = (f32[80,640]{1,0:T(8,128)S(1)}, f32[80,640]{1,0:T(8,128)S(1)}, u32[]{:S(2)}, u32[]{:S(2)}) collective-permute-start(f32[80,640]{1,0:T(8,128)S(1)} %get-tuple-element.114), channel_id=1, source_target_pairs={{0,14},{2,0},{4,2},{6,4},{8,6},{10,8},{12,10},{14,12},{1,15},{3,1}... | collective-permute-start | bytes 614408 | tf_op jit(solution)/shard_map/ppermute | solution.py:564
  26.4 0.0 copy-done.11
  27.0 1.3 %shard_map.52 = (f32[36,80,128]{2,1,0:T(8,128)S(1)}, f32[36,80,128]{2,1,0:T(8,128)S(1)}, f32[2,2,36,8,128]{4,3,2,1,0:T(8,128)S(1)}, f32[4,40,128]{2,1,0:T(8,128)}) custom-call(f32[4,40,128]{2,1,0:T(8,128)S(1)} %get-tuple-element.115.wide_ref), custom_call_target="tpu_custom_call" | custom-call | tf_op jit(solution)/shard_map/pallas_call | solution.py:569
  28.4 0.0 collective-permute-done.8.low_b_ref
  28.4 0.0 collective-permute-done.9.high_b_ref
  28.4 5.7 %shard_map.53 = (f32[2,5,36,40,128]{4,3,2,1,0:T(8,128)S(1)}, f32[5,37,40,128]{3,2,1,0:T(8,128)S(1)}, f32[4,32,640]{2,1,0:T(8,128)S(1)}, f32[40,640]{1,0:T(8,128)...) custom-call(s32[1]{0:T(128)} %bitcast.4.info_ref, f32[32,32,640]{2,1,0:T(8,128)} %state_ref.3, ...), custom_call_target="tpu_custom_call" | custom-call | bytes 1048576 | tf_op jit(solution)/shard_map/pallas_call | solution.py:585
  34.0 0.0 collective-permute-done.6.far_low_ref
  34.0 1.9 %collective-permute-done.7.far_high_ref = f32[80,640]{1,0:T(8,128)S(1)} collective-permute-done((f32[80,640]{1,0:T(8,128)S(1)}, f32[80,640]{1,0:T(8,128)S(1)}, u32[]{:S(2)}, u32[]{:S(2)}) %collective-permute-start.7) | collective-permute-done | bytes 204832 | tf_op jit(solution)/shard_map/ppermute | solution.py:564
  36.0 9.3 %shard_map.54 = (f32[32,32,640]{2,1,0:T(8,128)}, f32[2,5,36,40,128]{4,3,2,1,0:T(8,128)S(1)}, f32[80,640]{1,0:T(8,128)}, f32[80,640]{1,0:T(8,128)}) custom-call(s32[1]{0:T(128)} %bitcast.4.info_ref, s32[8,128]{1,0:T(8,128)S(1)} %get-tuple-element.112.notes_ref, f32[80,640]{1,0:T(8,128)S(1)} %collective-permute-done.6.far_low_ref, ...), custom_call_target="tpu_custom_call", output_to_operand_aliasing={{1}: (8, {})} | custom-call | tf_op jit(solution)/shard_map/pallas_call | solution.py:599
  (2 shorter events, 0.0 us)
Async XLA Ops:
  0.0 15.7 %copy-start.2 = (f32[32,32,640]{2,1,0:T(8,128)S(1)}, f32[32,32,640]{2,1,0:T(8,128)}, u32[]{:S(2)}) copy-start(f32[32,32,640]{2,1,0:T(8,128)} %state_ref.3) | copy-start | bytes 7864324
  0.0 26.4 %copy-start.11 = (f32[640]{0:T(1024)S(1)}, f32[640]{0:T(1024)}, u32[]{:S(2)}) copy-start(f32[640]{0:T(1024)} %param.13) | copy-start | bytes 7684
  1.6 3.5 %collective-permute-start.3 = (f32[4,32,640]{2,1,0:T(8,128)S(1)}, f32[4,32,640]{2,1,0:T(8,128)S(1)}, u32[]{:S(2)}, u32[]{:S(2)}) collective-permute-start(f32[4,32,640]{2,1,0:T(8,128)S(1)} %get-tuple-element.105), channel_id=1, source_target_pairs={{0,1},{1,0},{2,3},{3,2},{4,5},{5,4},{6,7},{7,6},{8,9},{9,8},{10,11... | collective-permute-start | bytes 983048 | tf_op jit(solution)/shard_map/ppermute | solution.py:531
  2.1 0.8 %copy-start = (s32[2,32,32]{2,1,0:T(8,128)S(1)}, s32[2,32,32]{2,1,0:T(8,128)}, u32[]{:S(2)}) copy-start(s32[2,32,32]{2,1,0:T(8,128)} %shift_ref.1) | copy-start | bytes 24580
  2.8 0.8 %copy-start.1 = (f32[2,32,32]{2,1,0:T(8,128)S(1)}, f32[2,32,32]{2,1,0:T(8,128)}, u32[]{:S(2)}) copy-start(f32[2,32,32]{2,1,0:T(8,128)} %frac_ref.1) | copy-start | bytes 24580
  3.7 1.3 %collective-permute-start.2 = (f32[4,32,128]{2,1,0:T(8,128)S(1)}, f32[4,32,128]{2,1,0:T(8,128)S(1)}, u32[]{:S(2)}, u32[]{:S(2)}) collective-permute-start(f32[4,32,128]{2,1,0:T(8,128)S(1)} %shard_map.48.own_ref), channel_id=1, source_target_pairs={{0,1},{1,0},{2,3},{3,2},{4,5},{5,4},{6,7},{7,6},{8,9},{9,8},{10,11... | collective-permute-start | bytes 196616 | tf_op jit(solution)/shard_map/ppermute | solution.py:530
  5.1 10.6 %collective-permute-start.4 = (f32[40,640]{1,0:T(8,128)S(1)}, f32[40,640]{1,0:T(8,128)S(1)}, u32[]{:S(2)}, u32[]{:S(2)}) collective-permute-start(f32[40,640]{1,0:T(8,128)S(1)} %get-tuple-element.109), channel_id=1, source_target_pairs={{0,2},{2,4},{4,6},{6,8},{8,10},{10,12},{12,14},{14,0},{1,3},{3,5},... | collective-permute-start | bytes 307208 | tf_op jit(solution)/shard_map/ppermute | solution.py:542
  7.9 7.8 %collective-permute-start.5 = (f32[40,640]{1,0:T(8,128)S(1)}, f32[40,640]{1,0:T(8,128)S(1)}, u32[]{:S(2)}, u32[]{:S(2)}) collective-permute-start(f32[40,640]{1,0:T(8,128)S(1)} %get-tuple-element.110), channel_id=1, source_target_pairs={{0,14},{2,0},{4,2},{6,4},{8,6},{10,8},{12,10},{14,12},{1,15},{3,1}... | collective-permute-start | bytes 307208 | tf_op jit(solution)/shard_map/ppermute | solution.py:543
  11.0 17.4 %collective-permute-start.8 = (f32[112,640]{1,0:T(8,128)S(1)}, f32[112,640]{1,0:T(8,128)S(1)}, u32[]{:S(2)}, u32[]{:S(2)}) collective-permute-start(f32[112,640]{1,0:T(8,128)S(1)} %get-tuple-element.118), channel_id=1, source_target_pairs={{0,2},{2,4},{4,6},{6,8},{8,10},{10,12},{12,14},{14,0},{1,3},{3,5},... | collective-permute-start | bytes 860168 | tf_op jit(solution)/shard_map/ppermute | solution.py:544
  11.0 17.4 %collective-permute-start.9 = (f32[112,640]{1,0:T(8,128)S(1)}, f32[112,640]{1,0:T(8,128)S(1)}, u32[]{:S(2)}, u32[]{:S(2)}) collective-permute-start(f32[112,640]{1,0:T(8,128)S(1)} %get-tuple-element.119), channel_id=1, source_target_pairs={{0,14},{2,0},{4,2},{6,4},{8,6},{10,8},{12,10},{14,12},{1,15},{3,1}... | collective-permute-start | bytes 860168 | tf_op jit(solution)/shard_map/ppermute | solution.py:545
  18.5 15.5 %collective-permute-start.6 = (f32[80,640]{1,0:T(8,128)S(1)}, f32[80,640]{1,0:T(8,128)S(1)}, u32[]{:S(2)}, u32[]{:S(2)}) collective-permute-start(f32[80,640]{1,0:T(8,128)S(1)} %get-tuple-element.113), channel_id=1, source_target_pairs={{0,2},{2,4},{4,6},{6,8},{8,10},{10,12},{12,14},{14,0},{1,3},{3,5},... | collective-permute-start | bytes 614408 | tf_op jit(solution)/shard_map/ppermute | solution.py:565
  18.6 17.4 %collective-permute-start.7 = (f32[80,640]{1,0:T(8,128)S(1)}, f32[80,640]{1,0:T(8,128)S(1)}, u32[]{:S(2)}, u32[]{:S(2)}) collective-permute-start(f32[80,640]{1,0:T(8,128)S(1)} %get-tuple-element.114), channel_id=1, source_target_pairs={{0,14},{2,0},{4,2},{6,4},{8,6},{10,8},{12,10},{14,12},{1,15},{3,1}... | collective-permute-start | bytes 614408 | tf_op jit(solution)/shard_map/ppermute | solution.py:564

commit v5 on v4

--- a/solution.py
+++ b/solution.py
@@ -17,8 +17,8 @@
 SLOTS = 80
 LANES = 128
 SIDE = 8
-UP_ROWS = 6
-SWEEP_ROWS = 17
+UP_ROWS = 12
+SWEEP_ROWS = 36
 
 
 def ring(axis, step):

time: 45.3 us -> 45.3 us (level)
  waiting for transfers between devices: 3.14 us -> 4.53 us
  Pallas kernels: 20.9 us -> 19.8 us
    ppermute x1, waiting for transfers between devices: 0.01 us -> 3.31 us  [shards(): high_b = lax.ppermute(left_b, 'lon', left)]
    ppermute x1, waiting for transfers between devices: 1.93 us -> 0.01 us  [shards(): far_high = lax.ppermute(send_low, 'lon', left)]
    pallas_call x1, Pallas kernels: 5.66 us -> 5.12 us  [gather(): pl.pallas_call(gather_kernel, out_shape=(rhs_shape, shape(x_shape)) + tup...]
    pallas_call x1, Pallas kernels: 9.33 us -> 8.81 us  [finish(): pl.pallas_call(functools.partial(main_kernel, slots=slots), out_shape=(sh...]
  transfers between devices with their start and end apart: 8 -> 8, of which waited for: 2 -> 2; matrix products, arithmetic and copies ran while one was open for 0% -> 0% of each run, Pallas kernels for 22% -> 20%
where the time goes in v5:
time: 45.3 us; the launch traced here: 45.6 us
  Pallas kernels  19.8 us (44%)
  starting transfers between devices  19 us (42%)
  waiting for transfers between devices  4.53 us (10%)
  local copies, waits for them, and re-layouts  1.53 us (3%)
  between operations  0.74 us (2%)
    pallas_call x1, Pallas kernels, finish(): pl.pallas_call(functools.partial(main_kernel, slots=slots), out_shape=(sh...  8.81 us
    ppermute x1, starting transfers between devices, shards(): far_high = lax.ppermute(send_low, 'lon', left)  7.72 us
    pallas_call x1, Pallas kernels, gather(): pl.pallas_call(gather_kernel, out_shape=(rhs_shape, shape(x_shape)) + tup...  5.12 us
    ppermute x1, starting transfers between devices, shards(): high_b = lax.ppermute(left_b, 'lon', left)  4.72 us
    ppermute x1, waiting for transfers between devices, shards(): high_b = lax.ppermute(left_b, 'lon', left)  3.31 us
    ppermute x1, starting transfers between devices, shards(): high_a = lax.ppermute(left_a, 'lon', left)  3.1 us
    pallas_call x1, Pallas kernels, shards(): pl.pallas_call(functools.partial(pack_kernel, rows=rows, slots=SLOTS), ou...  2.8 us
    ppermute x1, starting transfers between devices, shards(): low_a = lax.ppermute(right_a, 'lon', right)  2.72 us
  transfers between devices with their start and end apart: 8, of which 2 were waited for; matrix products, arithmetic and copies ran while one was open for 0% of the time, Pallas kernels for 20%

profile of v5, /device:TPU:0, one launch (start us, length us, event | category | flops | bytes accessed | tf_op | source)
XLA Modules:
  0.0 45.6 jit_solution(7004779435033501132)
XLA Ops:
  0.0 0.0 copy-start.2
  0.0 0.0 copy-start.11
  0.0 1.5 %shard_map.49 = (f32[4,32,640]{2,1,0:T(8,128)S(1)}, f32[128,640]{1,0:T(8,128)S(1)}, f32[128,640]{1,0:T(8,128)S(1)}) custom-call(s32[1]{0:T(128)} %bitcast.4.info_ref, f32[32,32,640]{2,1,0:T(8,128)} %state_ref.3), custom_call_target="tpu_custom_call" | custom-call | tf_op jit(solution)/shard_map/pallas_call | solution.py:511
  1.6 0.5 %collective-permute-start.3 = (f32[4,32,640]{2,1,0:T(8,128)S(1)}, f32[4,32,640]{2,1,0:T(8,128)S(1)}, u32[]{:S(2)}, u32[]{:S(2)}) collective-permute-start(f32[4,32,640]{2,1,0:T(8,128)S(1)} %get-tuple-element.105), channel_id=1, source_target_pairs={{0,1},{1,0},{2,3},{3,2},{4,5},{5,4},{6,7},{7,6},{8,9},{9,8},{10,11... | collective-permute-start | bytes 983048 | tf_op jit(solution)/shard_map/ppermute | solution.py:531
  2.1 0.0 copy-start
  2.1 0.8 %copy-done = s32[2,32,32]{2,1,0:T(8,128)S(1)} copy-done((s32[2,32,32]{2,1,0:T(8,128)S(1)}, s32[2,32,32]{2,1,0:T(8,128)}, u32[]{:S(2)}) %copy-start) | copy-done | bytes 8216
  2.8 0.0 copy-start.1
  2.8 0.8 %copy-done.1 = f32[2,32,32]{2,1,0:T(8,128)S(1)} copy-done((f32[2,32,32]{2,1,0:T(8,128)S(1)}, f32[2,32,32]{2,1,0:T(8,128)}, u32[]{:S(2)}) %copy-start.1) | copy-done | bytes 8216
  3.6 0.1 shard_map.48.own_ref
  3.7 0.1 collective-permute-start.2
  3.8 1.2 %collective-permute-done.2.next_ref = f32[4,32,128]{2,1,0:T(8,128)S(1)} collective-permute-done((f32[4,32,128]{2,1,0:T(8,128)S(1)}, f32[4,32,128]{2,1,0:T(8,128)S(1)}, u32[]{:S(2)}, u32[]{:S(2)}) %collective-permute-start.2) | collective-permute-done | bytes 65568 | tf_op jit(solution)/shard_map/ppermute | solution.py:530
  5.0 0.0 collective-permute-done.3.edge_ref
  5.0 0.1 shard_map.50
  5.1 2.7 %collective-permute-start.4 = (f32[40,640]{1,0:T(8,128)S(1)}, f32[40,640]{1,0:T(8,128)S(1)}, u32[]{:S(2)}, u32[]{:S(2)}) collective-permute-start(f32[40,640]{1,0:T(8,128)S(1)} %get-tuple-element.109), channel_id=1, source_target_pairs={{0,2},{2,4},{4,6},{6,8},{8,10},{10,12},{12,14},{14,0},{1,3},{3,5},... | collective-permute-start | bytes 307208 | tf_op jit(solution)/shard_map/ppermute | solution.py:542
  7.9 3.1 %collective-permute-start.5 = (f32[40,640]{1,0:T(8,128)S(1)}, f32[40,640]{1,0:T(8,128)S(1)}, u32[]{:S(2)}, u32[]{:S(2)}) collective-permute-start(f32[40,640]{1,0:T(8,128)S(1)} %get-tuple-element.110), channel_id=1, source_target_pairs={{0,14},{2,0},{4,2},{6,4},{8,6},{10,8},{12,10},{14,12},{1,15},{3,1}... | collective-permute-start | bytes 307208 | tf_op jit(solution)/shard_map/ppermute | solution.py:543
  11.0 0.0 collective-permute-start.8
  11.0 4.7 %collective-permute-start.9 = (f32[112,640]{1,0:T(8,128)S(1)}, f32[112,640]{1,0:T(8,128)S(1)}, u32[]{:S(2)}, u32[]{:S(2)}) collective-permute-start(f32[112,640]{1,0:T(8,128)S(1)} %get-tuple-element.119), channel_id=1, source_target_pairs={{0,14},{2,0},{4,2},{6,4},{8,6},{10,8},{12,10},{14,12},{1,15},{3,1}... | collective-permute-start | bytes 860168 | tf_op jit(solution)/shard_map/ppermute | solution.py:545
  15.7 0.0 collective-permute-done.4.from_left_ref.low_a_ref
  15.7 0.0 collective-permute-done.5.from_right_ref.high_a_ref
  15.7 0.0 copy-done.2
  15.7 2.8 %shard_map.51 = (f32[80,640]{1,0:T(8,128)S(1)}, f32[80,640]{1,0:T(8,128)S(1)}, s32[8,128]{1,0:T(8,128)S(1)}, s32[1]{0:T(128)}, f32[4,40,128]{2,1,0:T(8,128)S(1)}) custom-call(s32[1]{0:T(128)} %bitcast.4.info_ref, f32[4,32,128]{2,1,0:T(8,128)S(1)} %get-tuple-element.108.dep_ref, f32[1024,640]{1,0:T(8,128)S(1)} %bitcast.10, f32[128,640]{1,0:T(8,128)S(1)} %bitcast.9, ...), custom_call_target="tpu_custom_call" | custom-call | bytes 41943040 | tf_op jit(solution)/shard_map/pallas_call | solution.py:549
  18.5 0.1 collective-permute-start.6
  18.6 7.7 %collective-permute-start.7 = (f32[80,640]{1,0:T(8,128)S(1)}, f32[80,640]{1,0:T(8,128)S(1)}, u32[]{:S(2)}, u32[]{:S(2)}) collective-permute-start(f32[80,640]{1,0:T(8,128)S(1)} %get-tuple-element.114), channel_id=1, source_target_pairs={{0,14},{2,0},{4,2},{6,4},{8,6},{10,8},{12,10},{14,12},{1,15},{3,1}... | collective-permute-start | bytes 614408 | tf_op jit(solution)/shard_map/ppermute | solution.py:564
  26.3 0.0 copy-done.11
  27.0 1.3 %shard_map.52 = (f32[36,80,128]{2,1,0:T(8,128)S(1)}, f32[36,80,128]{2,1,0:T(8,128)S(1)}, f32[2,2,36,8,128]{4,3,2,1,0:T(8,128)S(1)}, f32[4,40,128]{2,1,0:T(8,128)}) custom-call(f32[4,40,128]{2,1,0:T(8,128)S(1)} %get-tuple-element.115.wide_ref), custom_call_target="tpu_custom_call" | custom-call | tf_op jit(solution)/shard_map/pallas_call | solution.py:569
  28.3 0.0 collective-permute-done.8.low_b_ref
  28.3 3.3 %collective-permute-done.9.high_b_ref = f32[112,640]{1,0:T(8,128)S(1)} collective-permute-done((f32[112,640]{1,0:T(8,128)S(1)}, f32[112,640]{1,0:T(8,128)S(1)}, u32[]{:S(2)}, u32[]{:S(2)}) %collective-permute-start.9) | collective-permute-done | bytes 286752 | tf_op jit(solution)/shard_map/ppermute | solution.py:545
  31.6 5.1 %shard_map.53 = (f32[2,5,36,40,128]{4,3,2,1,0:T(8,128)S(1)}, f32[5,37,40,128]{3,2,1,0:T(8,128)S(1)}, f32[4,32,640]{2,1,0:T(8,128)S(1)}, f32[40,640]{1,0:T(8,128)...) custom-call(s32[1]{0:T(128)} %bitcast.4.info_ref, f32[32,32,640]{2,1,0:T(8,128)} %state_ref.3, ...), custom_call_target="tpu_custom_call" | custom-call | bytes 1048576 | tf_op jit(solution)/shard_map/pallas_call | solution.py:585
  36.7 0.0 collective-permute-done.6.far_low_ref
  36.7 0.0 collective-permute-done.7.far_high_ref
  36.7 8.8 %shard_map.54 = (f32[32,32,640]{2,1,0:T(8,128)}, f32[2,5,36,40,128]{4,3,2,1,0:T(8,128)S(1)}, f32[80,640]{1,0:T(8,128)}, f32[80,640]{1,0:T(8,128)}) custom-call(s32[1]{0:T(128)} %bitcast.4.info_ref, s32[8,128]{1,0:T(8,128)S(1)} %get-tuple-element.112.notes_ref, f32[80,640]{1,0:T(8,128)S(1)} %collective-permute-done.6.far_low_ref, ...), custom_call_target="tpu_custom_call", output_to_operand_aliasing={{1}: (8, {})} | custom-call | tf_op jit(solution)/shard_map/pallas_call | solution.py:599
  (2 shorter events, 0.0 us)
Async XLA Ops:
  0.0 15.7 %copy-start.2 = (f32[32,32,640]{2,1,0:T(8,128)S(1)}, f32[32,32,640]{2,1,0:T(8,128)}, u32[]{:S(2)}) copy-start(f32[32,32,640]{2,1,0:T(8,128)} %state_ref.3) | copy-start | bytes 7864324
  0.0 26.3 %copy-start.11 = (f32[640]{0:T(1024)S(1)}, f32[640]{0:T(1024)}, u32[]{:S(2)}) copy-start(f32[640]{0:T(1024)} %param.13) | copy-start | bytes 7684
  1.6 3.5 %collective-permute-start.3 = (f32[4,32,640]{2,1,0:T(8,128)S(1)}, f32[4,32,640]{2,1,0:T(8,128)S(1)}, u32[]{:S(2)}, u32[]{:S(2)}) collective-permute-start(f32[4,32,640]{2,1,0:T(8,128)S(1)} %get-tuple-element.105), channel_id=1, source_target_pairs={{0,1},{1,0},{2,3},{3,2},{4,5},{5,4},{6,7},{7,6},{8,9},{9,8},{10,11... | collective-permute-start | bytes 983048 | tf_op jit(solution)/shard_map/ppermute | solution.py:531
  2.1 0.8 %copy-start = (s32[2,32,32]{2,1,0:T(8,128)S(1)}, s32[2,32,32]{2,1,0:T(8,128)}, u32[]{:S(2)}) copy-start(s32[2,32,32]{2,1,0:T(8,128)} %shift_ref.1) | copy-start | bytes 24580
  2.8 0.8 %copy-start.1 = (f32[2,32,32]{2,1,0:T(8,128)S(1)}, f32[2,32,32]{2,1,0:T(8,128)}, u32[]{:S(2)}) copy-start(f32[2,32,32]{2,1,0:T(8,128)} %frac_ref.1) | copy-start | bytes 24580
  3.7 1.3 %collective-permute-start.2 = (f32[4,32,128]{2,1,0:T(8,128)S(1)}, f32[4,32,128]{2,1,0:T(8,128)S(1)}, u32[]{:S(2)}, u32[]{:S(2)}) collective-permute-start(f32[4,32,128]{2,1,0:T(8,128)S(1)} %shard_map.48.own_ref), channel_id=1, source_target_pairs={{0,1},{1,0},{2,3},{3,2},{4,5},{5,4},{6,7},{7,6},{8,9},{9,8},{10,11... | collective-permute-start | bytes 196616 | tf_op jit(solution)/shard_map/ppermute | solution.py:530
  5.1 10.6 %collective-permute-start.4 = (f32[40,640]{1,0:T(8,128)S(1)}, f32[40,640]{1,0:T(8,128)S(1)}, u32[]{:S(2)}, u32[]{:S(2)}) collective-permute-start(f32[40,640]{1,0:T(8,128)S(1)} %get-tuple-element.109), channel_id=1, source_target_pairs={{0,2},{2,4},{4,6},{6,8},{8,10},{10,12},{12,14},{14,0},{1,3},{3,5},... | collective-permute-start | bytes 307208 | tf_op jit(solution)/shard_map/ppermute | solution.py:542
  7.9 7.8 %collective-permute-start.5 = (f32[40,640]{1,0:T(8,128)S(1)}, f32[40,640]{1,0:T(8,128)S(1)}, u32[]{:S(2)}, u32[]{:S(2)}) collective-permute-start(f32[40,640]{1,0:T(8,128)S(1)} %get-tuple-element.110), channel_id=1, source_target_pairs={{0,14},{2,0},{4,2},{6,4},{8,6},{10,8},{12,10},{14,12},{1,15},{3,1}... | collective-permute-start | bytes 307208 | tf_op jit(solution)/shard_map/ppermute | solution.py:543
  11.0 17.3 %collective-permute-start.8 = (f32[112,640]{1,0:T(8,128)S(1)}, f32[112,640]{1,0:T(8,128)S(1)}, u32[]{:S(2)}, u32[]{:S(2)}) collective-permute-start(f32[112,640]{1,0:T(8,128)S(1)} %get-tuple-element.118), channel_id=1, source_target_pairs={{0,2},{2,4},{4,6},{6,8},{8,10},{10,12},{12,14},{14,0},{1,3},{3,5},... | collective-permute-start | bytes 860168 | tf_op jit(solution)/shard_map/ppermute | solution.py:544
  11.0 20.6 %collective-permute-start.9 = (f32[112,640]{1,0:T(8,128)S(1)}, f32[112,640]{1,0:T(8,128)S(1)}, u32[]{:S(2)}, u32[]{:S(2)}) collective-permute-start(f32[112,640]{1,0:T(8,128)S(1)} %get-tuple-element.119), channel_id=1, source_target_pairs={{0,14},{2,0},{4,2},{6,4},{8,6},{10,8},{12,10},{14,12},{1,15},{3,1}... | collective-permute-start | bytes 860168 | tf_op jit(solution)/shard_map/ppermute | solution.py:545
  18.5 18.2 %collective-permute-start.6 = (f32[80,640]{1,0:T(8,128)S(1)}, f32[80,640]{1,0:T(8,128)S(1)}, u32[]{:S(2)}, u32[]{:S(2)}) collective-permute-start(f32[80,640]{1,0:T(8,128)S(1)} %get-tuple-element.113), channel_id=1, source_target_pairs={{0,2},{2,4},{4,6},{6,8},{8,10},{10,12},{12,14},{14,0},{1,3},{3,5},... | collective-permute-start | bytes 614408 | tf_op jit(solution)/shard_map/ppermute | solution.py:565
  18.6 18.2 %collective-permute-start.7 = (f32[80,640]{1,0:T(8,128)S(1)}, f32[80,640]{1,0:T(8,128)S(1)}, u32[]{:S(2)}, u32[]{:S(2)}) collective-permute-start(f32[80,640]{1,0:T(8,128)S(1)} %get-tuple-element.114), channel_id=1, source_target_pairs={{0,14},{2,0},{4,2},{6,4},{8,6},{10,8},{12,10},{14,12},{1,15},{3,1}... | collective-permute-start | bytes 614408 | tf_op jit(solution)/shard_map/ppermute | solution.py:564
